TPU v7x, 1024 devices: a whole 4x8x16 slice. The times are simulated.
1024 devices in a mesh: tile: 128 (over y, z_lo, core), case: 8 (over x, z_hi).
Axes of the slice: x: 4, y: 8, z: 16 (z_hi: 2, z_lo: 8; z = z_hi * 8 + z_lo), core: 2. Of those that a mesh axis runs over, the one named last changes fastest.
Arguments:
- checkpoint: bfloat16 [8, 19, 1024, 8, 128], P('case', None, 'tile'), may hold values from 0 to 0.6, as said below
- adjoint_field: float32 [8, 19, 1024, 8, 128], P('case', None, 'tile'), may hold values from -6 to 6
- accel_table: int32 [8, 2, 3], P('case'), may hold values from -20 to 20
- design: float32 [128, 1, 16], P('tile'), may hold values from 0 to 1
- design_mask: int32 [128, 1, 16], P('tile'), may hold values 0 or 1
- first_moment: float32 [128, 1, 16], P('tile'), may hold values from -1 to 1
- second_moment: float32 [128, 1, 16], P('tile'), may hold values from 0.001 to 0.1
Outputs:
- adjoint_start: float32 [8, 19, 1024, 8, 128], P('case', None, 'tile')
- design_new: float32 [128, 1, 16], P('tile')
- first_new: float32 [128, 1, 16], P('tile')
- second_new: float32 [128, 1, 16], P('tile')
Inputs may be any that keep to these rules, and one draw needn't show every extreme that they name: `checkpoint`: every population is positive.
All inputs are finite; a program needn't handle non-finite values. No bound on the sum of `design_mask` on one device may be relied on, other than what follows from the above.
Results may differ from a plain program's by a relative error of at most 0.0003.
Values sent between devices are 32-bit elements; how exact they have to be, the bound alone decides.
No kernel may reach another device: no remote copies, remote signals or barrier semaphores. Data moves between devices by JAX's collectives and lax.ppermute only.
A program may use at most 32 MiB of HBM per device.

v0:
```python
import jax
import jax.numpy as jnp
import numpy as np
from jax import lax
from jax.sharding import PartitionSpec as P

Q = 19
BLOCK = 8
STEPS = 2


VELOCITIES = [
    (0, 0, 0),
    (1, 0, 0),
    (-1, 0, 0),
    (0, 1, 0),
    (0, -1, 0),
    (0, 0, 1),
    (0, 0, -1),
    (1, 1, 0),
    (-1, -1, 0),
    (1, -1, 0),
    (-1, 1, 0),
    (1, 0, 1),
    (-1, 0, -1),
    (1, 0, -1),
    (-1, 0, 1),
    (0, 1, 1),
    (0, -1, -1),
    (0, 1, -1),
    (0, -1, 1),
]
OPPOSITE = [0, 2, 1, 4, 3, 6, 5, 8, 7, 10, 9, 12, 11, 14, 13, 16, 15, 18, 17]
WEIGHTS = np.array([1.0 / 3.0] + [1.0 / 18.0] * 6 + [1.0 / 36.0] * 12, np.float32)
VEL_TABLE = np.array(VELOCITIES, np.float32)
RELAX_RATE = 0.9
SOLID_MAX = 0.5
FACE_WEIGHT = 0.5
ACCEL_SCALE = 400.0
BETA_ONE = 0.9
BETA_TWO = 0.999
LEARN_RATE = 0.2
ADAM_EPS = 1e-08
BIAS_ONE = 1.0 - 0.9**10
BIAS_TWO = 1.0 - 0.999**10


def extended(block, sides, width):
    for axis, dim in sides:
        count = lax.axis_size(axis)
        forward = [(i, i + 1) for i in range(count - 1)]
        forward.append((count - 1, 0))
        backward = [(target, source) for source, target in forward]
        low = lax.ppermute(
            lax.slice_in_dim(block, block.shape[dim] - width, None, axis=dim), axis, forward
        )
        high = lax.ppermute(lax.slice_in_dim(block, 0, width, axis=dim), axis, backward)
        block = jnp.concatenate([low, block, high], axis=dim)
    return block


def collide(populations, solid, accel):
    density = jnp.sum(populations, axis=0)
    velocity = [
        jnp.sum(populations * VEL_TABLE[:, axis_id][:, None, None, None], axis=0) / density
        for axis_id in range(3)
    ]
    speed_sq = velocity[0] * velocity[0] + velocity[1] * velocity[1] + velocity[2] * velocity[2]
    project = sum(
        (
            VEL_TABLE[:, axis_id][:, None, None, None] * velocity[axis_id][None]
            for axis_id in range(3)
        )
    )
    forcing = sum(
        (VEL_TABLE[:, axis_id][:, None, None, None] * accel[axis_id] for axis_id in range(3))
    )
    weight = WEIGHTS[:, None, None, None]
    equil = weight * density * (1.0 + 3.0 * project + 4.5 * project * project - 1.5 * speed_sq)
    post = populations + RELAX_RATE * (equil - populations) + 3.0 * weight * density * forcing
    flipped = post[jnp.array(OPPOSITE)]
    return (1.0 - solid) * post + solid * flipped


def transport(field, direction):
    slab = field.shape[1]
    padded = extended(field, (("tile", 1),), 1)
    pieces = []
    for vel_id in range(Q):
        shift_x, shift_y, shift_z = VELOCITIES[vel_id]
        start = 1 - direction * shift_x
        piece = padded[vel_id, start : start + slab]
        pieces.append(jnp.roll(piece, (direction * shift_y, direction * shift_z), axis=(1, 2)))
    return jnp.stack(pieces)


def block_filter(grid):
    padded = extended(grid, (("tile", 0),), 1)
    beside_all = padded[:-2] + padded[2:]
    for axis_id in (1, 2):
        beside_all = beside_all + jnp.roll(grid, 1, axis_id) + jnp.roll(grid, -1, axis_id)
    return (grid + FACE_WEIGHT * beside_all) / (1.0 + 6.0 * FACE_WEIGHT)


def expand_cells(blocks):
    blocks_x, blocks_y, blocks_z = blocks.shape
    return SOLID_MAX * jnp.broadcast_to(
        blocks[:, None, :, None, :, None], (blocks_x, BLOCK, blocks_y, BLOCK, blocks_z, BLOCK)
    ).reshape(blocks_x * BLOCK, blocks_y * BLOCK, blocks_z * BLOCK)


def body(checkpoint, adjoint_field, accel_table, design, design_mask, first_moment, second_moment):
    mask_float = design_mask.astype(jnp.float32)
    filtered = block_filter(design * mask_float)
    blocks_x, blocks_y, blocks_z = filtered.shape
    accel = accel_table[0].astype(jnp.float32) / ACCEL_SCALE
    solid = expand_cells(filtered)
    states = [checkpoint[0].astype(jnp.float32)]
    turn = 0
    states.append(transport(collide(states[-1], solid, accel[turn]), 1))
    cotangent = adjoint_field[0]
    sensitivity = jnp.zeros_like(solid)
    for turn in reversed(range(STEPS)):
        acc_now = accel[turn]
        pulled = transport(cotangent, -1)
        _, pull = jax.vjp(lambda pops, cells: collide(pops, cells, acc_now), states[turn], solid)
        cotangent, dsolid = pull(pulled)
        sensitivity = sensitivity + dsolid
    blocks = sensitivity.reshape(blocks_x, BLOCK, blocks_y, BLOCK, blocks_z, BLOCK).sum(
        axis=(1, 3, 5)
    )
    block_sens = SOLID_MAX * lax.psum(blocks, "case")
    gradient = mask_float * block_filter(block_sens)
    first_new = BETA_ONE * first_moment + (1.0 - BETA_ONE) * gradient
    second_new = BETA_TWO * second_moment + (1.0 - BETA_TWO) * gradient * gradient
    stepped = design - LEARN_RATE * (first_new / BIAS_ONE) / (
        jnp.sqrt(second_new / BIAS_TWO) + ADAM_EPS
    )
    design_new = jnp.clip(stepped, 0.0, 1.0)
    return (cotangent[None], design_new, first_new, second_new)


def solution(mesh):
    placed = (
        P("case", None, "tile", None, None),
        P("case", None, "tile", None, None),
        P("case", None, None),
        P("tile", None, None),
        P("tile", None, None),
        P("tile", None, None),
        P("tile", None, None),
    )
    return jax.shard_map(
        body,
        mesh=mesh,
        in_specs=placed,
        out_specs=(
            P("case", None, "tile", None, None),
            P("tile", None, None),
            P("tile", None, None),
            P("tile", None, None),
        ),
        check_vma=False,
    )
```

profile of v0, /device:TPU:32, one launch (start us, length us, event | category | flops | bytes accessed | tf_op | source)
XLA Modules:
  0.0 180.9 jit_solution(1128064886823229861)
XLA Ops:
  0.6 0.7 convert_multiply_fusion
  1.3 1.9 %collective-permute-start = (f32[1,1,16]{2,1,0:T(1,128)S(1)}, f32[1,1,16]{2,1,0:T(1,128)S(1)}, u32[]{:S(2)}, u32[]{:S(2)}) collective-permute-start(f32[1,1,16]{2,1,0:T(1,128)S(1)} %convert_multiply_fusion), channel_id=1, source_target_pairs={{0,8},{8,16},{16,24},{24,32},{32,40},{40,48},{48,56},{56,64},{64,7... | collective-permute-start | bytes 200 | tf_op jit(solution)/shard_map/ppermute | solution.py:54
  3.2 15.7 %collective-permute-start.1 = (f32[1,1,16]{2,1,0:T(1,128)S(1)}, f32[1,1,16]{2,1,0:T(1,128)S(1)}, u32[]{:S(2)}, u32[]{:S(2)}) collective-permute-start(f32[1,1,16]{2,1,0:T(1,128)S(1)} %convert_multiply_fusion), channel_id=1, source_target_pairs={{8,0},{16,8},{24,16},{32,24},{40,32},{48,40},{56,48},{64,56},{72,6... | collective-permute-start | bytes 200 | tf_op jit(solution)/shard_map/ppermute | solution.py:57
  18.9 0.9 fusion.87
  19.8 1.9 %collective-permute-start.3 = (f32[19,1,8,128]{3,2,1,0:T(8,128)S(1)}, f32[19,1,8,128]{3,2,1,0:T(8,128)}, u32[]{:S(2)}, u32[]{:S(2)}) collective-permute-start(f32[19,1,8,128]{3,2,1,0:T(8,128)S(1)} %get-tuple-element.130), channel_id=1, source_target_pairs={{0,8},{8,16},{16,24},{24,32},{32,40},{40,48},{48,56},{56,64},{64,7... | collective-permute-start | bytes 233480 | tf_op jit(solution)/shard_map/ppermute | solution.py:54
  21.8 12.4 %collective-permute-start.2 = (f32[19,1,8,128]{3,2,1,0:T(8,128)S(1)}, f32[19,1,8,128]{3,2,1,0:T(8,128)}, u32[]{:S(2)}, u32[]{:S(2)}) collective-permute-start(f32[19,1,8,128]{3,2,1,0:T(8,128)S(1)} %get-tuple-element.131), channel_id=1, source_target_pairs={{8,0},{16,8},{24,16},{32,24},{40,32},{48,40},{56,48},{64,56},{72,6... | collective-permute-start | bytes 233480 | tf_op jit(solution)/shard_map/ppermute | solution.py:57
  34.1 0.8 constant_dynamic-update-slice_fusion.18
  34.9 0.9 slice_bitcast_fusion.16
  35.8 0.6 slice.883
  36.5 0.7 fusion.91
  37.2 0.6 slice.884
  38.0 0.7 copy-done.122
  38.7 0.7 fusion.88
  39.4 0.6 copy-done.120
  40.4 0.5 copy-done.89
  41.0 0.2 fusion.5
  41.3 0.5 copy-done.67
  41.9 0.7 copy-done.127
  42.6 4.3 %add_bitcast_fusion.1 = (f32[19]{0:T(128)}, f32[19]{0:T(128)S(1)}) fusion(f32[19,1,1,1]{0,3,2,1:T(1,128)S(1)} %copy-done.127, f32[19,1,1,1]{0,3,2,1:T(1,128)S(1)} %copy-done.128, f32[19,1,1,1]{0,3,2,1:T(1,128)S(1)} %copy-done.129, f32[]{:T(128)} %bitcast.83, f32[]{:T(128)} %bitcast.82, f32[]{:T(128)} %bitcast.81, f32[]{:T(128)} %bitcast.39, f32[]{:T(128)} %bitcast.38, ...), kind=kLoop, calls=%fused_computation.325 | loop fusion | flops 190 | bytes 404 | tf_op jit(solution)/shard_map/transpose(jvp())/mul | solution.py:80
  46.9 0.7 copy-done.104
  47.6 0.5 fusion.9
  48.1 0.6 gather_fusion
  48.7 1.5 multiply_bitcast_fusion.2
  50.4 0.5 copy-done.114
  50.8 0.6 multiply_add_fusion.1
  51.5 1.9 %collective-permute-start.5 = (f32[19,1,8,128]{3,2,1,0:T(8,128)S(1)}, f32[19,1,8,128]{3,2,1,0:T(8,128)S(1)}, u32[]{:S(2)}, u32[]{:S(2)}) collective-permute-start(f32[19,1,8,128]{3,2,1,0:T(8,128)S(1)} %get-tuple-element.120), channel_id=1, source_target_pairs={{8,0},{16,8},{24,16},{32,24},{40,32},{48,40},{56,48},{64,56},{72,6... | collective-permute-start | bytes 233480 | tf_op jit(solution)/shard_map/ppermute | solution.py:57
  53.4 2.4 %collective-permute-start.4 = (f32[19,1,8,128]{3,2,1,0:T(8,128)S(1)}, f32[19,1,8,128]{3,2,1,0:T(8,128)S(1)}, u32[]{:S(2)}, u32[]{:S(2)}) collective-permute-start(f32[19,1,8,128]{3,2,1,0:T(8,128)S(1)} %get-tuple-element.121), channel_id=1, source_target_pairs={{0,8},{8,16},{16,24},{24,32},{32,40},{40,48},{48,56},{56,64},{64,7... | collective-permute-start | bytes 233480 | tf_op jit(solution)/shard_map/ppermute | solution.py:54
  55.8 0.7 fusion.49
  56.6 0.7 fusion.48
  57.7 0.5 copy-done.110
  58.9 0.6 copy-done.99
  59.6 0.6 copy-done.103
  60.2 0.6 copy-done.97
  60.9 0.6 copy-done.101
  61.6 6.2 %collective-permute-done.4 = f32[19,1,8,128]{3,2,1,0:T(8,128)S(1)} collective-permute-done((f32[19,1,8,128]{3,2,1,0:T(8,128)S(1)}, f32[19,1,8,128]{3,2,1,0:T(8,128)S(1)}, u32[]{:S(2)}, u32[]{:S(2)}) %collective-permute-start.4) | collective-permute-done | bytes 77856 | tf_op jit(solution)/shard_map/ppermute | solution.py:54
  70.2 0.7 copy-done.94
  70.8 0.2 multiply_reduce_fusion.14
  71.3 0.2 fusion.76
  71.8 0.4 copy-done.2
  72.1 0.2 copy-done.27
  72.4 0.5 fusion.21
  72.9 0.7 gather_fusion.1
  73.6 3.2 %multiply_reduce_fusion.2 = (f32[8,8,128]{2,1,0:T(8,128)}, f32[8,8,128]{2,1,0:T(8,128)}, f32[19,8,8,128]{3,2,1,0:T(8,128)}, f32[19,8,8,128]{3,2,1,0:T(8,128)S(1)}) fusion(f32[19,8,8,128]{3,2,1,0:T(8,128)} %copy-done.18, f32[19,8,8,128]{3,2,1,0:T(8,128)S(1)} %gather_fusion.1, f32[128]{0:T(128)} %copy-done.114, f32[128]{0:T(128)} %copy-done.118, ...), kind=kLoop, calls=%fused_computation.38 | loop fusion | flops 3874816 | bytes 3343816 | tf_op jit(solution)/shard_map/transpose(jvp())/reduce_sum | solution.py:82
  76.9 0.7 copy-done.121
  77.6 3.6 %scatter_fusion = f32[19,8,8,128]{3,2,1,0:T(8,128)S(1)} fusion(f32[19,8,8,128]{3,2,1,0:T(8,128)S(1)} %get-tuple-element.88, s32[19]{0:T(128)S(1)} %copy-done.121, f32[19,8,8,128]{3,2,1,0:T(8,128)} %get-tuple-element.87), kind=kCustom, calls=%fused_computation.2 | custom fusion | flops 155648 | bytes 1867852 | tf_op jit(solution)/shard_map/transpose(jvp())/scatter-add | solution.py:81
  81.6 1.6 fusion.23
  83.6 0.2 fusion.68
  83.7 0.6 copy-done.54
  84.4 0.3 add_add_fusion
  84.7 6.4 %collective-permute-start.6 = (f32[19,1,8,128]{3,2,1,0:T(8,128)S(1)}, f32[19,1,8,128]{3,2,1,0:T(8,128)S(1)}, u32[]{:S(2)}, u32[]{:S(2)}) collective-permute-start(f32[19,1,8,128]{3,2,1,0:T(8,128)S(1)} %get-tuple-element.105), channel_id=1, source_target_pairs={{8,0},{16,8},{24,16},{32,24},{40,32},{48,40},{56,48},{64,56},{72,6... | collective-permute-start | bytes 233480 | tf_op jit(solution)/shard_map/ppermute | solution.py:57
  91.1 1.9 %collective-permute-start.7 = (f32[19,1,8,128]{3,2,1,0:T(8,128)S(1)}, f32[19,1,8,128]{3,2,1,0:T(8,128)S(1)}, u32[]{:S(2)}, u32[]{:S(2)}) collective-permute-start(f32[19,1,8,128]{3,2,1,0:T(8,128)S(1)} %get-tuple-element.104), channel_id=1, source_target_pairs={{0,8},{8,16},{16,24},{24,32},{32,40},{40,48},{48,56},{56,64},{64,7... | collective-permute-start | bytes 233480 | tf_op jit(solution)/shard_map/ppermute | solution.py:54
  93.2 12.4 %collective-permute-done.7 = f32[19,1,8,128]{3,2,1,0:T(8,128)S(1)} collective-permute-done((f32[19,1,8,128]{3,2,1,0:T(8,128)S(1)}, f32[19,1,8,128]{3,2,1,0:T(8,128)S(1)}, u32[]{:S(2)}, u32[]{:S(2)}) %collective-permute-start.7) | collective-permute-done | bytes 77856 | tf_op jit(solution)/shard_map/ppermute | solution.py:54
  107.5 0.6 copy-done.17
  108.2 0.7 multiply_reduce_fusion
  109.1 0.1 reduce_sum.576
  109.2 49.9 %psum.7 = f32[1,1,16]{2,1,0:T(1,128)S(1)} all-reduce(f32[1,1,16]{2,1,0:T(1,128)S(1)} %bitcast.522), channel_id=1, replica_groups=mesh['tile'=128,'case'=8] {'case'}, use_global_device_ids=true, to_apply=%region_30.31 | all-reduce | flops 16 | bytes 128 | tf_op jit(solution)/shard_map/psum | solution.py:132
  159.1 1.9 %collective-permute-start.8 = (f32[1,1,16]{2,1,0:T(1,128)S(1)}, f32[1,1,16]{2,1,0:T(1,128)S(1)}, u32[]{:S(2)}, u32[]{:S(2)}) collective-permute-start(f32[1,1,16]{2,1,0:T(1,128)S(1)} %broadcast_multiply_fusion.4), channel_id=1, source_target_pairs={{0,8},{8,16},{16,24},{24,32},{32,40},{40,48},{48,56},{56,64},{64,7... | collective-permute-start | bytes 200 | tf_op jit(solution)/shard_map/ppermute | solution.py:54
  161.0 12.4 %collective-permute-start.9 = (f32[1,1,16]{2,1,0:T(1,128)S(1)}, f32[1,1,16]{2,1,0:T(1,128)S(1)}, u32[]{:S(2)}, u32[]{:S(2)}) collective-permute-start(f32[1,1,16]{2,1,0:T(1,128)S(1)} %broadcast_multiply_fusion.4), channel_id=1, source_target_pairs={{8,0},{16,8},{24,16},{32,24},{40,32},{48,40},{56,48},{64,56},{72,6... | collective-permute-start | bytes 200 | tf_op jit(solution)/shard_map/ppermute | solution.py:57
  173.4 2.2 %scatter_fusion.1 = f32[19,8,8,128]{3,2,1,0:T(8,128)S(1)} fusion(f32[19,8,8,128]{3,2,1,0:T(8,128)S(1)} %get-tuple-element.90, s32[19]{0:T(128)S(1)} %copy-done.121, f32[19,8,8,128]{3,2,1,0:T(8,128)S(1)} %get-tuple-element.89), kind=kCustom, calls=%fused_computation.3 | custom fusion | flops 155648 | bytes 1867852 | tf_op jit(solution)/shard_map/transpose(jvp())/scatter-add | solution.py:81
  175.7 0.9 fusion.22
  176.6 1.1 add_bitcast_fusion
  177.7 0.6 fusion.89
  178.4 0.6 copy-done.123
  179.0 1.8 %subtract_clamp_fusion = (f32[1,1,16]{2,1,0:T(1,128)}, f32[1,1,16]{2,1,0:T(1,128)}, f32[1,1,16]{2,1,0:T(1,128)}) fusion(f32[1,1,16]{2,1,0:T(1,128)S(1)} %copy-done.123, f32[1,1,16]{2,1,0:T(1,128)S(1)} %copy-done.125, f32[1,1,16]{2,1,0:T(1,128)S(1)} %copy-done.126, f32[1,1,1]{2,1,0:T(1,128)} %get-tuple-element.151, f32[1,1,15]{2,1,0:T(1,128)S(1)} %get-tuple-element.153, ...), kind=kLoop, calls=%fused_computation.322 | loop fusion | flops 416 | bytes 768 | tf_op jit(solution)/shard_map/jit(clip)/min | solution.py:139
  (393 shorter events, 7.1 us)
Async XLA Ops:
  1.3 47.4 %collective-permute-start = (f32[1,1,16]{2,1,0:T(1,128)S(1)}, f32[1,1,16]{2,1,0:T(1,128)S(1)}, u32[]{:S(2)}, u32[]{:S(2)}) collective-permute-start(f32[1,1,16]{2,1,0:T(1,128)S(1)} %convert_multiply_fusion), channel_id=1, source_target_pairs={{0,8},{8,16},{16,24},{24,32},{32,40},{40,48},{48,56},{56,64},{64,7... | collective-permute-start | bytes 200 | tf_op jit(solution)/shard_map/ppermute | solution.py:54
  3.2 45.5 %collective-permute-start.1 = (f32[1,1,16]{2,1,0:T(1,128)S(1)}, f32[1,1,16]{2,1,0:T(1,128)S(1)}, u32[]{:S(2)}, u32[]{:S(2)}) collective-permute-start(f32[1,1,16]{2,1,0:T(1,128)S(1)} %convert_multiply_fusion), channel_id=1, source_target_pairs={{8,0},{16,8},{24,16},{32,24},{40,32},{48,40},{56,48},{64,56},{72,6... | collective-permute-start | bytes 200 | tf_op jit(solution)/shard_map/ppermute | solution.py:57
  19.8 36.8 %collective-permute-start.3 = (f32[19,1,8,128]{3,2,1,0:T(8,128)S(1)}, f32[19,1,8,128]{3,2,1,0:T(8,128)}, u32[]{:S(2)}, u32[]{:S(2)}) collective-permute-start(f32[19,1,8,128]{3,2,1,0:T(8,128)S(1)} %get-tuple-element.130), channel_id=1, source_target_pairs={{0,8},{8,16},{16,24},{24,32},{32,40},{40,48},{48,56},{56,64},{64,7... | collective-permute-start | bytes 233480 | tf_op jit(solution)/shard_map/ppermute | solution.py:54
  21.8 34.0 %collective-permute-start.2 = (f32[19,1,8,128]{3,2,1,0:T(8,128)S(1)}, f32[19,1,8,128]{3,2,1,0:T(8,128)}, u32[]{:S(2)}, u32[]{:S(2)}) collective-permute-start(f32[19,1,8,128]{3,2,1,0:T(8,128)S(1)} %get-tuple-element.131), channel_id=1, source_target_pairs={{8,0},{16,8},{24,16},{32,24},{40,32},{48,40},{56,48},{64,56},{72,6... | collective-permute-start | bytes 233480 | tf_op jit(solution)/shard_map/ppermute | solution.py:57
  35.8 3.5 %copy-start = (bf16[1,19,8,8,128]{4,3,2,1,0:T(8,128)(2,1)S(1)}, bf16[1,19,8,8,128]{4,3,2,1,0:T(8,128)(2,1)}, u32[]{:S(2)}) copy-start(bf16[1,19,8,8,128]{4,3,2,1,0:T(8,128)(2,1)} %param.43) | copy-start | bytes 933892
  36.4 3.6 %copy-start.98 = (f32[8,1,128]{2,1,0:T(1,128)}, f32[8,1,128]{2,1,0:T(1,128)S(1)}, u32[]{:S(2)}) copy-start(f32[8,1,128]{2,1,0:T(1,128)S(1)} %slice.907) | copy-start | bytes 12292
  36.5 3.8 %copy-start.96 = (f32[8,1,128]{2,1,0:T(1,128)}, f32[8,1,128]{2,1,0:T(1,128)S(1)}, u32[]{:S(2)}) copy-start(f32[8,1,128]{2,1,0:T(1,128)S(1)} %slice.915) | copy-start | bytes 12292
  38.0 2.1 %copy-start.102 = (f32[8,1,128]{2,1,0:T(1,128)}, f32[8,1,128]{2,1,0:T(1,128)S(1)}, u32[]{:S(2)}) copy-start(f32[8,1,128]{2,1,0:T(1,128)S(1)} %slice.910) | copy-start | bytes 12292
  40.0 8.1 %copy-start.117 = (s32[1024]{0:T(1024)}, s32[1024]{0:T(1024)S(1)}, u32[]{:S(2)}) copy-start(s32[1024]{0:T(1024)S(1)} %pad_clamp_fusion) | copy-start | bytes 12292
  41.9 8.5 %copy-start.16 = (f32[8,8,128]{2,1,0:T(8,128)}, f32[8,8,128]{2,1,0:T(8,128)S(1)}, u32[]{:S(2)}) copy-start(f32[8,8,128]{2,1,0:T(8,128)S(1)} %get-tuple-element.51) | copy-start | bytes 98308
  46.9 3.5 %copy-start.112 = (f32[19]{0:T(128)}, f32[19]{0:T(128)S(1)}, u32[]{:S(2)}) copy-start(f32[19]{0:T(128)S(1)} %get-tuple-element.143) | copy-start | bytes 232
  50.8 5.0 %copy-start.1 = (f32[1,19,8,8,128]{4,3,2,1,0:T(8,128)S(1)}, f32[1,19,8,8,128]{4,3,2,1,0:T(8,128)}, u32[]{:S(2)}) copy-start(f32[1,19,8,8,128]{4,3,2,1,0:T(8,128)} %param.44) | copy-start | bytes 1867780
  51.5 16.5 %collective-permute-start.5 = (f32[19,1,8,128]{3,2,1,0:T(8,128)S(1)}, f32[19,1,8,128]{3,2,1,0:T(8,128)S(1)}, u32[]{:S(2)}, u32[]{:S(2)}) collective-permute-start(f32[19,1,8,128]{3,2,1,0:T(8,128)S(1)} %get-tuple-element.120), channel_id=1, source_target_pairs={{8,0},{16,8},{24,16},{32,24},{40,32},{48,40},{56,48},{64,56},{72,6... | collective-permute-start | bytes 233480 | tf_op jit(solution)/shard_map/ppermute | solution.py:57
  53.4 14.4 %collective-permute-start.4 = (f32[19,1,8,128]{3,2,1,0:T(8,128)S(1)}, f32[19,1,8,128]{3,2,1,0:T(8,128)S(1)}, u32[]{:S(2)}, u32[]{:S(2)}) collective-permute-start(f32[19,1,8,128]{3,2,1,0:T(8,128)S(1)} %get-tuple-element.121), channel_id=1, source_target_pairs={{0,8},{8,16},{16,24},{24,32},{32,40},{40,48},{48,56},{56,64},{64,7... | collective-permute-start | bytes 233480 | tf_op jit(solution)/shard_map/ppermute | solution.py:54
  61.6 6.3 %copy-start.18 = (f32[19,8,8,128]{3,2,1,0:T(8,128)}, f32[19,8,8,128]{3,2,1,0:T(8,128)S(1)}, u32[]{:S(2)}) copy-start(f32[19,8,8,128]{3,2,1,0:T(8,128)S(1)} %constant_dynamic-update-slice_fusion) | copy-start | bytes 1867780
  67.9 3.2 %copy-start.8 = (f32[8,8,128]{2,1,0:T(8,128)}, f32[8,8,128]{2,1,0:T(8,128)S(1)}, u32[]{:S(2)}) copy-start(f32[8,8,128]{2,1,0:T(8,128)S(1)} %get-tuple-element.110) | copy-start | bytes 98308
  67.9 3.2 %copy-start.10 = (f32[8,8,128]{2,1,0:T(8,128)}, f32[8,8,128]{2,1,0:T(8,128)S(1)}, u32[]{:S(2)}) copy-start(f32[8,8,128]{2,1,0:T(8,128)S(1)} %get-tuple-element.111) | copy-start | bytes 98308
  67.9 3.2 %copy-start.12 = (f32[8,8,128]{2,1,0:T(8,128)}, f32[8,8,128]{2,1,0:T(8,128)S(1)}, u32[]{:S(2)}) copy-start(f32[8,8,128]{2,1,0:T(8,128)S(1)} %get-tuple-element.118) | copy-start | bytes 98308
  67.9 3.2 %copy-start.14 = (f32[8,8,128]{2,1,0:T(8,128)}, f32[8,8,128]{2,1,0:T(8,128)S(1)}, u32[]{:S(2)}) copy-start(f32[8,8,128]{2,1,0:T(8,128)S(1)} %get-tuple-element.119) | copy-start | bytes 98308
  67.9 3.2 %copy-start.21 = (f32[8,8,128]{2,1,0:T(8,128)}, f32[8,8,128]{2,1,0:T(8,128)S(1)}, u32[]{:S(2)}) copy-start(f32[8,8,128]{2,1,0:T(8,128)S(1)} %get-tuple-element.113) | copy-start | bytes 98308
  67.9 3.2 %copy-start.23 = (f32[8,8,128]{2,1,0:T(8,128)}, f32[8,8,128]{2,1,0:T(8,128)S(1)}, u32[]{:S(2)}) copy-start(f32[8,8,128]{2,1,0:T(8,128)S(1)} %get-tuple-element.116) | copy-start | bytes 98308
  67.9 3.2 %copy-start.57 = (f32[1,8,8,128]{3,2,1,0:T(8,128)}, f32[1,8,8,128]{3,2,1,0:T(8,128)S(1)}, u32[]{:S(2)}) copy-start(f32[1,8,8,128]{3,2,1,0:T(8,128)S(1)} %get-tuple-element.115) | copy-start | bytes 98308
  68.0 3.2 %copy-start.77 = (f32[8,1,128]{2,1,0:T(1,128)}, f32[8,1,128]{2,1,0:T(1,128)S(1)}, u32[]{:S(2)}) copy-start(f32[8,1,128]{2,1,0:T(1,128)S(1)} %slice.930) | copy-start | bytes 12292
  68.0 3.1 %copy-start.45 = (f32[8,7,128]{2,1,0:T(8,128)}, f32[8,7,128]{2,1,0:T(8,128)S(1)}, u32[]{:S(2)}) copy-start(f32[8,7,128]{2,1,0:T(8,128)S(1)} %slice.929) | copy-start | bytes 86020
  68.0 3.1 %copy-start.4 = (f32[8,8,128]{2,1,0:T(8,128)}, f32[8,8,128]{2,1,0:T(8,128)S(1)}, u32[]{:S(2)}) copy-start(f32[8,8,128]{2,1,0:T(8,128)S(1)} %get-tuple-element.65) | copy-start | bytes 98308
  68.0 3.1 %copy-start.6 = (f32[8,8,128]{2,1,0:T(8,128)}, f32[8,8,128]{2,1,0:T(8,128)S(1)}, u32[]{:S(2)}) copy-start(f32[8,8,128]{2,1,0:T(8,128)S(1)} %get-tuple-element.66) | copy-start | bytes 98308
  68.0 3.1 %copy-start.19 = (f32[8,8,128]{2,1,0:T(8,128)}, f32[8,8,128]{2,1,0:T(8,128)S(1)}, u32[]{:S(2)}) copy-start(f32[8,8,128]{2,1,0:T(8,128)S(1)} %get-tuple-element.67) | copy-start | bytes 98308
  68.1 3.1 %copy-start.55 = (f32[1,8,8,128]{3,2,1,0:T(8,128)}, f32[1,8,8,128]{3,2,1,0:T(8,128)S(1)}, u32[]{:S(2)}) copy-start(f32[1,8,8,128]{3,2,1,0:T(8,128)S(1)} %get-tuple-element.70) | copy-start | bytes 98308
  68.1 3.1 %copy-start.79 = (f32[8,1,128]{2,1,0:T(1,128)}, f32[8,1,128]{2,1,0:T(1,128)S(1)}, u32[]{:S(2)}) copy-start(f32[8,1,128]{2,1,0:T(1,128)S(1)} %slice.940) | copy-start | bytes 12292
  68.1 3.1 %copy-start.47 = (f32[8,7,128]{2,1,0:T(8,128)}, f32[8,7,128]{2,1,0:T(8,128)S(1)}, u32[]{:S(2)}) copy-start(f32[8,7,128]{2,1,0:T(8,128)S(1)} %slice.939) | copy-start | bytes 86020
  68.1 3.1 %copy-start.81 = (f32[8,1,128]{2,1,0:T(1,128)}, f32[8,1,128]{2,1,0:T(1,128)S(1)}, u32[]{:S(2)}) copy-start(f32[8,1,128]{2,1,0:T(1,128)S(1)} %slice.942) | copy-start | bytes 12292
  68.1 3.1 %copy-start.49 = (f32[8,7,128]{2,1,0:T(8,128)}, f32[8,7,128]{2,1,0:T(8,128)S(1)}, u32[]{:S(2)}) copy-start(f32[8,7,128]{2,1,0:T(8,128)S(1)} %slice.941) | copy-start | bytes 86020
  68.2 3.0 %copy-start.83 = (f32[8,1,128]{2,1,0:T(1,128)}, f32[8,1,128]{2,1,0:T(1,128)S(1)}, u32[]{:S(2)}) copy-start(f32[8,1,128]{2,1,0:T(1,128)S(1)} %slice.926) | copy-start | bytes 12292
  68.3 2.9 %copy-start.33 = (f32[8,8,1]{2,1,0:T(8,128)}, f32[8,8,1]{2,1,0:T(8,128)S(1)}, u32[]{:S(2)}) copy-start(f32[8,8,1]{2,1,0:T(8,128)S(1)} %slice.932) | copy-start | bytes 772
  68.4 2.9 %copy-start.35 = (f32[8,8,127]{2,1,0:T(8,128)}, f32[8,8,127]{2,1,0:T(8,128)S(1)}, u32[]{:S(2)}) copy-start(f32[8,8,127]{2,1,0:T(8,128)S(1)} %slice.935) | copy-start | bytes 97540
  68.4 2.8 %copy-start.85 = (f32[8,1,128]{2,1,0:T(1,128)}, f32[8,1,128]{2,1,0:T(1,128)S(1)}, u32[]{:S(2)}) copy-start(f32[8,1,128]{2,1,0:T(1,128)S(1)} %slice.937) | copy-start | bytes 12292
  68.4 2.8 %copy-start.87 = (f32[8,1,128]{2,1,0:T(1,128)}, f32[8,1,128]{2,1,0:T(1,128)S(1)}, u32[]{:S(2)}) copy-start(f32[8,1,128]{2,1,0:T(1,128)S(1)} %slice.943) | copy-start | bytes 12292
  68.5 2.8 %copy-start.37 = (f32[8,8,1]{2,1,0:T(8,128)}, f32[8,8,1]{2,1,0:T(8,128)S(1)}, u32[]{:S(2)}) copy-start(f32[8,8,1]{2,1,0:T(8,128)S(1)} %slice.945) | copy-start | bytes 772
  68.6 2.7 %copy-start.39 = (f32[8,8,127]{2,1,0:T(8,128)}, f32[8,8,127]{2,1,0:T(8,128)S(1)}, u32[]{:S(2)}) copy-start(f32[8,8,127]{2,1,0:T(8,128)S(1)} %slice.947) | copy-start | bytes 97540
  68.7 2.6 %copy-start.41 = (f32[8,8,127]{2,1,0:T(8,128)}, f32[8,8,127]{2,1,0:T(8,128)S(1)}, u32[]{:S(2)}) copy-start(f32[8,8,127]{2,1,0:T(8,128)S(1)} %slice.949) | copy-start | bytes 97540
  68.8 2.5 %copy-start.43 = (f32[8,8,1]{2,1,0:T(8,128)}, f32[8,8,1]{2,1,0:T(8,128)S(1)}, u32[]{:S(2)}) copy-start(f32[8,8,1]{2,1,0:T(8,128)S(1)} %slice.951) | copy-start | bytes 772
  77.5 3.7 %copy-start.3 = (f32[1,8,8,128]{3,2,1,0:T(8,128)S(1)}, f32[1,8,8,128]{3,2,1,0:T(8,128)}, u32[]{:S(2)}) copy-start(f32[1,8,8,128]{3,2,1,0:T(8,128)} %copy-done.2) | copy-start | bytes 98308
  77.5 3.7 %copy-start.26 = (f32[8,8,128]{2,1,0:T(8,128)S(1)}, f32[8,8,128]{2,1,0:T(8,128)}, u32[]{:S(2)}) copy-start(f32[8,8,128]{2,1,0:T(8,128)} %copy-done.25) | copy-start | bytes 98308
  77.5 3.7 %copy-start.28 = (f32[8,8,128]{2,1,0:T(8,128)S(1)}, f32[8,8,128]{2,1,0:T(8,128)}, u32[]{:S(2)}) copy-start(f32[8,8,128]{2,1,0:T(8,128)} %copy-done.27) | copy-start | bytes 98308
  77.5 3.7 %copy-start.30 = (f32[8,8,128]{2,1,0:T(8,128)S(1)}, f32[8,8,128]{2,1,0:T(8,128)}, u32[]{:S(2)}) copy-start(f32[8,8,128]{2,1,0:T(8,128)} %copy-done.29) | copy-start | bytes 98308
  77.5 3.7 %copy-start.32 = (f32[8,8,128]{2,1,0:T(8,128)S(1)}, f32[8,8,128]{2,1,0:T(8,128)}, u32[]{:S(2)}) copy-start(f32[8,8,128]{2,1,0:T(8,128)} %copy-done.31) | copy-start | bytes 98308
  77.5 3.7 %copy-start.90 = (f32[19]{0:T(128)S(1)}, f32[19]{0:T(128)}, u32[]{:S(2)}) copy-start(f32[19]{0:T(128)} %constant.78) | copy-start | bytes 232
  77.5 3.7 %copy-start.92 = (f32[19]{0:T(128)S(1)}, f32[19]{0:T(128)}, u32[]{:S(2)}) copy-start(f32[19]{0:T(128)} %constant.77) | copy-start | bytes 232
  77.6 3.7 %copy-start.95 = (f32[19]{0:T(128)S(1)}, f32[19]{0:T(128)}, u32[]{:S(2)}) copy-start(f32[19]{0:T(128)} %constant.80) | copy-start | bytes 232
  77.6 3.7 %copy-start.106 = (f32[19]{0:T(128)S(1)}, f32[19]{0:T(128)}, u32[]{:S(2)}) copy-start(f32[19]{0:T(128)} %constant.81) | copy-start | bytes 232
  81.3 1.9 %copy-start.5 = (f32[8,8,128]{2,1,0:T(8,128)S(1)}, f32[8,8,128]{2,1,0:T(8,128)}, u32[]{:S(2)}) copy-start(f32[8,8,128]{2,1,0:T(8,128)} %copy-done.4) | copy-start | bytes 98308
  81.3 1.9 %copy-start.7 = (f32[8,8,128]{2,1,0:T(8,128)S(1)}, f32[8,8,128]{2,1,0:T(8,128)}, u32[]{:S(2)}) copy-start(f32[8,8,128]{2,1,0:T(8,128)} %copy-done.6) | copy-start | bytes 98308
  81.3 1.9 %copy-start.9 = (f32[8,8,128]{2,1,0:T(8,128)S(1)}, f32[8,8,128]{2,1,0:T(8,128)}, u32[]{:S(2)}) copy-start(f32[8,8,128]{2,1,0:T(8,128)} %copy-done.8) | copy-start | bytes 98308
  81.4 1.9 %copy-start.11 = (f32[8,8,128]{2,1,0:T(8,128)S(1)}, f32[8,8,128]{2,1,0:T(8,128)}, u32[]{:S(2)}) copy-start(f32[8,8,128]{2,1,0:T(8,128)} %copy-done.10) | copy-start | bytes 98308
  81.4 1.9 %copy-start.13 = (f32[8,8,128]{2,1,0:T(8,128)S(1)}, f32[8,8,128]{2,1,0:T(8,128)}, u32[]{:S(2)}) copy-start(f32[8,8,128]{2,1,0:T(8,128)} %copy-done.12) | copy-start | bytes 98308
  81.4 1.9 %copy-start.15 = (f32[8,8,128]{2,1,0:T(8,128)S(1)}, f32[8,8,128]{2,1,0:T(8,128)}, u32[]{:S(2)}) copy-start(f32[8,8,128]{2,1,0:T(8,128)} %copy-done.14) | copy-start | bytes 98308
  81.4 1.9 %copy-start.20 = (f32[8,8,128]{2,1,0:T(8,128)S(1)}, f32[8,8,128]{2,1,0:T(8,128)}, u32[]{:S(2)}) copy-start(f32[8,8,128]{2,1,0:T(8,128)} %copy-done.19) | copy-start | bytes 98308
  81.4 1.9 %copy-start.22 = (f32[8,8,128]{2,1,0:T(8,128)S(1)}, f32[8,8,128]{2,1,0:T(8,128)}, u32[]{:S(2)}) copy-start(f32[8,8,128]{2,1,0:T(8,128)} %copy-done.21) | copy-start | bytes 98308
  81.4 1.9 %copy-start.24 = (f32[8,8,128]{2,1,0:T(8,128)S(1)}, f32[8,8,128]{2,1,0:T(8,128)}, u32[]{:S(2)}) copy-start(f32[8,8,128]{2,1,0:T(8,128)} %copy-done.23) | copy-start | bytes 98308
  81.4 1.9 %copy-start.34 = (f32[8,8,1]{2,1,0:T(8,128)S(1)}, f32[8,8,1]{2,1,0:T(8,128)}, u32[]{:S(2)}) copy-start(f32[8,8,1]{2,1,0:T(8,128)} %copy-done.33) | copy-start | bytes 772
  84.7 8.4 %collective-permute-start.6 = (f32[19,1,8,128]{3,2,1,0:T(8,128)S(1)}, f32[19,1,8,128]{3,2,1,0:T(8,128)S(1)}, u32[]{:S(2)}, u32[]{:S(2)}) collective-permute-start(f32[19,1,8,128]{3,2,1,0:T(8,128)S(1)} %get-tuple-element.105), channel_id=1, source_target_pairs={{8,0},{16,8},{24,16},{32,24},{40,32},{48,40},{56,48},{64,56},{72,6... | collective-permute-start | bytes 233480 | tf_op jit(solution)/shard_map/ppermute | solution.py:57
  91.1 14.5 %collective-permute-start.7 = (f32[19,1,8,128]{3,2,1,0:T(8,128)S(1)}, f32[19,1,8,128]{3,2,1,0:T(8,128)S(1)}, u32[]{:S(2)}, u32[]{:S(2)}) collective-permute-start(f32[19,1,8,128]{3,2,1,0:T(8,128)S(1)} %get-tuple-element.104), channel_id=1, source_target_pairs={{0,8},{8,16},{16,24},{24,32},{32,40},{40,48},{48,56},{56,64},{64,7... | collective-permute-start | bytes 233480 | tf_op jit(solution)/shard_map/ppermute | solution.py:54
  159.1 19.2 %collective-permute-start.8 = (f32[1,1,16]{2,1,0:T(1,128)S(1)}, f32[1,1,16]{2,1,0:T(1,128)S(1)}, u32[]{:S(2)}, u32[]{:S(2)}) collective-permute-start(f32[1,1,16]{2,1,0:T(1,128)S(1)} %broadcast_multiply_fusion.4), channel_id=1, source_target_pairs={{0,8},{8,16},{16,24},{24,32},{32,40},{40,48},{48,56},{56,64},{64,7... | collective-permute-start | bytes 200 | tf_op jit(solution)/shard_map/ppermute | solution.py:54
  161.0 17.3 %collective-permute-start.9 = (f32[1,1,16]{2,1,0:T(1,128)S(1)}, f32[1,1,16]{2,1,0:T(1,128)S(1)}, u32[]{:S(2)}, u32[]{:S(2)}) collective-permute-start(f32[1,1,16]{2,1,0:T(1,128)S(1)} %broadcast_multiply_fusion.4), channel_id=1, source_target_pairs={{8,0},{16,8},{24,16},{32,24},{40,32},{48,40},{56,48},{64,56},{72,6... | collective-permute-start | bytes 200 | tf_op jit(solution)/shard_map/ppermute | solution.py:57
  (76 other events, 83.0 us)
where the time goes:
time: 182 us; the launch traced here: 181 us
  starting transfers between devices  58.8 us (32%)
  blocking collectives  49.9 us (27%)
  other arithmetic  29.7 us (16%)
  local copies, waits for them, and re-layouts  20.7 us (11%)
  waiting for transfers between devices  18.7 us (10%)
  between operations  3.14 us (2%)
    psum x1, blocking collectives, body(): block_sens = SOLID_MAX * lax.psum(blocks, 'case')  49.9 us
    ppermute x5, starting transfers between devices, extended(): lax.ppermute(lax.slice_in_dim(block, 0, width, axis=dim), axis, backward)  48.7 us
    ppermute x5, waiting for transfers between devices, extended(): lax.ppermute(lax.slice_in_dim(block, block.shape[dim] - width, None, axis...  18.6 us
    unnamed x263, local copies, waits for them, and re-layouts  12.5 us
    ppermute x5, starting transfers between devices, extended(): lax.ppermute(lax.slice_in_dim(block, block.shape[dim] - width, None, axis...  10.1 us
    scatter-add x2, other arithmetic, collide(): flipped = post[jnp.array(OPPOSITE)]  5.86 us
    mul x1, other arithmetic, collide(): 3.0 * weight * density * forcing  4.33 us
    reduce_sum x2, other arithmetic, collide(): return (1.0 - solid) * post + solid * flipped  3.91 us
  transfers between devices with their start and end apart: 10, of which 3 were waited for; matrix products, arithmetic and copies ran while one was open for 12% of the time, Pallas kernels for 0%

commit v1 on v0

v1 whole, which is shorter than its diff:
```python
import functools

import jax
import jax.numpy as jnp
import numpy as np
from jax import lax
from jax.experimental import pallas as pl
from jax.experimental.pallas import tpu as pltpu
from jax.sharding import PartitionSpec as P

Q = 19
BLOCK = 8
VELOCITIES = [
    (0, 0, 0),
    (1, 0, 0),
    (-1, 0, 0),
    (0, 1, 0),
    (0, -1, 0),
    (0, 0, 1),
    (0, 0, -1),
    (1, 1, 0),
    (-1, -1, 0),
    (1, -1, 0),
    (-1, 1, 0),
    (1, 0, 1),
    (-1, 0, -1),
    (1, 0, -1),
    (-1, 0, 1),
    (0, 1, 1),
    (0, -1, -1),
    (0, 1, -1),
    (0, -1, 1),
]
W_REST, W_AXIS, W_DIAG = 1.0 / 3.0, 1.0 / 18.0, 1.0 / 36.0
RELAX_RATE = 0.9
SOLID_MAX = 0.5
FACE_WEIGHT = 0.5
ACCEL_SCALE = 400.0
BETA_ONE = 0.9
BETA_TWO = 0.999
LEARN_RATE = 0.2
ADAM_EPS = 1e-08
BIAS_ONE = 1.0 - 0.9**10
BIAS_TWO = 1.0 - 0.999**10

PAIRS = tuple(range(1, Q, 2))
Q_ZERO = [q for q in range(Q) if VELOCITIES[q][0] == 0]
Q_PLUS = [q for q in range(Q) if VELOCITIES[q][0] == 1]
Q_MINUS = [q for q in range(Q) if VELOCITIES[q][0] == -1]
N_NEAR = len(Q_ZERO) + len(Q_MINUS)
ROW_FAR = Q
ROW_ADJ = 2 * Q
ROW_ADJ_FAR = ROW_ADJ + N_NEAR
ROW_DESIGN = ROW_ADJ_FAR + len(Q_MINUS)
ROWS = ROW_DESIGN + 1
RUN = 16
GROUP = 4
OFFSET = 2


def shift_yz(value, vel_id, direction):
    _, shift_y, shift_z = VELOCITIES[vel_id]
    if shift_y:
        value = pltpu.roll(value, (direction * shift_y) % 8, 0)
    if shift_z:
        value = pltpu.roll(value, (direction * shift_z) % 128, 1)
    return value


def along(vector, vel_id):
    total = None
    for part, sign in zip(vector, VELOCITIES[vel_id]):
        if sign == 0:
            continue
        if total is None:
            total = part if sign > 0 else -part
        else:
            total = total + part if sign > 0 else total - part
    return total


def weight(pair):
    return W_AXIS if pair < 7 else W_DIAG


def moments(f):
    plus = {p: f[p] + f[p + 1] for p in PAIRS}
    minus = {p: f[p] - f[p + 1] for p in PAIRS}
    density = f[0]
    for p in PAIRS:
        density = density + plus[p]
    momentum = []
    for axis in range(3):
        total = None
        for p in PAIRS:
            sign = VELOCITIES[p][axis]
            if sign == 0:
                continue
            if total is None:
                total = minus[p]
            else:
                total = total + minus[p] if sign > 0 else total - minus[p]
        momentum.append(total)
    return density, momentum, plus, minus


def odd_parts(density, momentum, minus, accel):
    flow = [3.0 * RELAX_RATE * m + (3.0 * a) * density for m, a in zip(momentum, accel)]
    return {
        p: (1.0 - RELAX_RATE) * minus[p] + (2.0 * weight(p)) * along(flow, p) for p in PAIRS
    }


def collide(f, solid, accel):
    density, momentum, plus, minus = moments(f)
    odd = odd_parts(density, momentum, minus, accel)
    inverse = 1.0 / density
    velocity = [m * inverse for m in momentum]
    speed_sq = sum(m * u for m, u in zip(momentum, velocity))
    base = RELAX_RATE * (density - 1.5 * speed_sq)
    gray = {0: (1.0 - RELAX_RATE) * f[0] + W_REST * base}
    bent = 0.5 - solid
    for p in PAIRS:
        project = along(velocity, p)
        even = 0.5 * (1.0 - RELAX_RATE) * plus[p] + weight(p) * (
            base + (4.5 * RELAX_RATE) * density * (project * project)
        )
        turned = bent * odd[p]
        gray[p] = even + turned
        gray[p + 1] = even - turned
    return gray, odd


def collide_adjoint(f_moments, g, solid, accel):
    density, momentum = f_moments
    inverse = 1.0 / density
    velocity = [m * inverse for m in momentum]
    plus = {p: g[p] + g[p + 1] for p in PAIRS}
    fluid = 1.0 - 2.0 * solid
    minus = {p: fluid * (g[p] - g[p + 1]) for p in PAIRS}
    axis_sum = plus[1] + plus[3] + plus[5]
    diag_xy, diag_xz, diag_yz = plus[7] + plus[9], plus[11] + plus[13], plus[15] + plus[17]
    level = W_REST * g[0] + W_AXIS * axis_sum + W_DIAG * (diag_xy + diag_xz + diag_yz)
    second = {
        (0, 0): W_AXIS * plus[1] + W_DIAG * (diag_xy + diag_xz),
        (1, 1): W_AXIS * plus[3] + W_DIAG * (diag_xy + diag_yz),
        (2, 2): W_AXIS * plus[5] + W_DIAG * (diag_xz + diag_yz),
        (0, 1): W_DIAG * (plus[7] - plus[9]),
        (0, 2): W_DIAG * (plus[11] - plus[13]),
        (1, 2): W_DIAG * (plus[15] - plus[17]),
    }
    first = [
        W_AXIS * minus[1] + W_DIAG * (minus[7] + minus[9] + minus[11] + minus[13]),
        W_AXIS * minus[3] + W_DIAG * (minus[7] - minus[9] + minus[15] + minus[17]),
        W_AXIS * minus[5] + W_DIAG * (minus[11] - minus[13] + minus[15] - minus[17]),
    ]
    bent = [
        sum(second[(min(i, j), max(i, j))] * velocity[j] for j in range(3)) for i in range(3)
    ]
    pull = [
        RELAX_RATE * (3.0 * first[i] + 9.0 * bent[i] - (3.0 * level) * velocity[i])
        for i in range(3)
    ]
    speed_sq = sum(u * u for u in velocity)
    rest = RELAX_RATE * (
        level * (1.0 + 1.5 * speed_sq) - 4.5 * sum(b * u for b, u in zip(bent, velocity))
    )
    rest = rest + 3.0 * sum(a * b for a, b in zip(accel, first))
    out = {0: (1.0 - RELAX_RATE) * g[0] + rest}
    for p in PAIRS:
        even = 0.5 * (1.0 - RELAX_RATE) * plus[p] + rest
        odd = 0.5 * (1.0 - RELAX_RATE) * minus[p] + along(pull, p)
        out[p] = even + odd
        out[p + 1] = even - odd
    return out


def sens_terms(g, odd):
    return sum((g[p + 1] - g[p]) * odd[p] for p in PAIRS)


def lanes():
    return lax.broadcasted_iota(jnp.int32, (8, 128), 1)


def read_accel(accel_ref, turn):
    return [accel_ref[turn, axis].astype(jnp.float32) * (1.0 / ACCEL_SCALE) for axis in range(3)]


def pack_kernel(parity_ref, f_ref, adj_ref, design_ref, mask_ref, to_a, to_b, blocks_ref, row):
    row[...] = jnp.zeros_like(row)
    row[0:1, 0:16] = design_ref[...] * mask_ref[...].astype(jnp.float32)
    spread = jnp.take_along_axis(row[...], lanes() // BLOCK, axis=1)
    spread = jnp.broadcast_to(spread[0:1], (8, 128))
    blocks_ref[...] = spread
    to_a[ROW_DESIGN] = spread
    to_b[ROW_DESIGN] = spread

    def fill(out, right):
        near, far = (7, 6) if right else (0, 1)
        for q in range(Q):
            two = f_ref[q, 48:64, :] if right else f_ref[q, 0:16, :]
            two = two.astype(jnp.float32)
            low, high = two[0:8], two[8:16]
            out[q] = high if right else low
            out[ROW_FAR + q] = low if right else high
        moving = Q_MINUS if right else Q_PLUS
        for i, q in enumerate(Q_ZERO + moving):
            out[ROW_ADJ + i] = adj_ref[q, near]
        for i, q in enumerate(moving):
            out[ROW_ADJ_FAR + i] = adj_ref[q, far]

    @pl.when(parity_ref[0] == 0)
    def _():
        fill(to_b, False)
        fill(to_a, True)

    @pl.when(parity_ref[0] == 1)
    def _():
        fill(to_b, True)
        fill(to_a, False)


def smooth(beside, grid):
    around = beside + 2.0 * grid + pltpu.roll(grid, 8, 1) + pltpu.roll(grid, 120, 1)
    return (grid + FACE_WEIGHT * around) * (1.0 / (1.0 + 6.0 * FACE_WEIGHT))


def sens_kernel(
    parity_ref,
    accel_ref,
    f_ref,
    adj_ref,
    from_a,
    from_b,
    blocks_ref,
    low_ref,
    high_ref,
    g_out,
    f_out,
    solid_out,
    sum_out,
    turned_out,
    adj_ext,
    f_next,
    odd_ext,
    solid_ext,
):
    even = parity_ref[0] == 0

    def left(row):
        return jnp.where(even, from_b[row], from_a[row])

    def right(row):
        return jnp.where(even, from_a[row], from_b[row])

    own = blocks_ref[...]
    before, after = left(ROW_DESIGN), right(ROW_DESIGN)
    solid_own = SOLID_MAX * smooth(before + after, own)
    solid_before = SOLID_MAX * smooth(low_ref[...] + own, before)
    solid_after = SOLID_MAX * smooth(own + high_ref[...], after)
    for e in range(12):
        solid_ext[e] = solid_before if e < 2 else solid_own if e < 10 else solid_after
    solid_out[...] = solid_own

    for q in range(Q):
        f_out[q, 0] = left(ROW_FAR + q)
        f_out[q, 1] = left(q)
        f_out[q, 10] = right(q)
        f_out[q, 11] = right(ROW_FAR + q)
    for i, q in enumerate(Q_ZERO + Q_MINUS):
        adj_ext[q, 1] = left(ROW_ADJ + i)
    for i, q in enumerate(Q_ZERO + Q_PLUS):
        adj_ext[q, 10] = right(ROW_ADJ + i)
    for i, q in enumerate(Q_MINUS):
        adj_ext[q, 0] = left(ROW_ADJ_FAR + i)
    for i, q in enumerate(Q_PLUS):
        adj_ext[q, 11] = right(ROW_ADJ_FAR + i)
    for q in range(Q):
        for k in range(4):
            two = f_ref[q, 16 * k : 16 * k + 16, :].astype(jnp.float32)
            f_out[q, 2 + 2 * k] = two[0:8]
            f_out[q, 3 + 2 * k] = two[8:16]
        for x in range(8):
            adj_ext[q, 2 + x] = adj_ref[q, x]

    accel_first = read_accel(accel_ref, 0)
    accel_second = read_accel(accel_ref, 1)

    def forward(e, _):
        f = [f_out[q, e] for q in range(Q)]
        gray, odd = collide(f, solid_ext[e], accel_first)
        for q in range(Q):
            f_next[q, e + 1 + VELOCITIES[q][0]] = shift_yz(gray[q], q, 1)
        for i, p in enumerate(PAIRS):
            odd_ext[i, e] = odd[p]
        return 0

    lax.fori_loop(0, 12, forward, 0)

    def backward(e, total):
        f = [f_next[q, e + 1] for q in range(Q)]
        g = [shift_yz(adj_ext[q, e + VELOCITIES[q][0]], q, -1) for q in range(Q)]
        density, momentum, _, minus = moments(f)
        odd = odd_parts(density, momentum, minus, accel_second)
        inside = jnp.logical_and(e >= 2, e < 10)
        total = total + jnp.where(inside, sens_terms(g, odd), 0.0)
        adjoint = collide_adjoint((density, momentum), g, solid_ext[e], accel_second)
        for q in range(Q):
            g_out[q, e - VELOCITIES[q][0]] = shift_yz(adjoint[q], q, -1)
        return total

    total = lax.fori_loop(1, 11, backward, jnp.zeros((8, 128), jnp.float32))

    def early(e, total):
        g = [g_out[q, e] for q in range(Q)]
        odd = {p: odd_ext[i, e] for i, p in enumerate(PAIRS)}
        return total + sens_terms(g, odd)

    total = lax.fori_loop(2, 10, early, total)
    total = jnp.sum(total, axis=0, keepdims=True)
    total = jnp.broadcast_to(total, (8, 128))
    for step in (1, 2, 4):
        total = total + pltpu.roll(total, 128 - step, 1)
    total = jnp.where(lanes() % BLOCK == 0, total, 0.0)
    sum_out[...] = total[0:1]
    turned_out[...] = pltpu.roll(total, 1, 1)[0:1]


def start_kernel(accel_ref, g_ref, f_ref, solid_ref, out_ref):
    accel = read_accel(accel_ref, 0)
    solid = solid_ref[...]

    def layer(x, _):
        f = [f_ref[q, x + 2] for q in range(Q)]
        g = [g_ref[q, x + 2] for q in range(Q)]
        density, momentum, _, _ = moments(f)
        adjoint = collide_adjoint((density, momentum), g, solid, accel)
        for q in range(Q):
            out_ref[q, x] = adjoint[q]
        return 0

    lax.fori_loop(0, 8, layer, 0)


def update_kernel(
    cases,
    place_ref,
    sums_ref,
    design_ref,
    mask_ref,
    first_ref,
    second_ref,
    design_out,
    first_out,
    second_out,
):
    place = place_ref[0]
    totals = []
    for tile in range(GROUP):
        total = sums_ref[tile * cases]
        for case in range(1, cases):
            total = total + sums_ref[tile * cases + case]
        totals.append(jnp.broadcast_to(total, (8, 128)))
    ahead = pltpu.roll(totals[0], 127, 1)
    behind = pltpu.roll(totals[-1], 127, 1)
    line = [ahead] + totals + [behind]

    def pick(shift):
        value = line[shift]
        for k in range(1, GROUP):
            value = jnp.where(place == k, line[k + shift], value)
        return value

    gradient = SOLID_MAX * smooth(pick(0) + pick(2), pick(1))
    spots = jnp.minimum(lanes() * BLOCK, 127)
    gradient = jnp.take_along_axis(gradient, spots, axis=1)[0:1, 0:16]
    gradient = mask_ref[...].astype(jnp.float32) * gradient
    first = BETA_ONE * first_ref[...] + (1.0 - BETA_ONE) * gradient
    second = BETA_TWO * second_ref[...] + (1.0 - BETA_TWO) * gradient * gradient
    stepped = design_ref[...] - LEARN_RATE * (first * (1.0 / BIAS_ONE)) / (
        jnp.sqrt(second * (1.0 / BIAS_TWO)) + ADAM_EPS
    )
    design_out[...] = jnp.clip(stepped, 0.0, 1.0)
    first_out[...] = first
    second_out[...] = second


def tables(tiles, cases):
    run = RUN if tiles % RUN == 0 else tiles

    def device(tile, case):
        return (tile % tiles) * cases + case

    def near(tile, step, case):
        target = tile + step
        crossed = (target // run) != (tile // run)
        return device(target, case ^ 1 if crossed else case)

    chip, beyond, up, down, edge = [], [], [], [], []
    for tile in range(tiles):
        step = 1 if tile % 2 else -1
        for case in range(cases):
            here = device(tile, case)
            chip.append((here, device(tile ^ 1, case)))
            beyond.append((here, device(tile + step, case)))
            up.append((here, near(tile, 2, case)))
            down.append((here, near(tile, -2, case)))
            place = (tile - OFFSET) % GROUP
            if place == 0:
                edge.append((here, device(tile - 1, case)))
            if place == GROUP - 1:
                edge.append((here, device(tile + 1, case)))
    groups = [
        [device(OFFSET + g * GROUP + k, case) for k in range(GROUP) for case in range(cases)]
        for g in range(tiles // GROUP)
    ]
    return chip, beyond, up, down, edge, groups


VMEM_SPEC = pl.BlockSpec(memory_space=pltpu.VMEM)
SMEM_SPEC = pl.BlockSpec(memory_space=pltpu.SMEM)
F32 = jnp.float32


def body(
    tiles,
    cases,
    checkpoint,
    adjoint_field,
    accel_table,
    design,
    design_mask,
    first_moment,
    second_moment,
):
    axes = ("tile", "case")
    chip, beyond, up, down, edge, groups = tables(tiles, cases)
    tile = lax.axis_index("tile")
    parity = jnp.reshape(tile % 2, (1,)).astype(jnp.int32)
    place = jnp.reshape((tile - OFFSET) % GROUP, (1,)).astype(jnp.int32)
    f_zero = checkpoint.reshape(Q, 64, 128)
    adjoint = adjoint_field[0]
    accel = accel_table[0]
    flat = [a.reshape(1, 16) for a in (design, design_mask, first_moment, second_moment)]
    params = pltpu.CompilerParams(vmem_limit_bytes=32 * 1024 * 1024)

    face = jax.ShapeDtypeStruct((ROWS, 8, 128), F32)
    layer = jax.ShapeDtypeStruct((8, 128), F32)
    to_a, to_b, blocks = pl.pallas_call(
        pack_kernel,
        out_shape=(face, face, layer),
        in_specs=[SMEM_SPEC] + [VMEM_SPEC] * 4,
        out_specs=[VMEM_SPEC] * 3,
        scratch_shapes=[pltpu.VMEM((8, 128), F32)],
        compiler_params=params,
        name="pack_faces",
    )(parity, f_zero, adjoint, flat[0], flat[1])

    from_b = lax.ppermute(to_b, axes, beyond)
    from_a = lax.ppermute(to_a, axes, chip)
    low = lax.ppermute(blocks, axes, up)
    high = lax.ppermute(blocks, axes, down)

    ext = jax.ShapeDtypeStruct((Q, 12, 8, 128), F32)
    row = jax.ShapeDtypeStruct((1, 128), F32)
    g_one, f_ext, solid, sums, turned = pl.pallas_call(
        sens_kernel,
        out_shape=(ext, ext, layer, row, row),
        in_specs=[SMEM_SPEC] * 2 + [VMEM_SPEC] * 7,
        out_specs=[VMEM_SPEC] * 5,
        scratch_shapes=[
            pltpu.VMEM((Q, 12, 8, 128), F32),
            pltpu.VMEM((Q, 14, 8, 128), F32),
            pltpu.VMEM((len(PAIRS), 12, 8, 128), F32),
            pltpu.VMEM((12, 8, 128), F32),
        ],
        compiler_params=params,
        name="sensitivity",
    )(parity, accel, f_zero, adjoint, from_a, from_b, blocks, low, high)

    outside = lax.ppermute(turned, axes, edge)
    payload = jnp.broadcast_to((sums + outside)[None], (GROUP * cases, 1, 128))
    shared = lax.all_to_all(payload, axes, 0, 0, axis_index_groups=groups, tiled=True)

    start = pl.pallas_call(
        start_kernel,
        out_shape=jax.ShapeDtypeStruct((Q, 8, 8, 128), F32),
        in_specs=[SMEM_SPEC] + [VMEM_SPEC] * 3,
        out_specs=VMEM_SPEC,
        compiler_params=params,
        name="adjoint_start",
    )(accel, g_one, f_ext, solid)

    small = jax.ShapeDtypeStruct((1, 16), F32)
    updated = pl.pallas_call(
        functools.partial(update_kernel, cases),
        out_shape=(small, small, small),
        in_specs=[SMEM_SPEC] + [VMEM_SPEC] * 5,
        out_specs=[VMEM_SPEC] * 3,
        compiler_params=params,
        name="update",
    )(place, shared, *flat)
    return (start[None],) + tuple(u.reshape(1, 1, 16) for u in updated)


def solution(mesh):
    placed = (
        P("case", None, "tile", None, None),
        P("case", None, "tile", None, None),
        P("case", None, None),
        P("tile", None, None),
        P("tile", None, None),
        P("tile", None, None),
        P("tile", None, None),
    )
    return jax.shard_map(
        functools.partial(body, mesh.shape["tile"], mesh.shape["case"]),
        mesh=mesh,
        in_specs=placed,
        out_specs=(
            P("case", None, "tile", None, None),
            P("tile", None, None),
            P("tile", None, None),
            P("tile", None, None),
        ),
        check_vma=False,
    )
```

time: 182 us -> 71.8 us (0.39)
  the two profiles are of different devices: /device:TPU:32 before, /device:TPU:65 now
where the time goes in v1:
time: 71.8 us; the launch traced here: 71.4 us
  starting transfers between devices  39.9 us (56%)
  waiting for transfers between devices  20.1 us (28%)
  Pallas kernels  6.69 us (9%)
  local copies, waits for them, and re-layouts  3.98 us (6%)
  between operations  0.77 us (1%)
    all_to_all x1, starting transfers between devices, body(): lax.all_to_all(payload, axes, 0, 0, axis_index_groups=groups, tiled=True)  18.9 us
    all_to_all x1, waiting for transfers between devices, body(): lax.all_to_all(payload, axes, 0, 0, axis_index_groups=groups, tiled=True)  12.4 us
    ppermute x1, starting transfers between devices, body(): high = lax.ppermute(blocks, axes, down)  12 us
    ppermute x1, waiting for transfers between devices, body(): low = lax.ppermute(blocks, axes, up)  7.76 us
    pallas_call x1, Pallas kernels, body(): pl.pallas_call(sens_kernel, out_shape=(ext, ext, layer, row, row), in_spe...  4.12 us
    ppermute x1, starting transfers between devices, body(): from_b = lax.ppermute(to_b, axes, beyond)  3.9 us
    unnamed x14, local copies, waits for them, and re-layouts  3.37 us
    ppermute x1, starting transfers between devices, body(): from_a = lax.ppermute(to_a, axes, chip)  2.54 us
  transfers between devices with their start and end apart: 6, of which 2 were waited for; matrix products, arithmetic and copies ran while one was open for 0% of the time, Pallas kernels for 2%

profile of v1, /device:TPU:65, one launch (start us, length us, event | category | flops | bytes accessed | tf_op | source)
XLA Modules:
  0.0 71.4 jit_solution(11815925415822477975)
XLA Ops:
  0.6 0.0 copy-start.3
  0.7 0.0 copy-start.4
  0.7 0.6 copy-done.3
  1.3 0.0 copy-done.4
  1.3 0.0 copy-start
  1.3 1.1 %copy-done = f32[1,19,8,8,128]{4,3,2,1,0:T(8,128)S(1)} copy-done((f32[1,19,8,8,128]{4,3,2,1,0:T(8,128)S(1)}, f32[1,19,8,8,128]{4,3,2,1,0:T(8,128)}, u32[]{:S(2)}) %copy-start) | copy-done | bytes 622616
  2.4 0.0 copy-start.1
  2.4 1.0 %copy-done.1 = bf16[1,19,8,8,128]{4,3,2,1,0:T(8,128)(2,1)S(1)} copy-done((bf16[1,19,8,8,128]{4,3,2,1,0:T(8,128)(2,1)S(1)}, bf16[1,19,8,8,128]{4,3,2,1,0:T(8,128)(2,1)}, u32[]{:S(2)}) %copy-start.1) | copy-done | bytes 311320
  3.4 0.1 pack_faces.1
  3.5 2.5 %collective-permute-start = (f32[58,8,128]{2,1,0:T(8,128)S(1)}, f32[58,8,128]{2,1,0:T(8,128)S(1)}, u32[]{:S(2)}, u32[]{:S(2)}) collective-permute-start(f32[58,8,128]{2,1,0:T(8,128)S(1)} %get-tuple-element.15), channel_id=1, source_target_pairs={{0,8},{1,9},{2,10},{3,11},{4,12},{5,13},{6,14},{7,15},{8,0},{9,1},... | collective-permute-start | bytes 712712 | tf_op jit(solution)/shard_map/ppermute | solution.py:461
  6.0 3.9 %collective-permute-start.1 = (f32[58,8,128]{2,1,0:T(8,128)S(1)}, f32[58,8,128]{2,1,0:T(8,128)S(1)}, u32[]{:S(2)}, u32[]{:S(2)}) collective-permute-start(f32[58,8,128]{2,1,0:T(8,128)S(1)} %get-tuple-element.16), channel_id=1, source_target_pairs={{0,1016},{1,1017},{2,1018},{3,1019},{4,1020},{5,1021},{6,1022},{7,... | collective-permute-start | bytes 712712 | tf_op jit(solution)/shard_map/ppermute | solution.py:460
  9.9 0.0 copy-start.2
  9.9 12.0 %collective-permute-start.3 = (f32[8,128]{1,0:T(8,128)S(1)}, f32[8,128]{1,0:T(8,128)S(1)}, u32[]{:S(2)}, u32[]{:S(2)}) collective-permute-start(f32[8,128]{1,0:T(8,128)S(1)} %get-tuple-element.17.blocks_ref), channel_id=1, source_target_pairs={{0,1009},{1,1008},{2,1011},{3,1010},{4,1013},{5,1012},{6,1015},{7,... | collective-permute-start | bytes 12296 | tf_op jit(solution)/shard_map/ppermute | solution.py:463
  21.9 1.9 %collective-permute-start.2 = (f32[8,128]{1,0:T(8,128)S(1)}, f32[8,128]{1,0:T(8,128)S(1)}, u32[]{:S(2)}, u32[]{:S(2)}) collective-permute-start(f32[8,128]{1,0:T(8,128)S(1)} %get-tuple-element.17.blocks_ref), channel_id=1, source_target_pairs={{0,16},{1,17},{2,18},{3,19},{4,20},{5,21},{6,22},{7,23},{8,24},{9,... | collective-permute-start | bytes 12296 | tf_op jit(solution)/shard_map/ppermute | solution.py:462
  23.8 0.0 collective-permute-done.3.high_ref
  23.8 7.8 %collective-permute-done.2.low_ref = f32[8,128]{1,0:T(8,128)S(1)} collective-permute-done((f32[8,128]{1,0:T(8,128)S(1)}, f32[8,128]{1,0:T(8,128)S(1)}, u32[]{:S(2)}, u32[]{:S(2)}) %collective-permute-start.2) | collective-permute-done | bytes 4128 | tf_op jit(solution)/shard_map/ppermute | solution.py:462
  31.6 0.0 collective-permute-done.from_a
  31.6 0.0 collective-permute-done.1.from_b
  31.6 0.0 copy-done.2
  31.6 4.1 %sensitivity.1 = (f32[19,12,8,128]{3,2,1,0:T(8,128)S(1)}, f32[19,12,8,128]{3,2,1,0:T(8,128)S(1)}, f32[8,128]{1,0:T(8,128)S(1)}, f32[1,128]{1,0:T(1,128)S(1)}, f32[1,128]{1,0:T(1,128)S(1)}) custom-call(s32[1]{0:T(128)} %bitcast.1.parity_ref, s32[2,3]{1,0:T(2,128)S(1)} %bitcast.19, bf16[19,64,128]{2,1,0:T(8,128)(2,1)S(1)} %bitcast.18, ...), custom_call_target="tpu_custom_call" | custom-call | tf_op jit(solution)/shard_map/sensitivity/pallas_call | solution.py:467
  35.7 0.7 collective-permute-start.4
  36.4 0.0 collective-permute-done.4
  36.4 0.6 broadcast_in_dim.13
  37.0 18.9 %all-to-all-start = ((f32[32,1,128]{2,1,0:T(1,128)}), f32[32,1,128]{2,1,0:T(1,128)S(1)}, u32[]{:S(2)}, u32[]{:S(2)}) async-start(f32[32,1,128]{2,1,0:T(1,128)} %broadcast_in_dim.13), calls=%async_computation | async-start | bytes 32768 | tf_op jit(solution)/shard_map/all_to_all | solution.py:484
  55.9 1.8 %adjoint_start.1 = f32[19,8,8,128]{3,2,1,0:T(8,128)} custom-call(s32[2,3]{1,0:T(2,128)S(1)} %bitcast.20, f32[19,12,8,128]{3,2,1,0:T(8,128)S(1)} %get-tuple-element.18.g_ref, f32[19,12,8,128]{3,2,1,0:T(8,128)S(1)} %get-tuple-element.19.f_ref, f32[8,128]{1,0:T(8,128)S(1)} %get-tuple-element.20.solid_ref), custom_call_target="tpu_custom_call" | custom-call | tf_op jit(solution)/shard_map/adjoint_start/pallas_call | solution.py:486
  57.7 12.4 %all-to-all-done.sums_ref = f32[32,1,128]{2,1,0:T(1,128)S(1)} async-done(((f32[32,1,128]{2,1,0:T(1,128)}), f32[32,1,128]{2,1,0:T(1,128)S(1)}, u32[]{:S(2)}, u32[]{:S(2)}) %all-to-all-start) | async-done | bytes 16416 | tf_op jit(solution)/shard_map/all_to_all | solution.py:484
  70.1 0.0 copy-start.5
  70.1 0.0 copy-start.6
  70.1 0.7 copy-done.5
  70.7 0.0 copy-done.6
  70.7 0.7 update.1
  (1 shorter events, 0.0 us)
Async XLA Ops:
  0.6 0.7 copy-start.3
  0.7 0.7 copy-start.4
  1.3 1.1 %copy-start = (f32[1,19,8,8,128]{4,3,2,1,0:T(8,128)S(1)}, f32[1,19,8,8,128]{4,3,2,1,0:T(8,128)}, u32[]{:S(2)}) copy-start(f32[1,19,8,8,128]{4,3,2,1,0:T(8,128)} %param.8) | copy-start | bytes 1867780
  2.4 1.0 %copy-start.1 = (bf16[1,19,8,8,128]{4,3,2,1,0:T(8,128)(2,1)S(1)}, bf16[1,19,8,8,128]{4,3,2,1,0:T(8,128)(2,1)}, u32[]{:S(2)}) copy-start(bf16[1,19,8,8,128]{4,3,2,1,0:T(8,128)(2,1)} %param.7) | copy-start | bytes 933892
  3.5 28.1 %collective-permute-start = (f32[58,8,128]{2,1,0:T(8,128)S(1)}, f32[58,8,128]{2,1,0:T(8,128)S(1)}, u32[]{:S(2)}, u32[]{:S(2)}) collective-permute-start(f32[58,8,128]{2,1,0:T(8,128)S(1)} %get-tuple-element.15), channel_id=1, source_target_pairs={{0,8},{1,9},{2,10},{3,11},{4,12},{5,13},{6,14},{7,15},{8,0},{9,1},... | collective-permute-start | bytes 712712 | tf_op jit(solution)/shard_map/ppermute | solution.py:461
  6.0 25.6 %collective-permute-start.1 = (f32[58,8,128]{2,1,0:T(8,128)S(1)}, f32[58,8,128]{2,1,0:T(8,128)S(1)}, u32[]{:S(2)}, u32[]{:S(2)}) collective-permute-start(f32[58,8,128]{2,1,0:T(8,128)S(1)} %get-tuple-element.16), channel_id=1, source_target_pairs={{0,1016},{1,1017},{2,1018},{3,1019},{4,1020},{5,1021},{6,1022},{7,... | collective-permute-start | bytes 712712 | tf_op jit(solution)/shard_map/ppermute | solution.py:460
  9.9 21.7 %copy-start.2 = (s32[1,2,3]{2,1,0:T(2,128)S(1)}, s32[1,2,3]{2,1,0:T(2,128)}, u32[]{:S(2)}) copy-start(s32[1,2,3]{2,1,0:T(2,128)} %param.9) | copy-start | bytes 76
  9.9 13.9 %collective-permute-start.3 = (f32[8,128]{1,0:T(8,128)S(1)}, f32[8,128]{1,0:T(8,128)S(1)}, u32[]{:S(2)}, u32[]{:S(2)}) collective-permute-start(f32[8,128]{1,0:T(8,128)S(1)} %get-tuple-element.17.blocks_ref), channel_id=1, source_target_pairs={{0,1009},{1,1008},{2,1011},{3,1010},{4,1013},{5,1012},{6,1015},{7,... | collective-permute-start | bytes 12296 | tf_op jit(solution)/shard_map/ppermute | solution.py:463
  21.9 9.7 %collective-permute-start.2 = (f32[8,128]{1,0:T(8,128)S(1)}, f32[8,128]{1,0:T(8,128)S(1)}, u32[]{:S(2)}, u32[]{:S(2)}) collective-permute-start(f32[8,128]{1,0:T(8,128)S(1)} %get-tuple-element.17.blocks_ref), channel_id=1, source_target_pairs={{0,16},{1,17},{2,18},{3,19},{4,20},{5,21},{6,22},{7,23},{8,24},{9,... | collective-permute-start | bytes 12296 | tf_op jit(solution)/shard_map/ppermute | solution.py:462
  35.7 0.7 collective-permute-start.4
  37.0 33.0 %all-to-all-start = ((f32[32,1,128]{2,1,0:T(1,128)}), f32[32,1,128]{2,1,0:T(1,128)S(1)}, u32[]{:S(2)}, u32[]{:S(2)}) async-start(f32[32,1,128]{2,1,0:T(1,128)} %broadcast_in_dim.13), calls=%async_computation | async-start | bytes 32768 | tf_op jit(solution)/shard_map/all_to_all | solution.py:484
  70.1 0.7 copy-start.5
  70.1 0.7 copy-start.6

commit v2 on v1

v2 whole, which is shorter than its diff:
```python
import functools

import jax
import jax.numpy as jnp
import numpy as np
from jax import lax
from jax.experimental import pallas as pl
from jax.experimental.pallas import tpu as pltpu
from jax.sharding import PartitionSpec as P

Q = 19
BLOCK = 8
VELOCITIES = [
    (0, 0, 0),
    (1, 0, 0),
    (-1, 0, 0),
    (0, 1, 0),
    (0, -1, 0),
    (0, 0, 1),
    (0, 0, -1),
    (1, 1, 0),
    (-1, -1, 0),
    (1, -1, 0),
    (-1, 1, 0),
    (1, 0, 1),
    (-1, 0, -1),
    (1, 0, -1),
    (-1, 0, 1),
    (0, 1, 1),
    (0, -1, -1),
    (0, 1, -1),
    (0, -1, 1),
]
W_REST, W_AXIS, W_DIAG = 1.0 / 3.0, 1.0 / 18.0, 1.0 / 36.0
RELAX_RATE = 0.9
SOLID_MAX = 0.5
FACE_WEIGHT = 0.5
ACCEL_SCALE = 400.0
BETA_ONE = 0.9
BETA_TWO = 0.999
LEARN_RATE = 0.2
ADAM_EPS = 1e-08
BIAS_ONE = 1.0 - 0.9**10
BIAS_TWO = 1.0 - 0.999**10

PAIRS = tuple(range(1, Q, 2))
Q_ZERO = [q for q in range(Q) if VELOCITIES[q][0] == 0]
Q_PLUS = [q for q in range(Q) if VELOCITIES[q][0] == 1]
Q_MINUS = [q for q in range(Q) if VELOCITIES[q][0] == -1]
ROW_FAR = len(Q_ZERO) + len(Q_PLUS)
ROW_ADJ = ROW_FAR + len(Q_PLUS)
ROW_ADJ_FAR = ROW_ADJ + len(Q_ZERO) + len(Q_PLUS)
ROW_SOLID = ROW_ADJ_FAR + len(Q_PLUS)
ROWS = ROW_SOLID + 1
RAW_FAR = Q
RAW_ADJ = RAW_FAR + 2 * len(Q_PLUS)
RAW_ADJ_FAR = RAW_ADJ + len(Q_ZERO) + len(Q_PLUS)
RAW_ROWS = RAW_ADJ_FAR + len(Q_PLUS)
RUN = 16
GROUP = 8
OFFSET = 5


def shift_yz(value, vel_id, direction):
    _, shift_y, shift_z = VELOCITIES[vel_id]
    if shift_y:
        value = pltpu.roll(value, (direction * shift_y) % 8, 0)
    if shift_z:
        value = pltpu.roll(value, (direction * shift_z) % 128, 1)
    return value


def along(vector, vel_id):
    total = None
    for part, sign in zip(vector, VELOCITIES[vel_id]):
        if sign == 0:
            continue
        if total is None:
            total = part if sign > 0 else -part
        else:
            total = total + part if sign > 0 else total - part
    return total


def weight(pair):
    return W_AXIS if pair < 7 else W_DIAG


def moments(f):
    plus = {p: f[p] + f[p + 1] for p in PAIRS}
    minus = {p: f[p] - f[p + 1] for p in PAIRS}
    density = f[0]
    for p in PAIRS:
        density = density + plus[p]
    momentum = []
    for axis in range(3):
        total = None
        for p in PAIRS:
            sign = VELOCITIES[p][axis]
            if sign == 0:
                continue
            if total is None:
                total = minus[p]
            else:
                total = total + minus[p] if sign > 0 else total - minus[p]
        momentum.append(total)
    return density, momentum, plus, minus


def odd_parts(density, momentum, minus, accel):
    flow = [3.0 * RELAX_RATE * m + (3.0 * a) * density for m, a in zip(momentum, accel)]
    return {
        p: (1.0 - RELAX_RATE) * minus[p] + (2.0 * weight(p)) * along(flow, p) for p in PAIRS
    }


def collide(f, solid, accel):
    density, momentum, plus, minus = moments(f)
    odd = odd_parts(density, momentum, minus, accel)
    inverse = 1.0 / density
    velocity = [m * inverse for m in momentum]
    speed_sq = sum(m * u for m, u in zip(momentum, velocity))
    base = RELAX_RATE * (density - 1.5 * speed_sq)
    gray = {0: (1.0 - RELAX_RATE) * f[0] + W_REST * base}
    bent = 0.5 - solid
    for p in PAIRS:
        project = along(velocity, p)
        even = 0.5 * (1.0 - RELAX_RATE) * plus[p] + weight(p) * (
            base + (4.5 * RELAX_RATE) * density * (project * project)
        )
        turned = bent * odd[p]
        gray[p] = even + turned
        gray[p + 1] = even - turned
    return gray, odd


def collide_adjoint(f_moments, g, solid, accel):
    density, momentum = f_moments
    inverse = 1.0 / density
    velocity = [m * inverse for m in momentum]
    plus = {p: g[p] + g[p + 1] for p in PAIRS}
    fluid = 1.0 - 2.0 * solid
    minus = {p: fluid * (g[p] - g[p + 1]) for p in PAIRS}
    axis_sum = plus[1] + plus[3] + plus[5]
    diag_xy, diag_xz, diag_yz = plus[7] + plus[9], plus[11] + plus[13], plus[15] + plus[17]
    level = W_REST * g[0] + W_AXIS * axis_sum + W_DIAG * (diag_xy + diag_xz + diag_yz)
    second = {
        (0, 0): W_AXIS * plus[1] + W_DIAG * (diag_xy + diag_xz),
        (1, 1): W_AXIS * plus[3] + W_DIAG * (diag_xy + diag_yz),
        (2, 2): W_AXIS * plus[5] + W_DIAG * (diag_xz + diag_yz),
        (0, 1): W_DIAG * (plus[7] - plus[9]),
        (0, 2): W_DIAG * (plus[11] - plus[13]),
        (1, 2): W_DIAG * (plus[15] - plus[17]),
    }
    first = [
        W_AXIS * minus[1] + W_DIAG * (minus[7] + minus[9] + minus[11] + minus[13]),
        W_AXIS * minus[3] + W_DIAG * (minus[7] - minus[9] + minus[15] + minus[17]),
        W_AXIS * minus[5] + W_DIAG * (minus[11] - minus[13] + minus[15] - minus[17]),
    ]
    bent = [
        sum(second[(min(i, j), max(i, j))] * velocity[j] for j in range(3)) for i in range(3)
    ]
    pull = [
        RELAX_RATE * (3.0 * first[i] + 9.0 * bent[i] - (3.0 * level) * velocity[i])
        for i in range(3)
    ]
    speed_sq = sum(u * u for u in velocity)
    rest = RELAX_RATE * (
        level * (1.0 + 1.5 * speed_sq) - 4.5 * sum(b * u for b, u in zip(bent, velocity))
    )
    rest = rest + 3.0 * sum(a * b for a, b in zip(accel, first))
    out = {0: (1.0 - RELAX_RATE) * g[0] + rest}
    for p in PAIRS:
        even = 0.5 * (1.0 - RELAX_RATE) * plus[p] + rest
        odd = 0.5 * (1.0 - RELAX_RATE) * minus[p] + along(pull, p)
        out[p] = even + odd
        out[p + 1] = even - odd
    return out


def sens_terms(g, odd):
    return sum((g[p + 1] - g[p]) * odd[p] for p in PAIRS)


def lanes():
    return lax.broadcasted_iota(jnp.int32, (8, 128), 1)


def read_accel(accel_ref, turn):
    return [accel_ref[turn, axis] for axis in range(3)]


def is_even():
    return lax.axis_index("tile") & 1 == 0


def spread(row, blocks):
    row[...] = jnp.zeros_like(row)
    row[0:1, 0:16] = blocks
    wide = jnp.take_along_axis(row[...], lanes() // BLOCK, axis=1)
    return jnp.broadcast_to(wide[0:1], (8, 128))


def smooth(beside, grid):
    around = beside + 2.0 * grid + pltpu.roll(grid, 8, 1) + pltpu.roll(grid, 120, 1)
    return (grid + FACE_WEIGHT * around) * (1.0 / (1.0 + 6.0 * FACE_WEIGHT))


def read_layer(f_ref, q, x):
    two = f_ref[q, 16 * (x // 2) : 16 * (x // 2) + 16, :].astype(jnp.float32)
    return two[8:16] if x % 2 else two[0:8]


def pack(f_ref, adj_ref, out, high, solid, accel):
    near, far = (7, 6) if high else (0, 1)
    onward, back = (Q_PLUS, Q_MINUS) if high else (Q_MINUS, Q_PLUS)
    gray, _ = collide([read_layer(f_ref, q, near) for q in range(Q)], solid, accel)
    for i, q in enumerate(Q_ZERO + onward):
        out[i] = shift_yz(gray[q], q, 1)
    gray, _ = collide([read_layer(f_ref, q, far) for q in range(Q)], solid, accel)
    for i, q in enumerate(onward):
        out[ROW_FAR + i] = shift_yz(gray[q], q, 1)
    for i, q in enumerate(Q_ZERO + back):
        out[ROW_ADJ + i] = adj_ref[q, near]
    for i, q in enumerate(back):
        out[ROW_ADJ_FAR + i] = adj_ref[q, far]
    out[ROW_SOLID] = solid


def load_kernel(
    design_hbm,
    mask_hbm,
    accel_hbm,
    f_hbm,
    adj_hbm,
    blocks_out,
    accel_out,
    f_out,
    adj_out,
    design,
    mask,
    table,
    sems,
):
    copies = [
        pltpu.make_async_copy(source, target, sems.at[i])
        for i, (source, target) in enumerate(
            (
                (design_hbm, design),
                (mask_hbm, mask),
                (accel_hbm, table),
                (f_hbm, f_out),
                (adj_hbm, adj_out),
            )
        )
    ]
    for copy in copies:
        copy.start()
    for copy in copies[:3]:
        copy.wait()
    blocks_out[...] = design[...] * mask[...].astype(jnp.float32)
    for turn in range(2):
        for axis in range(3):
            value = table[turn, axis].astype(jnp.float32) * (1.0 / ACCEL_SCALE)
            accel_out[turn, axis] = jnp.full((8, 128), value, jnp.float32)
    for copy in copies[3:]:
        copy.wait()


def pack_raw(f_ref, adj_ref, out, high, accel):
    near, far = (7, 6) if high else (0, 1)
    back = Q_MINUS if high else Q_PLUS
    post, _ = collide([read_layer(f_ref, q, near) for q in range(Q)], 0.0, accel)
    for q in range(Q):
        out[q] = post[q]
    post, _ = collide([read_layer(f_ref, q, far) for q in range(Q)], 0.0, accel)
    for i, p in enumerate(Q_PLUS):
        out[RAW_FAR + 2 * i] = post[p]
        out[RAW_FAR + 2 * i + 1] = post[p + 1]
    for i, q in enumerate(Q_ZERO + back):
        out[RAW_ADJ + i] = adj_ref[q, near]
    for i, q in enumerate(back):
        out[RAW_ADJ_FAR + i] = adj_ref[q, far]


def duo_kernel(own_ref, mate_ref, duo_out):
    duo_out[0:1] = own_ref[...]
    duo_out[1:2] = mate_ref[...]


def raw_kernel(f_ref, adj_ref, accel_ref, duo_ref, to_b):
    del duo_ref
    accel = read_accel(accel_ref, 0)
    even = is_even()
    pl.when(even)(lambda: pack_raw(f_ref, adj_ref, to_b, False, accel))
    pl.when(jnp.logical_not(even))(lambda: pack_raw(f_ref, adj_ref, to_b, True, accel))


def pack_kernel(
    f_ref, adj_ref, accel_ref, own_ref, mate_ref, duo_ref, to_a, solid_out, solid_beyond, row
):
    duo = duo_ref[...]
    beside, past = duo[0:1], duo[1:2]
    own = spread(row, own_ref[...])
    solid = SOLID_MAX * smooth(spread(row, mate_ref[...] + beside), own)
    solid_out[...] = solid
    solid_beyond[...] = SOLID_MAX * smooth(own + spread(row, past), spread(row, beside))
    accel = read_accel(accel_ref, 0)
    even = is_even()
    pl.when(even)(lambda: pack(f_ref, adj_ref, to_a, True, solid, accel))
    pl.when(jnp.logical_not(even))(lambda: pack(f_ref, adj_ref, to_a, False, solid, accel))


def mid_kernel(
    accel_ref,
    solid_ref,
    f_ref,
    adj_ref,
    from_a,
    g_out,
    f_next,
    odd_out,
    mom_out,
    sum_out,
    adj_ext,
    solid_ext,
):
    even = is_even()
    solid_own = solid_ref[...]
    solid_mate = from_a[ROW_SOLID]
    for e in range(12):
        solid_ext[e] = solid_own if 2 <= e < 10 else solid_mate
    accel_first = read_accel(accel_ref, 0)
    accel_second = read_accel(accel_ref, 1)
    for q in range(Q):
        for x in range(8):
            adj_ext[q, 2 + x] = adj_ref[q, x]
        for e in (2, 3, 8, 9):
            g_out[q, e] = jnp.zeros((8, 128), jnp.float32)

    def forward(k, _):
        for half in range(2):
            e = 2 * k + 2 + half
            f = [
                f_ref[q, pl.ds(pl.multiple_of(16 * k, 16), 16), :].astype(jnp.float32)[
                    8 * half : 8 * half + 8
                ]
                for q in range(Q)
            ]
            gray, odd = collide(f, solid_own, accel_first)
            density, momentum, _, _ = moments(f)
            for i, part in enumerate([density] + momentum):
                mom_out[i, e - 2] = part
            for q in range(Q):
                f_next[q, e + 1 + VELOCITIES[q][0]] = shift_yz(gray[q], q, 1)
            for i, p in enumerate(PAIRS):
                odd_out[i, e] = odd[p]
        return 0

    lax.fori_loop(0, 4, forward, 0)

    def mate_side(low):
        face, near, far = (2, 1, 0) if low else (9, 10, 11)
        inward, outward = (Q_PLUS, Q_MINUS) if low else (Q_MINUS, Q_PLUS)
        for i, q in enumerate(Q_ZERO):
            f_next[q, near + 1] = from_a[i]
        for i, q in enumerate(inward):
            f_next[q, face + 1] = from_a[len(Q_ZERO) + i]
            f_next[q, near + 1] = from_a[ROW_FAR + i]
        for i, q in enumerate(Q_ZERO + outward):
            adj_ext[q, near] = from_a[ROW_ADJ + i]
        for i, q in enumerate(outward):
            adj_ext[q, far] = from_a[ROW_ADJ_FAR + i]

    pl.when(even)(lambda: mate_side(False))
    pl.when(jnp.logical_not(even))(lambda: mate_side(True))

    def backward(e, total):
        f = [f_next[q, e + 1] for q in range(Q)]
        g = [shift_yz(adj_ext[q, e + VELOCITIES[q][0]], q, -1) for q in range(Q)]
        density, momentum, _, minus = moments(f)
        odd = odd_parts(density, momentum, minus, accel_second)
        inside = jnp.logical_and(e >= 2, e < 10)
        total = total + jnp.where(inside, sens_terms(g, odd), 0.0)
        adjoint = collide_adjoint((density, momentum), g, solid_ext[e], accel_second)
        for q in range(Q):
            g_out[q, e - VELOCITIES[q][0]] = shift_yz(adjoint[q], q, -1)
        return total

    first = jnp.where(even, 3, 1)
    total = lax.fori_loop(first, first + 8, backward, jnp.zeros((8, 128), jnp.float32))

    def early(e, total):
        g = [g_out[q, e] for q in range(Q)]
        odd = {p: odd_out[i, e] for i, p in enumerate(PAIRS)}
        return total + sens_terms(g, odd)

    sum_out[...] = lax.fori_loop(2, 10, early, total)


def edge(low, message, solid_own, solid, f_next, adj_ref, accel):
    inward, outward = (Q_PLUS, Q_MINUS) if low else (Q_MINUS, Q_PLUS)
    beside, face, layer, behind = (2, 3, 0, 1) if low else (11, 10, 7, 6)
    adj = {q: message[RAW_ADJ + i] for i, q in enumerate(Q_ZERO + outward)}

    def mixed(row, q):
        if q == 0:
            return message[row]
        opposite = row + 1 if q % 2 else row - 1
        value = message[row]
        return shift_yz(value + solid * (message[opposite] - value), q, 1)

    first = 0 if low else 1
    f = {q: mixed(RAW_FAR + 2 * i + first, q) for i, q in enumerate(inward)}
    f.update({q: mixed(q, q) for q in Q_ZERO})
    f.update({q: f_next[q, beside] for q in outward})
    g = {q: message[RAW_ADJ_FAR + i] for i, q in enumerate(outward)}
    g.update({q: adj[q] for q in Q_ZERO})
    g.update({q: adj_ref[q, layer] for q in inward})
    g = {q: shift_yz(g[q], q, -1) for q in range(Q)}
    density, momentum, _, _ = moments(f)
    adj_beside = collide_adjoint((density, momentum), g, solid, accel)

    f = {q: f_next[q, face] for q in Q_ZERO + outward}
    f.update({q: mixed(q, q) for q in inward})
    g = {q: adj[q] for q in outward}
    g.update({q: adj_ref[q, layer] for q in Q_ZERO})
    g.update({q: adj_ref[q, behind] for q in inward})
    g = {q: shift_yz(g[q], q, -1) for q in range(Q)}
    density, momentum, _, minus = moments(f)
    odd = odd_parts(density, momentum, minus, accel)
    adj_face = collide_adjoint((density, momentum), g, solid_own, accel)
    adj_beside = {q: shift_yz(adj_beside[q], q, -1) for q in outward}
    adj_face = {q: shift_yz(adj_face[q], q, -1) for q in Q_ZERO + outward}
    return adj_beside, adj_face, sens_terms(g, odd)


def turned_odd(odd, q):
    return -odd[q] if q % 2 else odd[q - 1]


def post_kernel(
    message,
    accel_ref,
    solid_ref,
    beyond_ref,
    f_next,
    adj_ref,
    g_ref,
    odd_ref,
    sum_ref,
    head_out,
    tail_out,
    sums_out,
    turned_out,
    own_sum,
):
    for q in range(Q):
        head_out[q, 0] = g_ref[q, 2]
        head_out[q, 1] = g_ref[q, 3]
        tail_out[q, 0] = g_ref[q, 8]
        tail_out[q, 1] = g_ref[q, 9]

    def side(low):
        adj_beside, adj_face, own = edge(
            low,
            message,
            solid_ref[...],
            beyond_ref[...],
            f_next,
            adj_ref,
            read_accel(accel_ref, 1),
        )
        face, behind = (2, 3) if low else (9, 8)
        out, at_face, at_behind = (head_out, 0, 1) if low else (tail_out, 1, 0)
        first = {p: odd_ref[i, face] for i, p in enumerate(PAIRS)}
        second = {p: odd_ref[i, behind] for i, p in enumerate(PAIRS)}
        for q in Q_ZERO:
            if q:
                own = own + adj_face[q] * turned_odd(first, q)
            out[q, at_face] = adj_face[q]
        for q in Q_MINUS if low else Q_PLUS:
            own = own + adj_beside[q] * turned_odd(first, q)
            own = own + adj_face[q] * turned_odd(second, q)
            out[q, at_face] = adj_beside[q]
            out[q, at_behind] = adj_face[q]
        own_sum[...] = own

    even = is_even()
    pl.when(even)(lambda: side(True))
    pl.when(jnp.logical_not(even))(lambda: side(False))
    total = jnp.sum(own_sum[...] + sum_ref[...], axis=0, keepdims=True)
    total = jnp.broadcast_to(total, (8, 128))
    for step in (1, 2, 4):
        total = total + pltpu.roll(total, 128 - step, 1)
    total = jnp.where(lanes() % BLOCK == 0, total, 0.0)
    sums_out[...] = total[0:1]
    turned_out[...] = pltpu.roll(total, 1, 1)[0:1]


def start_kernel(accel_ref, solid_ref, g_ref, mom_ref, head_ref, tail_ref, out_ref):
    accel = read_accel(accel_ref, 0)
    solid = solid_ref[...]

    def layers(low, high, source, offset):
        def step(x, _):
            g = [source[q, x + offset] for q in range(Q)]
            momentum = [mom_ref[1 + axis, x] for axis in range(3)]
            adjoint = collide_adjoint((mom_ref[0, x], momentum), g, solid, accel)
            for q in range(Q):
                out_ref[q, x] = adjoint[q]
            return 0

        lax.fori_loop(low, high, step, 0)

    layers(0, 2, head_ref, 0)
    layers(2, 6, g_ref, 2)
    layers(6, 8, tail_ref, -6)


def share_kernel(sums_ref, outside_ref, out):
    out[...] = jnp.broadcast_to((sums_ref[...] + outside_ref[...])[None], out.shape)


def update_kernel(
    cases,
    sums_ref,
    design_ref,
    mask_ref,
    first_ref,
    second_ref,
    design_out,
    first_out,
    second_out,
):
    place = (lax.axis_index("tile") - OFFSET) & (GROUP - 1)
    totals = []
    for tile in range(GROUP):
        total = sums_ref[tile * cases]
        for case in range(1, cases):
            total = total + sums_ref[tile * cases + case]
        totals.append(jnp.broadcast_to(total, (8, 128)))

    line = [pltpu.roll(totals[0], 127, 1)] + totals + [pltpu.roll(totals[-1], 127, 1)]

    def pick(shift):
        value = line[shift]
        for k in range(1, GROUP):
            value = jnp.where(place == k, line[k + shift], value)
        return value

    gradient = SOLID_MAX * smooth(pick(0) + pick(2), pick(1))
    spots = jnp.minimum(lanes() * BLOCK, 127)
    gradient = jnp.take_along_axis(gradient, spots, axis=1)[0:1, 0:16]
    gradient = mask_ref[...].astype(jnp.float32) * gradient
    first = BETA_ONE * first_ref[...] + (1.0 - BETA_ONE) * gradient
    second = BETA_TWO * second_ref[...] + (1.0 - BETA_TWO) * gradient * gradient
    stepped = design_ref[...] - LEARN_RATE * (first * (1.0 / BIAS_ONE)) / (
        jnp.sqrt(second * (1.0 / BIAS_TWO)) + ADAM_EPS
    )
    design_out[...] = jnp.clip(stepped, 0.0, 1.0)
    first_out[...] = first
    second_out[...] = second


def tables(tiles, cases):
    run = RUN if tiles % RUN == 0 else tiles

    def device(tile, case):
        return (tile % tiles) * cases + case

    def near(tile, step, case):
        target = tile + step
        crossed = (target // run) != (tile // run)
        return device(target, case ^ 1 if crossed else case)

    found = {name: [] for name in ("chip", "beyond", "beside", "ends")}
    for tile in range(tiles):
        step = 1 if tile % 2 else -1
        for case in range(cases):
            here = device(tile, case)
            found["chip"].append((here, device(tile ^ 1, case)))
            found["beyond"].append((here, device(tile + step, case)))
            found["beside"].append((here, near(tile, step, case)))
            place = (tile - OFFSET) % GROUP
            if place == 0:
                found["ends"].append((here, device(tile - 1, case)))
            if place == GROUP - 1:
                found["ends"].append((here, device(tile + 1, case)))
    groups = [
        [device(OFFSET + g * GROUP + k, case) for k in range(GROUP) for case in range(cases)]
        for g in range(tiles // GROUP)
    ]
    return found, groups


VMEM_SPEC = pl.BlockSpec(memory_space=pltpu.VMEM)
HBM_SPEC = pl.BlockSpec(memory_space=pltpu.HBM)
F32 = jnp.float32


def body(
    tiles,
    cases,
    checkpoint,
    adjoint_field,
    accel_table,
    design,
    design_mask,
    first_moment,
    second_moment,
):
    axes = ("tile", "case")
    pairs, groups = tables(tiles, cases)
    f_zero = checkpoint.reshape(Q, 64, 128)
    adjoint = adjoint_field[0]
    flat = [a.reshape(1, 16) for a in (design, design_mask, first_moment, second_moment)]
    params = pltpu.CompilerParams(vmem_limit_bytes=32 * 1024 * 1024)

    def send(value, name):
        return lax.ppermute(value, axes, pairs[name])

    def call(kernel, name, out_shape, in_specs, scratch, *args):
        many = isinstance(out_shape, tuple)
        return pl.pallas_call(
            kernel,
            out_shape=out_shape,
            in_specs=in_specs,
            out_specs=[VMEM_SPEC] * len(out_shape) if many else VMEM_SPEC,
            scratch_shapes=scratch,
            compiler_params=params,
            name=name,
        )(*args)

    def shape(*dims):
        return jax.ShapeDtypeStruct(dims, F32)

    row = pltpu.VMEM((8, 128), F32)
    blocks, accel, f_zero, adjoint = call(
        load_kernel,
        "load",
        (
            shape(1, 16),
            shape(2, 3, 8, 128),
            jax.ShapeDtypeStruct((Q, 64, 128), jnp.bfloat16),
            shape(Q, 8, 8, 128),
        ),
        [HBM_SPEC] * 5,
        [
            pltpu.VMEM((1, 16), F32),
            pltpu.VMEM((1, 16), jnp.int32),
            pltpu.SMEM((2, 3), jnp.int32),
            pltpu.SemaphoreType.DMA((5,)),
        ],
        *(
            pltpu.with_memory_space_constraint(a, pltpu.HBM)
            for a in (flat[0], flat[1], accel_table[0], f_zero, adjoint)
        ),
    )
    mate = send(blocks, "chip")
    duo = call(duo_kernel, "chip_blocks", shape(2, 16), [VMEM_SPEC] * 2, [], blocks, mate)
    duo_beside = send(duo, "beside")
    to_b = call(
        raw_kernel,
        "pack_beyond",
        shape(RAW_ROWS, 8, 128),
        [VMEM_SPEC] * 4,
        [],
        f_zero,
        adjoint,
        accel,
        duo,
    )
    from_b = send(to_b, "beyond")
    to_a, solid, solid_beyond = call(
        pack_kernel,
        "pack_chip",
        (shape(ROWS, 8, 128), shape(8, 128), shape(8, 128)),
        [VMEM_SPEC] * 6,
        [row],
        f_zero,
        adjoint,
        accel,
        blocks,
        mate,
        duo_beside,
    )
    from_a = send(to_a, "chip")
    g_one, f_next, odd, mom, sums = call(
        mid_kernel,
        "middle",
        (
            shape(Q, 12, 8, 128),
            shape(Q, 14, 8, 128),
            shape(len(PAIRS), 12, 8, 128),
            shape(4, 8, 8, 128),
            shape(8, 128),
        ),
        [VMEM_SPEC] * 5,
        [pltpu.VMEM((Q, 12, 8, 128), F32), pltpu.VMEM((12, 8, 128), F32)],
        accel,
        solid,
        f_zero,
        adjoint,
        from_a,
    )
    head, tail, sums, turned = call(
        post_kernel,
        "chip_edge",
        (shape(Q, 2, 8, 128), shape(Q, 2, 8, 128), shape(1, 128), shape(1, 128)),
        [VMEM_SPEC] * 9,
        [row],
        from_b,
        accel,
        solid,
        solid_beyond,
        f_next,
        adjoint,
        g_one,
        odd,
        sums,
    )
    outside = send(turned, "ends")
    payload = call(
        share_kernel, "share", shape(GROUP * cases, 1, 128), [VMEM_SPEC] * 2, [], sums, outside
    )
    payload, head = lax.optimization_barrier((payload, head))
    shared = lax.all_to_all(payload, axes, 0, 0, axis_index_groups=groups, tiled=True)
    start = call(
        start_kernel,
        "adjoint_start",
        shape(Q, 8, 8, 128),
        [VMEM_SPEC] * 6,
        [],
        accel,
        solid,
        g_one,
        mom,
        head,
        tail,
    )
    small = shape(1, 16)
    updated = call(
        functools.partial(update_kernel, cases),
        "update",
        (small, small, small),
        [VMEM_SPEC] * 5,
        [],
        shared,
        *flat,
    )
    return (start[None],) + tuple(u.reshape(1, 1, 16) for u in updated)


def solution(mesh):
    placed = (
        P("case", None, "tile", None, None),
        P("case", None, "tile", None, None),
        P("case", None, None),
        P("tile", None, None),
        P("tile", None, None),
        P("tile", None, None),
        P("tile", None, None),
    )
    return jax.shard_map(
        functools.partial(body, mesh.shape["tile"], mesh.shape["case"]),
        mesh=mesh,
        in_specs=placed,
        out_specs=(
            P("case", None, "tile", None, None),
            P("tile", None, None),
            P("tile", None, None),
            P("tile", None, None),
        ),
        check_vma=False,
    )
```

time: 71.8 us -> 66.1 us (0.921)
  the two profiles are of different devices: /device:TPU:65 before, /device:TPU:1 now
where the time goes in v2:
time: 66.1 us; the launch traced here: 65.8 us
  starting transfers between devices  47.2 us (71%)
  waiting for transfers between devices  11.1 us (17%)
  Pallas kernels  6.75 us (10%)
  between operations  0.73 us (1%)
    ppermute x5, starting transfers between devices, send(): return lax.ppermute(value, axes, pairs[name])  30.5 us
    all_to_all x1, starting transfers between devices, body(): lax.all_to_all(payload, axes, 0, 0, axis_index_groups=groups, tiled=True)  16.7 us
    pallas_call x9, Pallas kernels, call(): pl.pallas_call(kernel, out_shape=out_shape, in_specs=in_specs, out_specs=...  6.75 us
    all_to_all x1, waiting for transfers between devices, body(): lax.all_to_all(payload, axes, 0, 0, axis_index_groups=groups, tiled=True)  6.17 us
    ppermute x5, waiting for transfers between devices, send(): return lax.ppermute(value, axes, pairs[name])  4.94 us
  transfers between devices with their start and end apart: 6, of which 4 were waited for; matrix products, arithmetic and copies ran while one was open for 0% of the time, Pallas kernels for 5%

profile of v2, /device:TPU:1, one launch (start us, length us, event | category | flops | bytes accessed | tf_op | source)
XLA Modules:
  0.0 65.8 jit_solution(17119725398214016537)
XLA Ops:
  0.6 1.2 %load.1 = (f32[1,16]{1,0:T(1,128)S(1)}, f32[2,3,8,128]{3,2,1,0:T(8,128)S(1)}, bf16[19,64,128]{2,1,0:T(8,128)(2,1)S(1)}, f32[19,8,8,128]{3,2,1,0:T(8,128)S(1)}) custom-call(f32[1,16]{1,0:T(1,128)} %bitcast.11, s32[1,16]{1,0:T(1,128)} %bitcast.13, s32[2,3]{1,0:T(2,128)} %bitcast.20, bf16[19,64,128]{2,1,0:T(8,128)(2,1)} %bitcast.19, f32[19,8,8,128]{3,2,1,0:T(8,128)} %bitcast.17), custom_call_target="tpu_custom_call" | custom-call | tf_op jit(solution)/shard_map/load/pallas_call | solution.py:625
  1.9 16.1 %collective-permute-start = (f32[1,16]{1,0:T(1,128)S(1)}, f32[1,16]{1,0:T(1,128)S(1)}, u32[]{:S(2)}, u32[]{:S(2)}) collective-permute-start(f32[1,16]{1,0:T(1,128)S(1)} %get-tuple-element.28.own_ref), channel_id=1, source_target_pairs={{0,8},{1,9},{2,10},{3,11},{4,12},{5,13},{6,14},{7,15},{8,0},{9,1},... | collective-permute-start | bytes 200 | tf_op jit(solution)/shard_map/ppermute | solution.py:621
  18.0 0.8 %collective-permute-done.mate_ref = f32[1,16]{1,0:T(1,128)S(1)} collective-permute-done((f32[1,16]{1,0:T(1,128)S(1)}, f32[1,16]{1,0:T(1,128)S(1)}, u32[]{:S(2)}, u32[]{:S(2)}) %collective-permute-start) | collective-permute-done | bytes 96 | tf_op jit(solution)/shard_map/ppermute | solution.py:621
  18.8 0.1 pack_beyond.1
  18.8 1.9 %collective-permute-start.3 = (f32[48,8,128]{2,1,0:T(8,128)S(1)}, f32[48,8,128]{2,1,0:T(8,128)S(1)}, u32[]{:S(2)}, u32[]{:S(2)}) collective-permute-start(f32[48,8,128]{2,1,0:T(8,128)S(1)} %pack_beyond.1), channel_id=1, source_target_pairs={{0,1016},{1,1017},{2,1018},{3,1019},{4,1020},{5,1021},{6,1022},{7,... | collective-permute-start | bytes 589832 | tf_op jit(solution)/shard_map/ppermute | solution.py:621
  20.8 3.6 %collective-permute-start.1 = (f32[2,16]{1,0:T(2,128)S(1)}, f32[2,16]{1,0:T(2,128)S(1)}, u32[]{:S(2)}, u32[]{:S(2)}) collective-permute-start(f32[2,16]{1,0:T(2,128)S(1)} %chip_blocks.1.duo_ref), channel_id=1, source_target_pairs={{0,1017},{1,1016},{2,1019},{3,1018},{4,1021},{5,1020},{6,1023},{7,... | collective-permute-start | bytes 392 | tf_op jit(solution)/shard_map/ppermute | solution.py:621
  24.4 3.1 %collective-permute-done.1.duo_ref = f32[2,16]{1,0:T(2,128)S(1)} collective-permute-done((f32[2,16]{1,0:T(2,128)S(1)}, f32[2,16]{1,0:T(2,128)S(1)}, u32[]{:S(2)}, u32[]{:S(2)}) %collective-permute-start.1) | collective-permute-done | bytes 160 | tf_op jit(solution)/shard_map/ppermute | solution.py:621
  27.5 0.3 pack_chip.1
  27.8 8.1 %collective-permute-start.2 = (f32[39,8,128]{2,1,0:T(8,128)S(1)}, f32[39,8,128]{2,1,0:T(8,128)S(1)}, u32[]{:S(2)}, u32[]{:S(2)}) collective-permute-start(f32[39,8,128]{2,1,0:T(8,128)S(1)} %get-tuple-element.30), channel_id=1, source_target_pairs={{0,8},{1,9},{2,10},{3,11},{4,12},{5,13},{6,14},{7,15},{8,0},{9,1},... | collective-permute-start | bytes 479240 | tf_op jit(solution)/shard_map/ppermute | solution.py:621
  36.0 1.0 %collective-permute-done.2.from_a = f32[39,8,128]{2,1,0:T(8,128)S(1)} collective-permute-done((f32[39,8,128]{2,1,0:T(8,128)S(1)}, f32[39,8,128]{2,1,0:T(8,128)S(1)}, u32[]{:S(2)}, u32[]{:S(2)}) %collective-permute-start.2) | collective-permute-done | bytes 159776 | tf_op jit(solution)/shard_map/ppermute | solution.py:621
  37.0 2.2 %middle.1 = (f32[19,12,8,128]{3,2,1,0:T(8,128)S(1)}, f32[19,14,8,128]{3,2,1,0:T(8,128)S(1)}, f32[9,12,8,128]{3,2,1,0:T(8,128)S(1)}, f32[4,8,8,128]{3,2,1,0:T(8,128)S(1)}, f32[8,128]{1,0:T(8,128)S(1)}) custom-call(f32[2,3,8,128]{3,2,1,0:T(8,128)S(1)} %get-tuple-element.25.accel_ref, f32[8,128]{1,0:T(8,128)S(1)} %get-tuple-element.29.solid_ref, ...), custom_call_target="tpu_custom_call" | custom-call | tf_op jit(solution)/shard_map/middle/pallas_call | solution.py:625
  39.1 0.0 collective-permute-done.3.message
  39.2 0.5 chip_edge.1
  39.7 0.0 copy-start
  39.7 0.0 copy-start.1
  39.7 0.0 copy-start.2
  39.7 0.0 copy-start.3
  39.7 0.8 %collective-permute-start.4 = (f32[1,128]{1,0:T(1,128)S(1)}, f32[1,128]{1,0:T(1,128)S(1)}, u32[]{:S(2)}, u32[]{:S(2)}) collective-permute-start(f32[1,128]{1,0:T(1,128)S(1)} %get-tuple-element.38), channel_id=1, source_target_pairs={{32,40},{33,41},{34,42},{35,43},{36,44},{37,45},{38,46},{39,47},{4... | collective-permute-start | bytes 1544 | tf_op jit(solution)/shard_map/ppermute | solution.py:621
  40.5 0.0 collective-permute-done.4.outside_ref
  40.5 0.6 share.1
  41.1 16.7 %all-to-all-start = ((f32[64,1,128]{2,1,0:T(1,128)}), f32[64,1,128]{2,1,0:T(1,128)S(1)}, u32[]{:S(2)}, u32[]{:S(2)}) async-start(f32[64,1,128]{2,1,0:T(1,128)} %share.1), calls=%async_computation | async-start | bytes 65536 | tf_op jit(solution)/shard_map/all_to_all | solution.py:728
  57.8 1.1 %adjoint_start.1 = f32[19,8,8,128]{3,2,1,0:T(8,128)} custom-call(f32[2,3,8,128]{3,2,1,0:T(8,128)S(1)} %get-tuple-element.25.accel_ref, f32[8,128]{1,0:T(8,128)S(1)} %get-tuple-element.29.solid_ref, f32[19,12,8,128]{3,2,1,0:T(8,128)S(1)} %get-tuple-element.31.g_ref, f32[4,8,8,128]{3,2,1,0:T(8,128)S(1)} %get-tuple-element.32.mom_ref, ...), custom_call_target="tpu_custom_call" | custom-call | tf_op jit(solution)/shard_map/adjoint_start/pallas_call | solution.py:625
  58.9 6.2 %all-to-all-done.sums_ref = f32[64,1,128]{2,1,0:T(1,128)S(1)} async-done(((f32[64,1,128]{2,1,0:T(1,128)}), f32[64,1,128]{2,1,0:T(1,128)S(1)}, u32[]{:S(2)}, u32[]{:S(2)}) %all-to-all-start) | async-done | bytes 32800 | tf_op jit(solution)/shard_map/all_to_all | solution.py:728
  65.1 0.0 copy-done
  65.1 0.0 copy-done.1
  65.1 0.0 copy-done.2
  65.1 0.0 copy-done.3
  65.1 0.7 %update.1 = (f32[1,16]{1,0:T(1,128)}, f32[1,16]{1,0:T(1,128)}, f32[1,16]{1,0:T(1,128)}) custom-call(f32[64,1,128]{2,1,0:T(1,128)S(1)} %all-to-all-done.sums_ref, f32[1,16]{1,0:T(1,128)S(1)} %bitcast.12, s32[1,16]{1,0:T(1,128)S(1)} %bitcast.14, f32[1,16]{1,0:T(1,128)S(1)} %bitcast.15, f32[1,16]{1,0:T(1,128)S(1)} %bitcast.16), custom_call_target="tpu_custom_call" | custom-call | tf_op jit(solution)/shard_map/update/pallas_call | solution.py:625
  (1 shorter events, 0.0 us)
Async XLA Ops:
  1.9 16.9 %collective-permute-start = (f32[1,16]{1,0:T(1,128)S(1)}, f32[1,16]{1,0:T(1,128)S(1)}, u32[]{:S(2)}, u32[]{:S(2)}) collective-permute-start(f32[1,16]{1,0:T(1,128)S(1)} %get-tuple-element.28.own_ref), channel_id=1, source_target_pairs={{0,8},{1,9},{2,10},{3,11},{4,12},{5,13},{6,14},{7,15},{8,0},{9,1},... | collective-permute-start | bytes 200 | tf_op jit(solution)/shard_map/ppermute | solution.py:621
  18.8 20.3 %collective-permute-start.3 = (f32[48,8,128]{2,1,0:T(8,128)S(1)}, f32[48,8,128]{2,1,0:T(8,128)S(1)}, u32[]{:S(2)}, u32[]{:S(2)}) collective-permute-start(f32[48,8,128]{2,1,0:T(8,128)S(1)} %pack_beyond.1), channel_id=1, source_target_pairs={{0,1016},{1,1017},{2,1018},{3,1019},{4,1020},{5,1021},{6,1022},{7,... | collective-permute-start | bytes 589832 | tf_op jit(solution)/shard_map/ppermute | solution.py:621
  20.8 6.8 %collective-permute-start.1 = (f32[2,16]{1,0:T(2,128)S(1)}, f32[2,16]{1,0:T(2,128)S(1)}, u32[]{:S(2)}, u32[]{:S(2)}) collective-permute-start(f32[2,16]{1,0:T(2,128)S(1)} %chip_blocks.1.duo_ref), channel_id=1, source_target_pairs={{0,1017},{1,1016},{2,1019},{3,1018},{4,1021},{5,1020},{6,1023},{7,... | collective-permute-start | bytes 392 | tf_op jit(solution)/shard_map/ppermute | solution.py:621
  27.8 9.1 %collective-permute-start.2 = (f32[39,8,128]{2,1,0:T(8,128)S(1)}, f32[39,8,128]{2,1,0:T(8,128)S(1)}, u32[]{:S(2)}, u32[]{:S(2)}) collective-permute-start(f32[39,8,128]{2,1,0:T(8,128)S(1)} %get-tuple-element.30), channel_id=1, source_target_pairs={{0,8},{1,9},{2,10},{3,11},{4,12},{5,13},{6,14},{7,15},{8,0},{9,1},... | collective-permute-start | bytes 479240 | tf_op jit(solution)/shard_map/ppermute | solution.py:621
  39.7 25.4 %copy-start = (f32[1,1,16]{2,1,0:T(1,128)S(1)}, f32[1,1,16]{2,1,0:T(1,128)}, u32[]{:S(2)}) copy-start(f32[1,1,16]{2,1,0:T(1,128)} %param.10) | copy-start | bytes 196
  39.7 25.4 %copy-start.1 = (s32[1,1,16]{2,1,0:T(1,128)S(1)}, s32[1,1,16]{2,1,0:T(1,128)}, u32[]{:S(2)}) copy-start(s32[1,1,16]{2,1,0:T(1,128)} %param.11) | copy-start | bytes 196
  39.7 25.4 %copy-start.2 = (f32[1,1,16]{2,1,0:T(1,128)S(1)}, f32[1,1,16]{2,1,0:T(1,128)}, u32[]{:S(2)}) copy-start(f32[1,1,16]{2,1,0:T(1,128)} %param.12) | copy-start | bytes 196
  39.7 25.4 %copy-start.3 = (f32[1,1,16]{2,1,0:T(1,128)S(1)}, f32[1,1,16]{2,1,0:T(1,128)}, u32[]{:S(2)}) copy-start(f32[1,1,16]{2,1,0:T(1,128)} %param.13) | copy-start | bytes 196
  39.7 0.8 %collective-permute-start.4 = (f32[1,128]{1,0:T(1,128)S(1)}, f32[1,128]{1,0:T(1,128)S(1)}, u32[]{:S(2)}, u32[]{:S(2)}) collective-permute-start(f32[1,128]{1,0:T(1,128)S(1)} %get-tuple-element.38), channel_id=1, source_target_pairs={{32,40},{33,41},{34,42},{35,43},{36,44},{37,45},{38,46},{39,47},{4... | collective-permute-start | bytes 1544 | tf_op jit(solution)/shard_map/ppermute | solution.py:621
  41.1 24.0 %all-to-all-start = ((f32[64,1,128]{2,1,0:T(1,128)}), f32[64,1,128]{2,1,0:T(1,128)S(1)}, u32[]{:S(2)}, u32[]{:S(2)}) async-start(f32[64,1,128]{2,1,0:T(1,128)} %share.1), calls=%async_computation | async-start | bytes 65536 | tf_op jit(solution)/shard_map/all_to_all | solution.py:728

commit v3 on v2

--- a/solution.py
+++ b/solution.py
@@ -52,10 +52,11 @@
 ROW_ADJ_FAR = ROW_ADJ + len(Q_ZERO) + len(Q_PLUS)
 ROW_SOLID = ROW_ADJ_FAR + len(Q_PLUS)
 ROWS = ROW_SOLID + 1
-RAW_FAR = Q
-RAW_ADJ = RAW_FAR + 2 * len(Q_PLUS)
-RAW_ADJ_FAR = RAW_ADJ + len(Q_ZERO) + len(Q_PLUS)
-RAW_ROWS = RAW_ADJ_FAR + len(Q_PLUS)
+B_FAR = Q
+B_ADJ = B_FAR + 2 * len(Q_PLUS)
+B_ADJ_FAR = B_ADJ + len(Q_ZERO) + len(Q_PLUS)
+B_BLOCKS = B_ADJ_FAR + len(Q_PLUS)
+B_ROWS = B_BLOCKS + 1
 RUN = 16
 GROUP = 8
 OFFSET = 5
@@ -267,7 +268,7 @@
         copy.wait()
 
 
-def pack_raw(f_ref, adj_ref, out, high, accel):
+def pack_beyond(f_ref, adj_ref, out, high, accel):
     near, far = (7, 6) if high else (0, 1)
     back = Q_MINUS if high else Q_PLUS
     post, _ = collide([read_layer(f_ref, q, near) for q in range(Q)], 0.0, accel)
@@ -275,48 +276,61 @@
         out[q] = post[q]
     post, _ = collide([read_layer(f_ref, q, far) for q in range(Q)], 0.0, accel)
     for i, p in enumerate(Q_PLUS):
-        out[RAW_FAR + 2 * i] = post[p]
-        out[RAW_FAR + 2 * i + 1] = post[p + 1]
+        out[B_FAR + 2 * i] = post[p]
+        out[B_FAR + 2 * i + 1] = post[p + 1]
     for i, q in enumerate(Q_ZERO + back):
-        out[RAW_ADJ + i] = adj_ref[q, near]
+        out[B_ADJ + i] = adj_ref[q, near]
     for i, q in enumerate(back):
-        out[RAW_ADJ_FAR + i] = adj_ref[q, far]
-
-
-def duo_kernel(own_ref, mate_ref, duo_out):
-    duo_out[0:1] = own_ref[...]
-    duo_out[1:2] = mate_ref[...]
-
-
-def raw_kernel(f_ref, adj_ref, accel_ref, duo_ref, to_b):
-    del duo_ref
+        out[B_ADJ_FAR + i] = adj_ref[q, far]
+
+
+def beyond_kernel(f_ref, adj_ref, accel_ref, own_ref, to_b, row):
     accel = read_accel(accel_ref, 0)
+    to_b[B_BLOCKS] = spread(row, own_ref[...])
     even = is_even()
-    pl.when(even)(lambda: pack_raw(f_ref, adj_ref, to_b, False, accel))
-    pl.when(jnp.logical_not(even))(lambda: pack_raw(f_ref, adj_ref, to_b, True, accel))
-
-
-def pack_kernel(
-    f_ref, adj_ref, accel_ref, own_ref, mate_ref, duo_ref, to_a, solid_out, solid_beyond, row
+    pl.when(even)(lambda: pack_beyond(f_ref, adj_ref, to_b, False, accel))
+    pl.when(jnp.logical_not(even))(lambda: pack_beyond(f_ref, adj_ref, to_b, True, accel))
+
+
+def chip_kernel(
+    f_ref,
+    adj_ref,
+    accel_ref,
+    own_ref,
+    mate_ref,
+    past_ref,
+    from_b,
+    to_a,
+    solid_out,
+    solid_beyond,
+    row,
 ):
-    duo = duo_ref[...]
-    beside, past = duo[0:1], duo[1:2]
     own = spread(row, own_ref[...])
-    solid = SOLID_MAX * smooth(spread(row, mate_ref[...] + beside), own)
+    beside = from_b[B_BLOCKS]
+    solid = SOLID_MAX * smooth(spread(row, mate_ref[...]) + beside, own)
     solid_out[...] = solid
-    solid_beyond[...] = SOLID_MAX * smooth(own + spread(row, past), spread(row, beside))
+    solid_beyond[...] = SOLID_MAX * smooth(own + spread(row, past_ref[...]), beside)
     accel = read_accel(accel_ref, 0)
     even = is_even()
     pl.when(even)(lambda: pack(f_ref, adj_ref, to_a, True, solid, accel))
     pl.when(jnp.logical_not(even))(lambda: pack(f_ref, adj_ref, to_a, False, solid, accel))
 
 
+def mix(message, solid, row, q):
+    value = message[row]
+    if q == 0:
+        return value
+    opposite = message[row + 1 if q % 2 else row - 1]
+    return shift_yz(value + solid * (opposite - value), q, 1)
+
+
 def mid_kernel(
     accel_ref,
     solid_ref,
+    beyond_ref,
     f_ref,
     adj_ref,
-    from_a,
+    from_b,
     g_out,
     f_next,
     odd_out,
@@ -327,11 +341,11 @@
 ):
     even = is_even()
     solid_own = solid_ref[...]
-    solid_mate = from_a[ROW_SOLID]
-    for e in range(12):
-        solid_ext[e] = solid_own if 2 <= e < 10 else solid_mate
+    solid_beyond = beyond_ref[...]
     accel_first = read_accel(accel_ref, 0)
     accel_second = read_accel(accel_ref, 1)
+    for e in range(1, 11):
+        solid_ext[e] = solid_own if 2 <= e < 10 else solid_beyond
     for q in range(Q):
         for x in range(8):
             adj_ext[q, 2 + x] = adj_ref[q, x]
@@ -359,21 +373,22 @@
 
     lax.fori_loop(0, 4, forward, 0)
 
-    def mate_side(low):
-        face, near, far = (2, 1, 0) if low else (9, 10, 11)
+    def far_side(low):
+        face, beside, far = (2, 1, 0) if low else (9, 10, 11)
         inward, outward = (Q_PLUS, Q_MINUS) if low else (Q_MINUS, Q_PLUS)
-        for i, q in enumerate(Q_ZERO):
-            f_next[q, near + 1] = from_a[i]
+        first = 0 if low else 1
+        for q in Q_ZERO:
+            f_next[q, beside + 1] = mix(from_b, solid_beyond, q, q)
         for i, q in enumerate(inward):
-            f_next[q, face + 1] = from_a[len(Q_ZERO) + i]
-            f_next[q, near + 1] = from_a[ROW_FAR + i]
+            f_next[q, face + 1] = mix(from_b, solid_beyond, q, q)
+            f_next[q, beside + 1] = mix(from_b, solid_beyond, B_FAR + 2 * i + first, q)
         for i, q in enumerate(Q_ZERO + outward):
-            adj_ext[q, near] = from_a[ROW_ADJ + i]
+            adj_ext[q, beside] = from_b[B_ADJ + i]
         for i, q in enumerate(outward):
-            adj_ext[q, far] = from_a[ROW_ADJ_FAR + i]
-
-    pl.when(even)(lambda: mate_side(False))
-    pl.when(jnp.logical_not(even))(lambda: mate_side(True))
+            adj_ext[q, far] = from_b[B_ADJ_FAR + i]
+
+    pl.when(even)(lambda: far_side(True))
+    pl.when(jnp.logical_not(even))(lambda: far_side(False))
 
     def backward(e, total):
         f = [f_next[q, e + 1] for q in range(Q)]
@@ -387,7 +402,7 @@
             g_out[q, e - VELOCITIES[q][0]] = shift_yz(adjoint[q], q, -1)
         return total
 
-    first = jnp.where(even, 3, 1)
+    first = jnp.where(even, 1, 3)
     total = lax.fori_loop(first, first + 8, backward, jnp.zeros((8, 128), jnp.float32))
 
     def early(e, total):
@@ -398,31 +413,23 @@
     sum_out[...] = lax.fori_loop(2, 10, early, total)
 
 
-def edge(low, message, solid_own, solid, f_next, adj_ref, accel):
+def edge(low, message, solid_own, f_next, adj_ref, accel):
     inward, outward = (Q_PLUS, Q_MINUS) if low else (Q_MINUS, Q_PLUS)
     beside, face, layer, behind = (2, 3, 0, 1) if low else (11, 10, 7, 6)
-    adj = {q: message[RAW_ADJ + i] for i, q in enumerate(Q_ZERO + outward)}
-
-    def mixed(row, q):
-        if q == 0:
-            return message[row]
-        opposite = row + 1 if q % 2 else row - 1
-        value = message[row]
-        return shift_yz(value + solid * (message[opposite] - value), q, 1)
-
-    first = 0 if low else 1
-    f = {q: mixed(RAW_FAR + 2 * i + first, q) for i, q in enumerate(inward)}
-    f.update({q: mixed(q, q) for q in Q_ZERO})
+    adj = {q: message[ROW_ADJ + i] for i, q in enumerate(Q_ZERO + outward)}
+
+    f = {q: message[ROW_FAR + i] for i, q in enumerate(inward)}
+    f.update({q: message[i] for i, q in enumerate(Q_ZERO)})
     f.update({q: f_next[q, beside] for q in outward})
-    g = {q: message[RAW_ADJ_FAR + i] for i, q in enumerate(outward)}
+    g = {q: message[ROW_ADJ_FAR + i] for i, q in enumerate(outward)}
     g.update({q: adj[q] for q in Q_ZERO})
     g.update({q: adj_ref[q, layer] for q in inward})
     g = {q: shift_yz(g[q], q, -1) for q in range(Q)}
     density, momentum, _, _ = moments(f)
-    adj_beside = collide_adjoint((density, momentum), g, solid, accel)
+    adj_beside = collide_adjoint((density, momentum), g, message[ROW_SOLID], accel)
 
     f = {q: f_next[q, face] for q in Q_ZERO + outward}
-    f.update({q: mixed(q, q) for q in inward})
+    f.update({q: message[len(Q_ZERO) + i] for i, q in enumerate(inward)})
     g = {q: adj[q] for q in outward}
     g.update({q: adj_ref[q, layer] for q in Q_ZERO})
     g.update({q: adj_ref[q, behind] for q in inward})
@@ -439,11 +446,10 @@
     return -odd[q] if q % 2 else odd[q - 1]
 
 
-def post_kernel(
+def edge_kernel(
     message,
     accel_ref,
     solid_ref,
-    beyond_ref,
     f_next,
     adj_ref,
     g_ref,
@@ -463,13 +469,7 @@
 
     def side(low):
         adj_beside, adj_face, own = edge(
-            low,
-            message,
-            solid_ref[...],
-            beyond_ref[...],
-            f_next,
-            adj_ref,
-            read_accel(accel_ref, 1),
+            low, message, solid_ref[...], f_next, adj_ref, read_accel(accel_ref, 1)
         )
         face, behind = (2, 3) if low else (9, 8)
         out, at_face, at_behind = (head_out, 0, 1) if low else (tail_out, 1, 0)
@@ -484,13 +484,13 @@
             own = own + adj_face[q] * turned_odd(second, q)
             out[q, at_face] = adj_beside[q]
             out[q, at_behind] = adj_face[q]
-        own_sum[...] = own
+        own_sum[...] = own + sum_ref[...]
 
     even = is_even()
-    pl.when(even)(lambda: side(True))
-    pl.when(jnp.logical_not(even))(lambda: side(False))
-    total = jnp.sum(own_sum[...] + sum_ref[...], axis=0, keepdims=True)
-    total = jnp.broadcast_to(total, (8, 128))
+    pl.when(even)(lambda: side(False))
+    pl.when(jnp.logical_not(even))(lambda: side(True))
+
+    total = jnp.broadcast_to(jnp.sum(own_sum[...], axis=0, keepdims=True), (8, 128))
     for step in (1, 2, 4):
         total = total + pltpu.roll(total, 128 - step, 1)
     total = jnp.where(lanes() % BLOCK == 0, total, 0.0)
@@ -574,14 +574,14 @@
         crossed = (target // run) != (tile // run)
         return device(target, case ^ 1 if crossed else case)
 
-    found = {name: [] for name in ("chip", "beyond", "beside", "ends")}
+    found = {name: [] for name in ("chip", "beyond", "past", "ends")}
     for tile in range(tiles):
         step = 1 if tile % 2 else -1
         for case in range(cases):
             here = device(tile, case)
             found["chip"].append((here, device(tile ^ 1, case)))
             found["beyond"].append((here, device(tile + step, case)))
-            found["beside"].append((here, near(tile, step, case)))
+            found["past"].append((here, near(tile, -2 * step, case)))
             place = (tile - OFFSET) % GROUP
             if place == 0:
                 found["ends"].append((here, device(tile - 1, case)))
@@ -657,33 +657,33 @@
             for a in (flat[0], flat[1], accel_table[0], f_zero, adjoint)
         ),
     )
-    mate = send(blocks, "chip")
-    duo = call(duo_kernel, "chip_blocks", shape(2, 16), [VMEM_SPEC] * 2, [], blocks, mate)
-    duo_beside = send(duo, "beside")
     to_b = call(
-        raw_kernel,
+        beyond_kernel,
         "pack_beyond",
-        shape(RAW_ROWS, 8, 128),
+        shape(B_ROWS, 8, 128),
         [VMEM_SPEC] * 4,
-        [],
+        [row],
         f_zero,
         adjoint,
         accel,
-        duo,
+        blocks,
     )
     from_b = send(to_b, "beyond")
+    mate = send(blocks, "chip")
+    past = send(blocks, "past")
     to_a, solid, solid_beyond = call(
-        pack_kernel,
+        chip_kernel,
         "pack_chip",
         (shape(ROWS, 8, 128), shape(8, 128), shape(8, 128)),
-        [VMEM_SPEC] * 6,
+        [VMEM_SPEC] * 7,
         [row],
         f_zero,
         adjoint,
         accel,
         blocks,
         mate,
-        duo_beside,
+        past,
+        from_b,
     )
     from_a = send(to_a, "chip")
     g_one, f_next, odd, mom, sums = call(
@@ -696,24 +696,24 @@
             shape(4, 8, 8, 128),
             shape(8, 128),
         ),
-        [VMEM_SPEC] * 5,
+        [VMEM_SPEC] * 6,
         [pltpu.VMEM((Q, 12, 8, 128), F32), pltpu.VMEM((12, 8, 128), F32)],
         accel,
         solid,
+        solid_beyond,
         f_zero,
         adjoint,
-        from_a,
+        from_b,
     )
     head, tail, sums, turned = call(
-        post_kernel,
+        edge_kernel,
         "chip_edge",
         (shape(Q, 2, 8, 128), shape(Q, 2, 8, 128), shape(1, 128), shape(1, 128)),
-        [VMEM_SPEC] * 9,
+        [VMEM_SPEC] * 8,
         [row],
-        from_b,
+        from_a,
         accel,
         solid,
-        solid_beyond,
         f_next,
         adjoint,
         g_one,

time: 66.1 us -> 64 us (0.968)
  waiting for transfers between devices: 11.1 us -> 7.25 us
  starting transfers between devices: 47.2 us -> 48.8 us
    ppermute x5, waiting for transfers between devices: 4.94 us -> 1.09 us  [send(): return lax.ppermute(value, axes, pairs[name])]
    ppermute x5, starting transfers between devices: 30.5 us -> 31.5 us  [send(): return lax.ppermute(value, axes, pairs[name])]
    pallas_call x9 -> x8, Pallas kernels: 6.75 us -> 6.89 us  [call(): pl.pallas_call(kernel, out_shape=out_shape, in_specs=in_specs, out_specs=...]
  transfers between devices with their start and end apart: 6 -> 6, of which waited for: 4 -> 2; matrix products, arithmetic and copies ran while one was open for 0% -> 0% of each run, Pallas kernels for 5% -> 5%
where the time goes in v3:
time: 64 us; the launch traced here: 63.7 us
  starting transfers between devices  48.8 us (76%)
  waiting for transfers between devices  7.25 us (11%)
  Pallas kernels  6.89 us (11%)
  between operations  0.74 us (1%)
    ppermute x5, starting transfers between devices, send(): return lax.ppermute(value, axes, pairs[name])  31.5 us
    all_to_all x1, starting transfers between devices, body(): lax.all_to_all(payload, axes, 0, 0, axis_index_groups=groups, tiled=True)  17.3 us
    pallas_call x8, Pallas kernels, call(): pl.pallas_call(kernel, out_shape=out_shape, in_specs=in_specs, out_specs=...  6.89 us
    all_to_all x1, waiting for transfers between devices, body(): lax.all_to_all(payload, axes, 0, 0, axis_index_groups=groups, tiled=True)  6.17 us
  transfers between devices with their start and end apart: 6, of which 2 were waited for; matrix products, arithmetic and copies ran while one was open for 0% of the time, Pallas kernels for 5%

profile of v3, /device:TPU:1, one launch (start us, length us, event | category | flops | bytes accessed | tf_op | source)
XLA Modules:
  0.0 63.7 jit_solution(10052116348974307186)
XLA Ops:
  0.6 1.2 %load.1 = (f32[1,16]{1,0:T(1,128)S(1)}, f32[2,3,8,128]{3,2,1,0:T(8,128)S(1)}, bf16[19,64,128]{2,1,0:T(8,128)(2,1)S(1)}, f32[19,8,8,128]{3,2,1,0:T(8,128)S(1)}) custom-call(f32[1,16]{1,0:T(1,128)} %bitcast.11, s32[1,16]{1,0:T(1,128)} %bitcast.13, s32[2,3]{1,0:T(2,128)} %bitcast.20, bf16[19,64,128]{2,1,0:T(8,128)(2,1)} %bitcast.19, f32[19,8,8,128]{3,2,1,0:T(8,128)} %bitcast.17), custom_call_target="tpu_custom_call" | custom-call | tf_op jit(solution)/shard_map/load/pallas_call | solution.py:625
  1.9 0.2 pack_beyond.1
  2.0 5.4 %collective-permute-start.2 = (f32[49,8,128]{2,1,0:T(8,128)S(1)}, f32[49,8,128]{2,1,0:T(8,128)S(1)}, u32[]{:S(2)}, u32[]{:S(2)}) collective-permute-start(f32[49,8,128]{2,1,0:T(8,128)S(1)} %pack_beyond.1), channel_id=1, source_target_pairs={{0,1016},{1,1017},{2,1018},{3,1019},{4,1020},{5,1021},{6,1022},{7,... | collective-permute-start | bytes 602120 | tf_op jit(solution)/shard_map/ppermute | solution.py:621
  7.4 19.4 %collective-permute-start.1 = (f32[1,16]{1,0:T(1,128)S(1)}, f32[1,16]{1,0:T(1,128)S(1)}, u32[]{:S(2)}, u32[]{:S(2)}) collective-permute-start(f32[1,16]{1,0:T(1,128)S(1)} %get-tuple-element.28.own_ref), channel_id=1, source_target_pairs={{0,16},{1,17},{2,18},{3,19},{4,20},{5,21},{6,22},{7,23},{8,1017},{... | collective-permute-start | bytes 200 | tf_op jit(solution)/shard_map/ppermute | solution.py:621
  26.8 1.9 %collective-permute-start = (f32[1,16]{1,0:T(1,128)S(1)}, f32[1,16]{1,0:T(1,128)S(1)}, u32[]{:S(2)}, u32[]{:S(2)}) collective-permute-start(f32[1,16]{1,0:T(1,128)S(1)} %get-tuple-element.28.own_ref), channel_id=1, source_target_pairs={{0,8},{1,9},{2,10},{3,11},{4,12},{5,13},{6,14},{7,15},{8,0},{9,1},... | collective-permute-start | bytes 200 | tf_op jit(solution)/shard_map/ppermute | solution.py:621
  28.8 0.0 collective-permute-done.1.past_ref
  28.8 1.1 %collective-permute-done.mate_ref = f32[1,16]{1,0:T(1,128)S(1)} collective-permute-done((f32[1,16]{1,0:T(1,128)S(1)}, f32[1,16]{1,0:T(1,128)S(1)}, u32[]{:S(2)}, u32[]{:S(2)}) %collective-permute-start) | collective-permute-done | bytes 96 | tf_op jit(solution)/shard_map/ppermute | solution.py:621
  29.8 0.0 collective-permute-done.2.from_b
  29.9 0.3 pack_chip.1
  30.1 4.0 %collective-permute-start.3 = (f32[39,8,128]{2,1,0:T(8,128)S(1)}, f32[39,8,128]{2,1,0:T(8,128)S(1)}, u32[]{:S(2)}, u32[]{:S(2)}) collective-permute-start(f32[39,8,128]{2,1,0:T(8,128)S(1)} %get-tuple-element.33), channel_id=1, source_target_pairs={{0,8},{1,9},{2,10},{3,11},{4,12},{5,13},{6,14},{7,15},{8,0},{9,1},... | collective-permute-start | bytes 479240 | tf_op jit(solution)/shard_map/ppermute | solution.py:621
  34.1 2.3 %middle.1 = (f32[19,12,8,128]{3,2,1,0:T(8,128)S(1)}, f32[19,14,8,128]{3,2,1,0:T(8,128)S(1)}, f32[9,12,8,128]{3,2,1,0:T(8,128)S(1)}, f32[4,8,8,128]{3,2,1,0:T(8,128)S(1)}, f32[8,128]{1,0:T(8,128)S(1)}) custom-call(f32[2,3,8,128]{3,2,1,0:T(8,128)S(1)} %get-tuple-element.25.accel_ref, f32[8,128]{1,0:T(8,128)S(1)} %get-tuple-element.29.solid_ref, ...), custom_call_target="tpu_custom_call" | custom-call | tf_op jit(solution)/shard_map/middle/pallas_call | solution.py:625
  36.4 0.0 collective-permute-done.3.message
  36.4 0.5 chip_edge.1
  36.9 0.0 copy-start
  36.9 0.0 copy-start.1
  36.9 0.0 copy-start.2
  36.9 0.0 copy-start.3
  36.9 0.8 %collective-permute-start.4 = (f32[1,128]{1,0:T(1,128)S(1)}, f32[1,128]{1,0:T(1,128)S(1)}, u32[]{:S(2)}, u32[]{:S(2)}) collective-permute-start(f32[1,128]{1,0:T(1,128)S(1)} %get-tuple-element.38), channel_id=1, source_target_pairs={{32,40},{33,41},{34,42},{35,43},{36,44},{37,45},{38,46},{39,47},{4... | collective-permute-start | bytes 1544 | tf_op jit(solution)/shard_map/ppermute | solution.py:621
  37.7 0.0 collective-permute-done.4.outside_ref
  37.7 0.6 share.1
  38.4 17.3 %all-to-all-start = ((f32[64,1,128]{2,1,0:T(1,128)}), f32[64,1,128]{2,1,0:T(1,128)S(1)}, u32[]{:S(2)}, u32[]{:S(2)}) async-start(f32[64,1,128]{2,1,0:T(1,128)} %share.1), calls=%async_computation | async-start | bytes 65536 | tf_op jit(solution)/shard_map/all_to_all | solution.py:728
  55.6 1.1 %adjoint_start.1 = f32[19,8,8,128]{3,2,1,0:T(8,128)} custom-call(f32[2,3,8,128]{3,2,1,0:T(8,128)S(1)} %get-tuple-element.25.accel_ref, f32[8,128]{1,0:T(8,128)S(1)} %get-tuple-element.29.solid_ref, f32[19,12,8,128]{3,2,1,0:T(8,128)S(1)} %get-tuple-element.31.g_ref, f32[4,8,8,128]{3,2,1,0:T(8,128)S(1)} %get-tuple-element.32.mom_ref, ...), custom_call_target="tpu_custom_call" | custom-call | tf_op jit(solution)/shard_map/adjoint_start/pallas_call | solution.py:625
  56.8 6.2 %all-to-all-done.sums_ref = f32[64,1,128]{2,1,0:T(1,128)S(1)} async-done(((f32[64,1,128]{2,1,0:T(1,128)}), f32[64,1,128]{2,1,0:T(1,128)S(1)}, u32[]{:S(2)}, u32[]{:S(2)}) %all-to-all-start) | async-done | bytes 32800 | tf_op jit(solution)/shard_map/all_to_all | solution.py:728
  62.9 0.0 copy-done
  62.9 0.0 copy-done.1
  62.9 0.0 copy-done.2
  63.0 0.0 copy-done.3
  63.0 0.7 %update.1 = (f32[1,16]{1,0:T(1,128)}, f32[1,16]{1,0:T(1,128)}, f32[1,16]{1,0:T(1,128)}) custom-call(f32[64,1,128]{2,1,0:T(1,128)S(1)} %all-to-all-done.sums_ref, f32[1,16]{1,0:T(1,128)S(1)} %bitcast.12, s32[1,16]{1,0:T(1,128)S(1)} %bitcast.14, f32[1,16]{1,0:T(1,128)S(1)} %bitcast.15, f32[1,16]{1,0:T(1,128)S(1)} %bitcast.16), custom_call_target="tpu_custom_call" | custom-call | tf_op jit(solution)/shard_map/update/pallas_call | solution.py:625
Async XLA Ops:
  2.0 27.8 %collective-permute-start.2 = (f32[49,8,128]{2,1,0:T(8,128)S(1)}, f32[49,8,128]{2,1,0:T(8,128)S(1)}, u32[]{:S(2)}, u32[]{:S(2)}) collective-permute-start(f32[49,8,128]{2,1,0:T(8,128)S(1)} %pack_beyond.1), channel_id=1, source_target_pairs={{0,1016},{1,1017},{2,1018},{3,1019},{4,1020},{5,1021},{6,1022},{7,... | collective-permute-start | bytes 602120 | tf_op jit(solution)/shard_map/ppermute | solution.py:621
  7.4 21.3 %collective-permute-start.1 = (f32[1,16]{1,0:T(1,128)S(1)}, f32[1,16]{1,0:T(1,128)S(1)}, u32[]{:S(2)}, u32[]{:S(2)}) collective-permute-start(f32[1,16]{1,0:T(1,128)S(1)} %get-tuple-element.28.own_ref), channel_id=1, source_target_pairs={{0,16},{1,17},{2,18},{3,19},{4,20},{5,21},{6,22},{7,23},{8,1017},{... | collective-permute-start | bytes 200 | tf_op jit(solution)/shard_map/ppermute | solution.py:621
  26.8 3.0 %collective-permute-start = (f32[1,16]{1,0:T(1,128)S(1)}, f32[1,16]{1,0:T(1,128)S(1)}, u32[]{:S(2)}, u32[]{:S(2)}) collective-permute-start(f32[1,16]{1,0:T(1,128)S(1)} %get-tuple-element.28.own_ref), channel_id=1, source_target_pairs={{0,8},{1,9},{2,10},{3,11},{4,12},{5,13},{6,14},{7,15},{8,0},{9,1},... | collective-permute-start | bytes 200 | tf_op jit(solution)/shard_map/ppermute | solution.py:621
  30.1 6.3 %collective-permute-start.3 = (f32[39,8,128]{2,1,0:T(8,128)S(1)}, f32[39,8,128]{2,1,0:T(8,128)S(1)}, u32[]{:S(2)}, u32[]{:S(2)}) collective-permute-start(f32[39,8,128]{2,1,0:T(8,128)S(1)} %get-tuple-element.33), channel_id=1, source_target_pairs={{0,8},{1,9},{2,10},{3,11},{4,12},{5,13},{6,14},{7,15},{8,0},{9,1},... | collective-permute-start | bytes 479240 | tf_op jit(solution)/shard_map/ppermute | solution.py:621
  36.9 26.0 %copy-start = (f32[1,1,16]{2,1,0:T(1,128)S(1)}, f32[1,1,16]{2,1,0:T(1,128)}, u32[]{:S(2)}) copy-start(f32[1,1,16]{2,1,0:T(1,128)} %param.10) | copy-start | bytes 196
  36.9 26.0 %copy-start.1 = (s32[1,1,16]{2,1,0:T(1,128)S(1)}, s32[1,1,16]{2,1,0:T(1,128)}, u32[]{:S(2)}) copy-start(s32[1,1,16]{2,1,0:T(1,128)} %param.11) | copy-start | bytes 196
  36.9 26.0 %copy-start.2 = (f32[1,1,16]{2,1,0:T(1,128)S(1)}, f32[1,1,16]{2,1,0:T(1,128)}, u32[]{:S(2)}) copy-start(f32[1,1,16]{2,1,0:T(1,128)} %param.12) | copy-start | bytes 196
  36.9 26.0 %copy-start.3 = (f32[1,1,16]{2,1,0:T(1,128)S(1)}, f32[1,1,16]{2,1,0:T(1,128)}, u32[]{:S(2)}) copy-start(f32[1,1,16]{2,1,0:T(1,128)} %param.13) | copy-start | bytes 196
  36.9 0.8 %collective-permute-start.4 = (f32[1,128]{1,0:T(1,128)S(1)}, f32[1,128]{1,0:T(1,128)S(1)}, u32[]{:S(2)}, u32[]{:S(2)}) collective-permute-start(f32[1,128]{1,0:T(1,128)S(1)} %get-tuple-element.38), channel_id=1, source_target_pairs={{32,40},{33,41},{34,42},{35,43},{36,44},{37,45},{38,46},{39,47},{4... | collective-permute-start | bytes 1544 | tf_op jit(solution)/shard_map/ppermute | solution.py:621
  38.4 24.6 %all-to-all-start = ((f32[64,1,128]{2,1,0:T(1,128)}), f32[64,1,128]{2,1,0:T(1,128)S(1)}, u32[]{:S(2)}, u32[]{:S(2)}) async-start(f32[64,1,128]{2,1,0:T(1,128)} %share.1), calls=%async_computation | async-start | bytes 65536 | tf_op jit(solution)/shard_map/all_to_all | solution.py:728

commit v4 on v2

v4 whole, which is shorter than its diff:
```python
import functools

import jax
import jax.numpy as jnp
import numpy as np
from jax import lax
from jax.experimental import pallas as pl
from jax.experimental.pallas import tpu as pltpu
from jax.sharding import PartitionSpec as P

Q = 19
BLOCK = 8
VELOCITIES = [
    (0, 0, 0),
    (1, 0, 0),
    (-1, 0, 0),
    (0, 1, 0),
    (0, -1, 0),
    (0, 0, 1),
    (0, 0, -1),
    (1, 1, 0),
    (-1, -1, 0),
    (1, -1, 0),
    (-1, 1, 0),
    (1, 0, 1),
    (-1, 0, -1),
    (1, 0, -1),
    (-1, 0, 1),
    (0, 1, 1),
    (0, -1, -1),
    (0, 1, -1),
    (0, -1, 1),
]
W_REST, W_AXIS, W_DIAG = 1.0 / 3.0, 1.0 / 18.0, 1.0 / 36.0
RELAX_RATE = 0.9
SOLID_MAX = 0.5
FACE_WEIGHT = 0.5
ACCEL_SCALE = 400.0
BETA_ONE = 0.9
BETA_TWO = 0.999
LEARN_RATE = 0.2
ADAM_EPS = 1e-08
BIAS_ONE = 1.0 - 0.9**10
BIAS_TWO = 1.0 - 0.999**10

PAIRS = tuple(range(1, Q, 2))
Q_ZERO = [q for q in range(Q) if VELOCITIES[q][0] == 0]
Q_PLUS = [q for q in range(Q) if VELOCITIES[q][0] == 1]
Q_MINUS = [q for q in range(Q) if VELOCITIES[q][0] == -1]
ROW_FAR = Q
ROW_ADJ = ROW_FAR + 2 * len(Q_PLUS)
ROW_ADJ_FAR = ROW_ADJ + len(Q_ZERO) + len(Q_PLUS)
ROW_BLOCKS = ROW_ADJ_FAR + len(Q_PLUS)
ROWS = ROW_BLOCKS + 1
B_ROWS = ROWS + 1
RUN = 16
FORWARD_UNROLL = 2
BACKWARD_UNROLL = 6
GROUP = 8
OFFSET = 5


def shift_yz(value, vel_id, direction):
    _, shift_y, shift_z = VELOCITIES[vel_id]
    if shift_y:
        value = pltpu.roll(value, (direction * shift_y) % 8, 0)
    if shift_z:
        value = pltpu.roll(value, (direction * shift_z) % 128, 1)
    return value


def along(vector, vel_id):
    total = None
    for part, sign in zip(vector, VELOCITIES[vel_id]):
        if sign == 0:
            continue
        if total is None:
            total = part if sign > 0 else -part
        else:
            total = total + part if sign > 0 else total - part
    return total


def weight(pair):
    return W_AXIS if pair < 7 else W_DIAG


def moments(f):
    plus = {p: f[p] + f[p + 1] for p in PAIRS}
    minus = {p: f[p] - f[p + 1] for p in PAIRS}
    density = f[0]
    for p in PAIRS:
        density = density + plus[p]
    momentum = []
    for axis in range(3):
        total = None
        for p in PAIRS:
            sign = VELOCITIES[p][axis]
            if sign == 0:
                continue
            if total is None:
                total = minus[p]
            else:
                total = total + minus[p] if sign > 0 else total - minus[p]
        momentum.append(total)
    return density, momentum, plus, minus


def odd_parts(density, momentum, minus, accel):
    flow = [3.0 * RELAX_RATE * m + (3.0 * a) * density for m, a in zip(momentum, accel)]
    return {
        p: (1.0 - RELAX_RATE) * minus[p] + (2.0 * weight(p)) * along(flow, p) for p in PAIRS
    }


def collide(f, solid, accel):
    density, momentum, plus, minus = moments(f)
    odd = odd_parts(density, momentum, minus, accel)
    inverse = 1.0 / density
    velocity = [m * inverse for m in momentum]
    speed_sq = sum(m * u for m, u in zip(momentum, velocity))
    base = RELAX_RATE * (density - 1.5 * speed_sq)
    gray = {0: (1.0 - RELAX_RATE) * f[0] + W_REST * base}
    bent = 0.5 - solid
    for p in PAIRS:
        project = along(velocity, p)
        even = 0.5 * (1.0 - RELAX_RATE) * plus[p] + weight(p) * (
            base + (4.5 * RELAX_RATE) * density * (project * project)
        )
        turned = bent * odd[p]
        gray[p] = even + turned
        gray[p + 1] = even - turned
    return gray, odd


def collide_adjoint(f_moments, g, solid, accel):
    density, momentum = f_moments
    inverse = 1.0 / density
    velocity = [m * inverse for m in momentum]
    plus = {p: g[p] + g[p + 1] for p in PAIRS}
    fluid = 1.0 - 2.0 * solid
    minus = {p: fluid * (g[p] - g[p + 1]) for p in PAIRS}
    axis_sum = plus[1] + plus[3] + plus[5]
    diag_xy, diag_xz, diag_yz = plus[7] + plus[9], plus[11] + plus[13], plus[15] + plus[17]
    level = W_REST * g[0] + W_AXIS * axis_sum + W_DIAG * (diag_xy + diag_xz + diag_yz)
    second = {
        (0, 0): W_AXIS * plus[1] + W_DIAG * (diag_xy + diag_xz),
        (1, 1): W_AXIS * plus[3] + W_DIAG * (diag_xy + diag_yz),
        (2, 2): W_AXIS * plus[5] + W_DIAG * (diag_xz + diag_yz),
        (0, 1): W_DIAG * (plus[7] - plus[9]),
        (0, 2): W_DIAG * (plus[11] - plus[13]),
        (1, 2): W_DIAG * (plus[15] - plus[17]),
    }
    first = [
        W_AXIS * minus[1] + W_DIAG * (minus[7] + minus[9] + minus[11] + minus[13]),
        W_AXIS * minus[3] + W_DIAG * (minus[7] - minus[9] + minus[15] + minus[17]),
        W_AXIS * minus[5] + W_DIAG * (minus[11] - minus[13] + minus[15] - minus[17]),
    ]
    bent = [
        sum(second[(min(i, j), max(i, j))] * velocity[j] for j in range(3)) for i in range(3)
    ]
    pull = [
        RELAX_RATE * (3.0 * first[i] + 9.0 * bent[i] - (3.0 * level) * velocity[i])
        for i in range(3)
    ]
    speed_sq = sum(u * u for u in velocity)
    rest = RELAX_RATE * (
        level * (1.0 + 1.5 * speed_sq) - 4.5 * sum(b * u for b, u in zip(bent, velocity))
    )
    rest = rest + 3.0 * sum(a * b for a, b in zip(accel, first))
    out = {0: (1.0 - RELAX_RATE) * g[0] + rest}
    for p in PAIRS:
        even = 0.5 * (1.0 - RELAX_RATE) * plus[p] + rest
        odd = 0.5 * (1.0 - RELAX_RATE) * minus[p] + along(pull, p)
        out[p] = even + odd
        out[p + 1] = even - odd
    return out


def sens_terms(g, odd):
    return sum((g[p + 1] - g[p]) * odd[p] for p in PAIRS)


def lanes():
    return lax.broadcasted_iota(jnp.int32, (8, 128), 1)


def read_accel(accel_ref, turn):
    return [accel_ref[turn, axis] for axis in range(3)]


def is_even():
    return lax.axis_index("tile") & 1 == 0


def spread(row, blocks):
    row[...] = jnp.zeros_like(row)
    row[0:1, 0:16] = blocks
    wide = jnp.take_along_axis(row[...], lanes() // BLOCK, axis=1)
    return jnp.broadcast_to(wide[0:1], (8, 128))


def smooth(beside, grid):
    around = beside + 2.0 * grid + pltpu.roll(grid, 8, 1) + pltpu.roll(grid, 120, 1)
    return (grid + FACE_WEIGHT * around) * (1.0 / (1.0 + 6.0 * FACE_WEIGHT))


def read_layer(f_ref, q, x):
    two = f_ref[q, 16 * (x // 2) : 16 * (x // 2) + 16, :].astype(jnp.float32)
    return two[8:16] if x % 2 else two[0:8]


def load_kernel(
    design_hbm,
    mask_hbm,
    accel_hbm,
    first_hbm,
    second_hbm,
    f_hbm,
    adj_hbm,
    blocks_out,
    accel_out,
    design_out,
    mask_out,
    first_out,
    second_out,
    f_out,
    adj_out,
    table,
    sems,
):
    copies = [
        pltpu.make_async_copy(source, target, sems.at[i])
        for i, (source, target) in enumerate(
            (
                (design_hbm, design_out),
                (mask_hbm, mask_out),
                (accel_hbm, table),
                (first_hbm, first_out),
                (second_hbm, second_out),
                (f_hbm, f_out),
                (adj_hbm, adj_out),
            )
        )
    ]
    for copy in copies:
        copy.start()
    for copy in copies[:5]:
        copy.wait()
    blocks_out[...] = design_out[...] * mask_out[...].astype(jnp.float32)
    for turn in range(2):
        for axis in range(3):
            value = table[turn, axis].astype(jnp.float32) * (1.0 / ACCEL_SCALE)
            accel_out[turn, axis] = jnp.full((8, 128), value, jnp.float32)
    for copy in copies[5:]:
        copy.wait()


def pack(f_ref, adj_ref, out, high, blocks, accel):
    near, far = (7, 6) if high else (0, 1)
    back = Q_MINUS if high else Q_PLUS
    post, _ = collide([read_layer(f_ref, q, near) for q in range(Q)], 0.0, accel)
    for q in range(Q):
        out[q] = post[q]
    post, _ = collide([read_layer(f_ref, q, far) for q in range(Q)], 0.0, accel)
    for i, p in enumerate(Q_PLUS):
        out[ROW_FAR + 2 * i] = post[p]
        out[ROW_FAR + 2 * i + 1] = post[p + 1]
    for i, q in enumerate(Q_ZERO + back):
        out[ROW_ADJ + i] = adj_ref[q, near]
    for i, q in enumerate(back):
        out[ROW_ADJ_FAR + i] = adj_ref[q, far]
    out[ROW_BLOCKS] = blocks


def pack_kernel(f_ref, adj_ref, accel_ref, own_ref, to_b, to_a, row):
    accel = read_accel(accel_ref, 0)
    blocks = spread(row, own_ref[...])
    for r in range(ROWS, B_ROWS):
        to_b[r] = jnp.zeros((8, 128), jnp.float32)

    def both(low, high):
        pack(f_ref, adj_ref, low, False, blocks, accel)
        pack(f_ref, adj_ref, high, True, blocks, accel)

    even = is_even()
    pl.when(even)(lambda: both(to_b, to_a))
    pl.when(jnp.logical_not(even))(lambda: both(to_a, to_b))


def boundary(low, message, solid, solid_own, f_next, adj_ref, accel):
    inward, outward = (Q_PLUS, Q_MINUS) if low else (Q_MINUS, Q_PLUS)
    beside, face, layer, behind = (2, 3, 0, 1) if low else (11, 10, 7, 6)
    first = 0 if low else 1

    def mixed(row, q):
        value = message[row]
        if q:
            opposite = message[row + 1 if q % 2 else row - 1]
            value = shift_yz(value + solid * (opposite - value), q, 1)
        return value

    adj = {q: message[ROW_ADJ + i] for i, q in enumerate(Q_ZERO + outward)}
    f = {q: mixed(ROW_FAR + 2 * i + first, q) for i, q in enumerate(inward)}
    f.update({q: mixed(q, q) for q in Q_ZERO})
    f.update({q: f_next[q, beside] for q in outward})
    g = {q: message[ROW_ADJ_FAR + i] for i, q in enumerate(outward)}
    g.update({q: adj[q] for q in Q_ZERO})
    g.update({q: adj_ref[q, layer] for q in inward})
    g = {q: shift_yz(g[q], q, -1) for q in range(Q)}
    density, momentum, _, _ = moments(f)
    adj_beside = collide_adjoint((density, momentum), g, solid, accel)

    f = {q: f_next[q, face] for q in Q_ZERO + outward}
    f.update({q: mixed(q, q) for q in inward})
    g = {q: adj[q] for q in outward}
    g.update({q: adj_ref[q, layer] for q in Q_ZERO})
    g.update({q: adj_ref[q, behind] for q in inward})
    g = {q: shift_yz(g[q], q, -1) for q in range(Q)}
    density, momentum, _, minus = moments(f)
    odd = odd_parts(density, momentum, minus, accel)
    adj_face = collide_adjoint((density, momentum), g, solid_own, accel)
    adj_beside = {q: shift_yz(adj_beside[q], q, -1) for q in outward}
    adj_face = {q: shift_yz(adj_face[q], q, -1) for q in Q_ZERO + outward}
    return adj_beside, adj_face, sens_terms(g, odd)


def boundary_sens(low, adj_beside, adj_face, odd_ref):
    face, behind = (2, 3) if low else (9, 8)
    total = 0.0
    for q in Q_ZERO:
        if q:
            total = total + adj_face[q] * turned(odd_ref, face, q)
    for q in Q_MINUS if low else Q_PLUS:
        total = total + adj_beside[q] * turned(odd_ref, face, q)
        total = total + adj_face[q] * turned(odd_ref, behind, q)
    return total


def sens_kernel(
    accel_ref,
    f_ref,
    adj_ref,
    from_a,
    from_b,
    own_ref,
    within_ref,
    across_ref,
    g_out,
    mom_out,
    solid_out,
    sums_out,
    turned_out,
    f_next,
    odd_ext,
    row,
    past_row,
):
    accel_first = read_accel(accel_ref, 0)
    accel_second = read_accel(accel_ref, 1)
    own = spread(row, own_ref[...])
    solid_own = SOLID_MAX * smooth(from_a[ROW_BLOCKS] + from_b[ROW_BLOCKS], own)
    solid_out[...] = solid_own

    def forward(k, _):
        for half in range(2):
            e = 2 * k + 2 + half
            f = [
                f_ref[q, pl.ds(pl.multiple_of(16 * k, 16), 16), :].astype(jnp.float32)[
                    8 * half : 8 * half + 8
                ]
                for q in range(Q)
            ]
            gray, odd = collide(f, solid_own, accel_first)
            density, momentum, _, _ = moments(f)
            for i, part in enumerate([density] + momentum):
                mom_out[i, e - 2] = part
            for q in range(Q):
                f_next[q, e + 1 + VELOCITIES[q][0]] = shift_yz(gray[q], q, 1)
            for i, p in enumerate(PAIRS):
                odd_ext[i, e] = odd[p]
        return 0

    lax.fori_loop(0, 4, forward, 0, unroll=FORWARD_UNROLL)

    def backward(e, total):
        f = [f_next[q, e + 1] for q in range(Q)]
        g = [shift_yz(adj_ref[q, e - 2 + VELOCITIES[q][0]], q, -1) for q in range(Q)]
        density, momentum, _, minus = moments(f)
        odd = odd_parts(density, momentum, minus, accel_second)
        total = total + sens_terms(g, odd)
        adjoint = collide_adjoint((density, momentum), g, solid_own, accel_second)
        for q in range(Q):
            to = e - VELOCITIES[q][0]
            value = shift_yz(adjoint[q], q, -1)
            g_out[q, to] = value
            if q:
                total = total + value * turned(odd_ext, to, q)
        return total

    total = lax.fori_loop(
        3, 9, backward, jnp.zeros((8, 128), jnp.float32), unroll=BACKWARD_UNROLL
    )
    row[...] = total

    odd_chip = lax.axis_index("tile") & 2 == 2

    def side(low, message):
        outward = Q_MINUS if low else Q_PLUS
        past = jnp.where(odd_chip == low, within_ref[...], across_ref[...])
        solid = SOLID_MAX * smooth(own + spread(past_row, past), message[ROW_BLOCKS])
        adj_beside, adj_face, sens = boundary(
            low, message, solid, solid_own, f_next, adj_ref, accel_second
        )
        face, behind = (2, 3) if low else (9, 8)
        for q in Q_ZERO:
            g_out[q, face] = adj_face[q]
        for q in outward:
            g_out[q, face] = adj_beside[q]
            g_out[q, behind] = adj_face[q]
        row[...] += sens + boundary_sens(low, adj_beside, adj_face, odd_ext)

    def both(low, high):
        side(True, low)
        side(False, high)

    even = is_even()
    pl.when(even)(lambda: both(from_b, from_a))
    pl.when(jnp.logical_not(even))(lambda: both(from_a, from_b))

    total = jnp.broadcast_to(jnp.sum(row[...], axis=0, keepdims=True), (8, 128))
    for step in (1, 2, 4):
        total = total + pltpu.roll(total, 128 - step, 1)
    total = jnp.where(lanes() % BLOCK == 0, total, 0.0)
    sums_out[...] = total[0:1]
    turned_out[...] = pltpu.roll(total, 1, 1)[0:1]


def turned(odd_ref, layer, q):
    return -odd_ref[q // 2, layer] if q % 2 else odd_ref[q // 2 - 1, layer]


def start_kernel(accel_ref, solid_ref, g_ref, mom_ref, out_ref):
    accel = read_accel(accel_ref, 0)
    solid = solid_ref[...]

    def layer(x, _):
        g = [g_ref[q, x + 2] for q in range(Q)]
        momentum = [mom_ref[1 + axis, x] for axis in range(3)]
        adjoint = collide_adjoint((mom_ref[0, x], momentum), g, solid, accel)
        for q in range(Q):
            out_ref[q, x] = adjoint[q]
        return 0

    lax.fori_loop(0, 8, layer, 0)


def share_kernel(sums_ref, outside_ref, out):
    out[...] = jnp.broadcast_to((sums_ref[...] + outside_ref[...])[None], out.shape)


def update_kernel(
    cases,
    sums_ref,
    design_ref,
    mask_ref,
    first_ref,
    second_ref,
    design_out,
    first_out,
    second_out,
):
    place = (lax.axis_index("tile") - OFFSET) & (GROUP - 1)
    totals = []
    for tile in range(GROUP):
        total = sums_ref[tile * cases]
        for case in range(1, cases):
            total = total + sums_ref[tile * cases + case]
        totals.append(jnp.broadcast_to(total, (8, 128)))

    line = [pltpu.roll(totals[0], 127, 1)] + totals + [pltpu.roll(totals[-1], 127, 1)]

    def pick(shift):
        value = line[shift]
        for k in range(1, GROUP):
            value = jnp.where(place == k, line[k + shift], value)
        return value

    gradient = SOLID_MAX * smooth(pick(0) + pick(2), pick(1))
    spots = jnp.minimum(lanes() * BLOCK, 127)
    gradient = jnp.take_along_axis(gradient, spots, axis=1)[0:1, 0:16]
    gradient = mask_ref[...].astype(jnp.float32) * gradient
    first = BETA_ONE * first_ref[...] + (1.0 - BETA_ONE) * gradient
    second = BETA_TWO * second_ref[...] + (1.0 - BETA_TWO) * gradient * gradient
    stepped = design_ref[...] - LEARN_RATE * (first * (1.0 / BIAS_ONE)) / (
        jnp.sqrt(second * (1.0 / BIAS_TWO)) + ADAM_EPS
    )
    design_out[...] = jnp.clip(stepped, 0.0, 1.0)
    first_out[...] = first
    second_out[...] = second


def tables(tiles, cases):
    run = RUN if tiles % RUN == 0 else tiles

    def device(tile, case):
        return (tile % tiles) * cases + case

    def near(tile, step, case):
        target = tile + step
        crossed = (target // run) != (tile // run)
        return device(target, case ^ 1 if crossed else case)

    found = {name: [] for name in ("chip", "beyond", "across", "within", "ends")}
    for tile in range(tiles):
        step = 1 if tile % 2 else -1
        for case in range(cases):
            here = device(tile, case)
            found["chip"].append((here, device(tile ^ 1, case)))
            found["beyond"].append((here, device(tile + step, case)))
            odd_chip = (tile // 2) % 2
            found["across"].append((here, near(tile, 2 if odd_chip else -2, case)))
            found["within"].append((here, near(tile, -2 if odd_chip else 2, case)))
            place = (tile - OFFSET) % GROUP
            if place == 0:
                found["ends"].append((here, device(tile - 1, case)))
            if place == GROUP - 1:
                found["ends"].append((here, device(tile + 1, case)))
    groups = [
        [device(OFFSET + g * GROUP + k, case) for k in range(GROUP) for case in range(cases)]
        for g in range(tiles // GROUP)
    ]
    return found, groups


VMEM_SPEC = pl.BlockSpec(memory_space=pltpu.VMEM)
HBM_SPEC = pl.BlockSpec(memory_space=pltpu.HBM)
F32 = jnp.float32


def body(
    tiles,
    cases,
    checkpoint,
    adjoint_field,
    accel_table,
    design,
    design_mask,
    first_moment,
    second_moment,
):
    axes = ("tile", "case")
    pairs, groups = tables(tiles, cases)
    f_zero = checkpoint.reshape(Q, 64, 128)
    adjoint = adjoint_field[0]
    flat = [a.reshape(1, 16) for a in (design, design_mask, first_moment, second_moment)]
    params = pltpu.CompilerParams(vmem_limit_bytes=32 * 1024 * 1024)

    def send(value, name):
        return lax.ppermute(value, axes, pairs[name])

    def call(kernel, name, out_shape, in_specs, scratch, *args):
        many = isinstance(out_shape, tuple)
        return pl.pallas_call(
            kernel,
            out_shape=out_shape,
            in_specs=in_specs,
            out_specs=[VMEM_SPEC] * len(out_shape) if many else VMEM_SPEC,
            scratch_shapes=scratch,
            compiler_params=params,
            name=name,
        )(*args)

    def shape(*dims):
        return jax.ShapeDtypeStruct(dims, F32)

    row = pltpu.VMEM((8, 128), F32)
    blocks, accel, *kept, f_zero, adjoint = call(
        load_kernel,
        "load",
        (
            shape(1, 16),
            shape(2, 3, 8, 128),
            shape(1, 16),
            jax.ShapeDtypeStruct((1, 16), jnp.int32),
            shape(1, 16),
            shape(1, 16),
            jax.ShapeDtypeStruct((Q, 64, 128), jnp.bfloat16),
            shape(Q, 8, 8, 128),
        ),
        [HBM_SPEC] * 7,
        [pltpu.SMEM((2, 3), jnp.int32), pltpu.SemaphoreType.DMA((7,))],
        *(
            pltpu.with_memory_space_constraint(a, pltpu.HBM)
            for a in (*flat[:2], accel_table[0], *flat[2:], f_zero, adjoint)
        ),
    )
    to_b, to_a = call(
        pack_kernel,
        "pack_faces",
        (shape(B_ROWS, 8, 128), shape(ROWS, 8, 128)),
        [VMEM_SPEC] * 4,
        [row],
        f_zero,
        adjoint,
        accel,
        blocks,
    )
    from_b = send(to_b, "beyond")
    from_a = send(to_a, "chip")
    within = send(blocks, "within")
    across = send(blocks, "across")
    g_one, mom, solid, sums, turned_sums = call(
        sens_kernel,
        "sensitivity",
        (
            shape(Q, 12, 8, 128),
            shape(4, 8, 8, 128),
            shape(8, 128),
            shape(1, 128),
            shape(1, 128),
        ),
        [VMEM_SPEC] * 8,
        [
            pltpu.VMEM((Q, 14, 8, 128), F32),
            pltpu.VMEM((len(PAIRS), 12, 8, 128), F32),
            row,
            row,
        ],
        accel,
        f_zero,
        adjoint,
        from_a,
        from_b,
        blocks,
        within,
        across,
    )
    outside = send(turned_sums, "ends")
    payload = call(
        share_kernel, "share", shape(GROUP * cases, 1, 128), [VMEM_SPEC] * 2, [], sums, outside
    )
    payload, g_one = lax.optimization_barrier((payload, g_one))
    shared = lax.all_to_all(payload, axes, 0, 0, axis_index_groups=groups, tiled=True)
    start = call(
        start_kernel,
        "adjoint_start",
        shape(Q, 8, 8, 128),
        [VMEM_SPEC] * 4,
        [],
        accel,
        solid,
        g_one,
        mom,
    )
    small = shape(1, 16)
    updated = call(
        functools.partial(update_kernel, cases),
        "update",
        (small, small, small),
        [VMEM_SPEC] * 5,
        [],
        shared,
        *kept,
    )
    return (start[None],) + tuple(u.reshape(1, 1, 16) for u in updated)


def solution(mesh):
    placed = (
        P("case", None, "tile", None, None),
        P("case", None, "tile", None, None),
        P("case", None, None),
        P("tile", None, None),
        P("tile", None, None),
        P("tile", None, None),
        P("tile", None, None),
    )
    return jax.shard_map(
        functools.partial(body, mesh.shape["tile"], mesh.shape["case"]),
        mesh=mesh,
        in_specs=placed,
        out_specs=(
            P("case", None, "tile", None, None),
            P("tile", None, None),
            P("tile", None, None),
            P("tile", None, None),
        ),
        check_vma=False,
    )
```

time: 66.1 us -> 60.9 us (0.921)
  waiting for transfers between devices: 11.1 us -> 8.77 us
  starting transfers between devices: 47.2 us -> 45.6 us
  Pallas kernels: 6.75 us -> 5.54 us
    ppermute x5, waiting for transfers between devices: 4.94 us -> 2.36 us  [send(): return lax.ppermute(value, axes, pairs[name])]
    ppermute x5, starting transfers between devices: 30.5 us -> 29.3 us  [send(): return lax.ppermute(value, axes, pairs[name])]
    pallas_call x9 -> x6, Pallas kernels: 6.75 us -> 5.54 us  [call(): pl.pallas_call(kernel, out_shape=out_shape, in_specs=in_specs, out_specs=...]
  transfers between devices with their start and end apart: 6 -> 6, of which waited for: 4 -> 3; matrix products, arithmetic and copies ran while one was open for 0% -> 0% of each run, Pallas kernels for 5% -> 2%
where the time goes in v4:
time: 60.9 us; the launch traced here: 60.6 us
  starting transfers between devices  45.6 us (75%)
  waiting for transfers between devices  8.77 us (14%)
  Pallas kernels  5.54 us (9%)
  between operations  0.7 us (1%)
    ppermute x5, starting transfers between devices, send(): return lax.ppermute(value, axes, pairs[name])  29.3 us
    all_to_all x1, starting transfers between devices, body(): lax.all_to_all(payload, axes, 0, 0, axis_index_groups=groups, tiled=True)  16.3 us
    all_to_all x1, waiting for transfers between devices, body(): lax.all_to_all(payload, axes, 0, 0, axis_index_groups=groups, tiled=True)  6.41 us
    pallas_call x6, Pallas kernels, call(): pl.pallas_call(kernel, out_shape=out_shape, in_specs=in_specs, out_specs=...  5.54 us
    ppermute x5, waiting for transfers between devices, send(): return lax.ppermute(value, axes, pairs[name])  2.36 us
  transfers between devices with their start and end apart: 6, of which 3 were waited for; matrix products, arithmetic and copies ran while one was open for 0% of the time, Pallas kernels for 2%

profile of v4, /device:TPU:1, one launch (start us, length us, event | category | flops | bytes accessed | tf_op | source)
XLA Modules:
  0.0 60.6 jit_solution(1871981109376594827)
XLA Ops:
  0.6 1.3 %load.1 = (f32[1,16]{1,0:T(1,128)S(1)}, f32[2,3,8,128]{3,2,1,0:T(8,128)S(1)}, f32[1,16]{1,0:T(1,128)S(1)}, s32[1,16]{1,0:T(1,128)S(1)}, f32[1,16]{1,0:T(1,128)S(...) custom-call(f32[1,16]{1,0:T(1,128)} %bitcast.15, s32[1,16]{1,0:T(1,128)} %bitcast.16, ...), custom_call_target="tpu_custom_call" | custom-call | tf_op jit(solution)/shard_map/load/pallas_call | solution.py:564
  1.9 0.2 pack_faces.1
  2.2 5.4 %collective-permute-start.1 = (f32[50,8,128]{2,1,0:T(8,128)S(1)}, f32[50,8,128]{2,1,0:T(8,128)S(1)}, u32[]{:S(2)}, u32[]{:S(2)}) collective-permute-start(f32[50,8,128]{2,1,0:T(8,128)S(1)} %get-tuple-element.29), channel_id=1, source_target_pairs={{0,1016},{1,1017},{2,1018},{3,1019},{4,1020},{5,1021},{6,1022},{7,... | collective-permute-start | bytes 614408 | tf_op jit(solution)/shard_map/ppermute | solution.py:560
  7.6 16.7 %collective-permute-start = (f32[49,8,128]{2,1,0:T(8,128)S(1)}, f32[49,8,128]{2,1,0:T(8,128)S(1)}, u32[]{:S(2)}, u32[]{:S(2)}) collective-permute-start(f32[49,8,128]{2,1,0:T(8,128)S(1)} %get-tuple-element.28), channel_id=1, source_target_pairs={{0,8},{1,9},{2,10},{3,11},{4,12},{5,13},{6,14},{7,15},{8,0},{9,1},... | collective-permute-start | bytes 602120 | tf_op jit(solution)/shard_map/ppermute | solution.py:560
  24.3 4.6 %collective-permute-start.3 = (f32[1,16]{1,0:T(1,128)S(1)}, f32[1,16]{1,0:T(1,128)S(1)}, u32[]{:S(2)}, u32[]{:S(2)}) collective-permute-start(f32[1,16]{1,0:T(1,128)S(1)} %get-tuple-element.27.own_ref), channel_id=1, source_target_pairs={{0,1009},{1,1008},{2,1011},{3,1010},{4,1013},{5,1012},{6,1015},{7,... | collective-permute-start | bytes 200 | tf_op jit(solution)/shard_map/ppermute | solution.py:560
  28.9 1.9 %collective-permute-start.2 = (f32[1,16]{1,0:T(1,128)S(1)}, f32[1,16]{1,0:T(1,128)S(1)}, u32[]{:S(2)}, u32[]{:S(2)}) collective-permute-start(f32[1,16]{1,0:T(1,128)S(1)} %get-tuple-element.27.own_ref), channel_id=1, source_target_pairs={{0,16},{1,17},{2,18},{3,19},{4,20},{5,21},{6,22},{7,23},{8,24},{9,... | collective-permute-start | bytes 200 | tf_op jit(solution)/shard_map/ppermute | solution.py:560
  30.8 1.1 %collective-permute-done.3.across_ref = f32[1,16]{1,0:T(1,128)S(1)} collective-permute-done((f32[1,16]{1,0:T(1,128)S(1)}, f32[1,16]{1,0:T(1,128)S(1)}, u32[]{:S(2)}, u32[]{:S(2)}) %collective-permute-start.3) | collective-permute-done | bytes 96 | tf_op jit(solution)/shard_map/ppermute | solution.py:560
  31.9 1.3 %collective-permute-done.2.within_ref = f32[1,16]{1,0:T(1,128)S(1)} collective-permute-done((f32[1,16]{1,0:T(1,128)S(1)}, f32[1,16]{1,0:T(1,128)S(1)}, u32[]{:S(2)}, u32[]{:S(2)}) %collective-permute-start.2) | collective-permute-done | bytes 96 | tf_op jit(solution)/shard_map/ppermute | solution.py:560
  33.2 0.0 collective-permute-done.from_a
  33.2 0.0 collective-permute-done.1.from_b
  33.2 1.5 %sensitivity.1 = (f32[19,12,8,128]{3,2,1,0:T(8,128)S(1)}, f32[4,8,8,128]{3,2,1,0:T(8,128)S(1)}, f32[8,128]{1,0:T(8,128)S(1)}, f32[1,128]{1,0:T(1,128)S(1)}, f32[1,128]{1,0:T(1,128)S(1)}) custom-call(f32[2,3,8,128]{3,2,1,0:T(8,128)S(1)} %get-tuple-element.24.accel_ref, bf16[19,64,128]{2,1,0:T(8,128)(2,1)S(1)} %get-tuple-element.25.f_ref, ...), custom_call_target="tpu_custom_call" | custom-call | tf_op jit(solution)/shard_map/sensitivity/pallas_call | solution.py:564
  34.7 0.7 %collective-permute-start.4 = (f32[1,128]{1,0:T(1,128)S(1)}, f32[1,128]{1,0:T(1,128)S(1)}, u32[]{:S(2)}, u32[]{:S(2)}) collective-permute-start(f32[1,128]{1,0:T(1,128)S(1)} %get-tuple-element.32), channel_id=1, source_target_pairs={{32,40},{33,41},{34,42},{35,43},{36,44},{37,45},{38,46},{39,47},{4... | collective-permute-start | bytes 1544 | tf_op jit(solution)/shard_map/ppermute | solution.py:560
  35.4 0.0 collective-permute-done.4.outside_ref
  35.4 0.6 %share.1 = f32[64,1,128]{2,1,0:T(1,128)} custom-call(f32[1,128]{1,0:T(1,128)S(1)} %get-tuple-element.31.sums_ref, f32[1,128]{1,0:T(1,128)S(1)} %collective-permute-done.4.outside_ref), custom_call_target="tpu_custom_call" | custom-call | tf_op jit(solution)/shard_map/share/pallas_call | solution.py:564
  36.0 16.3 %all-to-all-start = ((f32[64,1,128]{2,1,0:T(1,128)}), f32[64,1,128]{2,1,0:T(1,128)S(1)}, u32[]{:S(2)}, u32[]{:S(2)}) async-start(f32[64,1,128]{2,1,0:T(1,128)} %share.1), calls=%async_computation | async-start | bytes 65536 | tf_op jit(solution)/shard_map/all_to_all | solution.py:644
  52.3 1.1 %adjoint_start.1 = f32[19,8,8,128]{3,2,1,0:T(8,128)} custom-call(f32[2,3,8,128]{3,2,1,0:T(8,128)S(1)} %get-tuple-element.24.accel_ref, f32[8,128]{1,0:T(8,128)S(1)} %get-tuple-element.30.solid_ref, f32[19,12,8,128]{3,2,1,0:T(8,128)S(1)} %get-tuple-element.34.g_ref, f32[4,8,8,128]{3,2,1,0:T(8,128)S(1)} %get-tuple-element.35.mom_ref), custom_call_target="tpu_custom_call" | custom-call | tf_op jit(solution)/shard_map/adjoint_start/pallas_call | solution.py:564
  53.5 6.4 %all-to-all-done.sums_ref = f32[64,1,128]{2,1,0:T(1,128)S(1)} async-done(((f32[64,1,128]{2,1,0:T(1,128)}), f32[64,1,128]{2,1,0:T(1,128)S(1)}, u32[]{:S(2)}, u32[]{:S(2)}) %all-to-all-start) | async-done | bytes 32800 | tf_op jit(solution)/shard_map/all_to_all | solution.py:644
  59.9 0.7 %update.1 = (f32[1,16]{1,0:T(1,128)}, f32[1,16]{1,0:T(1,128)}, f32[1,16]{1,0:T(1,128)}) custom-call(f32[64,1,128]{2,1,0:T(1,128)S(1)} %all-to-all-done.sums_ref, f32[1,16]{1,0:T(1,128)S(1)} %get-tuple-element.37.design_ref, s32[1,16]{1,0:T(1,128)S(1)} %get-tuple-element.38.mask_ref, f32[1,16]{1,0:T(1,128)S(1)} %get-tuple-element.39.first_ref, ...), custom_call_target="tpu_custom_call" | custom-call | tf_op jit(solution)/shard_map/update/pallas_call | solution.py:564
Async XLA Ops:
  2.2 31.0 %collective-permute-start.1 = (f32[50,8,128]{2,1,0:T(8,128)S(1)}, f32[50,8,128]{2,1,0:T(8,128)S(1)}, u32[]{:S(2)}, u32[]{:S(2)}) collective-permute-start(f32[50,8,128]{2,1,0:T(8,128)S(1)} %get-tuple-element.29), channel_id=1, source_target_pairs={{0,1016},{1,1017},{2,1018},{3,1019},{4,1020},{5,1021},{6,1022},{7,... | collective-permute-start | bytes 614408 | tf_op jit(solution)/shard_map/ppermute | solution.py:560
  7.6 25.6 %collective-permute-start = (f32[49,8,128]{2,1,0:T(8,128)S(1)}, f32[49,8,128]{2,1,0:T(8,128)S(1)}, u32[]{:S(2)}, u32[]{:S(2)}) collective-permute-start(f32[49,8,128]{2,1,0:T(8,128)S(1)} %get-tuple-element.28), channel_id=1, source_target_pairs={{0,8},{1,9},{2,10},{3,11},{4,12},{5,13},{6,14},{7,15},{8,0},{9,1},... | collective-permute-start | bytes 602120 | tf_op jit(solution)/shard_map/ppermute | solution.py:560
  24.3 7.6 %collective-permute-start.3 = (f32[1,16]{1,0:T(1,128)S(1)}, f32[1,16]{1,0:T(1,128)S(1)}, u32[]{:S(2)}, u32[]{:S(2)}) collective-permute-start(f32[1,16]{1,0:T(1,128)S(1)} %get-tuple-element.27.own_ref), channel_id=1, source_target_pairs={{0,1009},{1,1008},{2,1011},{3,1010},{4,1013},{5,1012},{6,1015},{7,... | collective-permute-start | bytes 200 | tf_op jit(solution)/shard_map/ppermute | solution.py:560
  28.9 4.3 %collective-permute-start.2 = (f32[1,16]{1,0:T(1,128)S(1)}, f32[1,16]{1,0:T(1,128)S(1)}, u32[]{:S(2)}, u32[]{:S(2)}) collective-permute-start(f32[1,16]{1,0:T(1,128)S(1)} %get-tuple-element.27.own_ref), channel_id=1, source_target_pairs={{0,16},{1,17},{2,18},{3,19},{4,20},{5,21},{6,22},{7,23},{8,24},{9,... | collective-permute-start | bytes 200 | tf_op jit(solution)/shard_map/ppermute | solution.py:560
  34.7 0.7 %collective-permute-start.4 = (f32[1,128]{1,0:T(1,128)S(1)}, f32[1,128]{1,0:T(1,128)S(1)}, u32[]{:S(2)}, u32[]{:S(2)}) collective-permute-start(f32[1,128]{1,0:T(1,128)S(1)} %get-tuple-element.32), channel_id=1, source_target_pairs={{32,40},{33,41},{34,42},{35,43},{36,44},{37,45},{38,46},{39,47},{4... | collective-permute-start | bytes 1544 | tf_op jit(solution)/shard_map/ppermute | solution.py:560
  36.0 23.9 %all-to-all-start = ((f32[64,1,128]{2,1,0:T(1,128)}), f32[64,1,128]{2,1,0:T(1,128)S(1)}, u32[]{:S(2)}, u32[]{:S(2)}) async-start(f32[64,1,128]{2,1,0:T(1,128)} %share.1), calls=%async_computation | async-start | bytes 65536 | tf_op jit(solution)/shard_map/all_to_all | solution.py:644

commit v5 on v4

--- a/solution.py
+++ b/solution.py
@@ -47,17 +47,20 @@
 Q_ZERO = [q for q in range(Q) if VELOCITIES[q][0] == 0]
 Q_PLUS = [q for q in range(Q) if VELOCITIES[q][0] == 1]
 Q_MINUS = [q for q in range(Q) if VELOCITIES[q][0] == -1]
-ROW_FAR = Q
-ROW_ADJ = ROW_FAR + 2 * len(Q_PLUS)
-ROW_ADJ_FAR = ROW_ADJ + len(Q_ZERO) + len(Q_PLUS)
+ROW_MOMENTS = 2 * len(Q_PLUS)
+ROW_TURNED = ROW_MOMENTS + 4
+ROW_LEVEL = ROW_TURNED + 9
+ROW_ADJ = ROW_LEVEL + 6
+ROW_ADJ_FAR = ROW_ADJ + len(Q_PLUS)
 ROW_BLOCKS = ROW_ADJ_FAR + len(Q_PLUS)
 ROWS = ROW_BLOCKS + 1
 B_ROWS = ROWS + 1
+Z_MOTIONS = (0, 1, -1)
 RUN = 16
 FORWARD_UNROLL = 2
 BACKWARD_UNROLL = 6
 GROUP = 8
-OFFSET = 5
+OFFSET = 7
 
 
 def shift_yz(value, vel_id, direction):
@@ -67,6 +70,12 @@
     if shift_z:
         value = pltpu.roll(value, (direction * shift_z) % 128, 1)
     return value
+
+
+def add_signed(total, value, sign):
+    if sign == 0:
+        return total
+    return total + value if sign > 0 else total - value
 
 
 def along(vector, vel_id):
@@ -133,29 +142,10 @@
     return gray, odd
 
 
-def collide_adjoint(f_moments, g, solid, accel):
+def adjoint_parts(f_moments, level, first, second, accel):
     density, momentum = f_moments
     inverse = 1.0 / density
     velocity = [m * inverse for m in momentum]
-    plus = {p: g[p] + g[p + 1] for p in PAIRS}
-    fluid = 1.0 - 2.0 * solid
-    minus = {p: fluid * (g[p] - g[p + 1]) for p in PAIRS}
-    axis_sum = plus[1] + plus[3] + plus[5]
-    diag_xy, diag_xz, diag_yz = plus[7] + plus[9], plus[11] + plus[13], plus[15] + plus[17]
-    level = W_REST * g[0] + W_AXIS * axis_sum + W_DIAG * (diag_xy + diag_xz + diag_yz)
-    second = {
-        (0, 0): W_AXIS * plus[1] + W_DIAG * (diag_xy + diag_xz),
-        (1, 1): W_AXIS * plus[3] + W_DIAG * (diag_xy + diag_yz),
-        (2, 2): W_AXIS * plus[5] + W_DIAG * (diag_xz + diag_yz),
-        (0, 1): W_DIAG * (plus[7] - plus[9]),
-        (0, 2): W_DIAG * (plus[11] - plus[13]),
-        (1, 2): W_DIAG * (plus[15] - plus[17]),
-    }
-    first = [
-        W_AXIS * minus[1] + W_DIAG * (minus[7] + minus[9] + minus[11] + minus[13]),
-        W_AXIS * minus[3] + W_DIAG * (minus[7] - minus[9] + minus[15] + minus[17]),
-        W_AXIS * minus[5] + W_DIAG * (minus[11] - minus[13] + minus[15] - minus[17]),
-    ]
     bent = [
         sum(second[(min(i, j), max(i, j))] * velocity[j] for j in range(3)) for i in range(3)
     ]
@@ -167,13 +157,60 @@
     rest = RELAX_RATE * (
         level * (1.0 + 1.5 * speed_sq) - 4.5 * sum(b * u for b, u in zip(bent, velocity))
     )
-    rest = rest + 3.0 * sum(a * b for a, b in zip(accel, first))
+    return rest + 3.0 * sum(a * b for a, b in zip(accel, first)), pull
+
+
+def pair_adjoint(plus, minus, rest, pull, pair):
+    even = 0.5 * (1.0 - RELAX_RATE) * plus + rest
+    odd = 0.5 * (1.0 - RELAX_RATE) * minus + along(pull, pair)
+    return even + odd, even - odd
+
+
+def still_sums(plus, minus, rest):
+    diag = W_DIAG * (plus[15] + plus[17])
+    axis_y, axis_z = W_AXIS * plus[3], W_AXIS * plus[5]
+    return (
+        W_REST * rest + axis_y + axis_z + diag,
+        axis_y + diag,
+        axis_z + diag,
+        W_DIAG * (plus[15] - plus[17]),
+        W_AXIS * minus[3] + W_DIAG * (minus[15] + minus[17]),
+        W_AXIS * minus[5] + W_DIAG * (minus[15] - minus[17]),
+    )
+
+
+def all_sums(still, plus, minus, fluid):
+    level, yy, zz, yz, y, z = still
+    diag_xy, diag_xz = W_DIAG * (plus[7] + plus[9]), W_DIAG * (plus[11] + plus[13])
+    axis_x = W_AXIS * plus[1]
+    second = {
+        (0, 0): axis_x + diag_xy + diag_xz,
+        (1, 1): yy + diag_xy,
+        (2, 2): zz + diag_xz,
+        (0, 1): W_DIAG * (plus[7] - plus[9]),
+        (0, 2): W_DIAG * (plus[11] - plus[13]),
+        (1, 2): yz,
+    }
+    first = [
+        fluid * (W_AXIS * minus[1] + W_DIAG * (minus[7] + minus[9] + minus[11] + minus[13])),
+        fluid * (y + W_DIAG * (minus[7] - minus[9])),
+        fluid * (z + W_DIAG * (minus[11] - minus[13])),
+    ]
+    return level + axis_x + diag_xy + diag_xz, first, second
+
+
+def pair_sums(g, pairs):
+    return {p: g[p] + g[p + 1] for p in pairs}, {p: g[p] - g[p + 1] for p in pairs}
+
+
+def collide_adjoint(f_moments, g, solid, accel):
+    plus, minus = pair_sums(g, PAIRS)
+    fluid = 1.0 - 2.0 * solid
+    sums = all_sums(still_sums(plus, minus, g[0]), plus, minus, fluid)
+    rest, pull = adjoint_parts(f_moments, *sums, accel)
     out = {0: (1.0 - RELAX_RATE) * g[0] + rest}
     for p in PAIRS:
-        even = 0.5 * (1.0 - RELAX_RATE) * plus[p] + rest
-        odd = 0.5 * (1.0 - RELAX_RATE) * minus[p] + along(pull, p)
-        out[p] = even + odd
-        out[p + 1] = even - odd
+        out[p], out[p + 1] = pair_adjoint(plus[p], fluid * minus[p], rest, pull, p)
     return out
 
 
@@ -258,18 +295,39 @@
 
 def pack(f_ref, adj_ref, out, high, blocks, accel):
     near, far = (7, 6) if high else (0, 1)
-    back = Q_MINUS if high else Q_PLUS
+    onward, back = (Q_PLUS, Q_MINUS) if high else (Q_MINUS, Q_PLUS)
     post, _ = collide([read_layer(f_ref, q, near) for q in range(Q)], 0.0, accel)
-    for q in range(Q):
-        out[q] = post[q]
-    post, _ = collide([read_layer(f_ref, q, far) for q in range(Q)], 0.0, accel)
+    behind, _ = collide([read_layer(f_ref, q, far) for q in range(Q)], 0.0, accel)
     for i, p in enumerate(Q_PLUS):
-        out[ROW_FAR + 2 * i] = post[p]
-        out[ROW_FAR + 2 * i + 1] = post[p + 1]
-    for i, q in enumerate(Q_ZERO + back):
-        out[ROW_ADJ + i] = adj_ref[q, near]
+        out[2 * i] = post[p]
+        out[2 * i + 1] = post[p + 1]
+    total = [0.0] * 4
+    turned_away = {motion: [0.0] * 3 for motion in Z_MOTIONS}
+    for q in Q_ZERO + onward:
+        layer = behind if q in onward else post
+        value = shift_yz(layer[q], q, 1)
+        total = [
+            add_signed(kept, value, sign) for kept, sign in zip(total, (1,) + VELOCITIES[q])
+        ]
+        if q:
+            value = shift_yz(layer[q] - layer[q + 1 if q % 2 else q - 1], q, 1)
+            group = turned_away[VELOCITIES[q][2]]
+            signs = (1,) + VELOCITIES[q][:2]
+            turned_away[VELOCITIES[q][2]] = [
+                add_signed(kept, value, sign) for kept, sign in zip(group, signs)
+            ]
+    for i in range(4):
+        out[ROW_MOMENTS + i] = total[i]
+    for k, motion in enumerate(Z_MOTIONS):
+        for i in range(3):
+            out[ROW_TURNED + 3 * k + i] = turned_away[motion][i]
+    g = {q: shift_yz(adj_ref[q, near], q, -1) for q in Q_ZERO + back}
+    plus, minus = pair_sums(g, [p for p in PAIRS if p in Q_ZERO])
+    for i, value in enumerate(still_sums(plus, minus, g[0])):
+        out[ROW_LEVEL + i] = value
     for i, q in enumerate(back):
-        out[ROW_ADJ_FAR + i] = adj_ref[q, far]
+        out[ROW_ADJ + i] = g[q]
+        out[ROW_ADJ_FAR + i] = shift_yz(adj_ref[q, far], q, -1)
     out[ROW_BLOCKS] = blocks
 
 
@@ -293,34 +351,36 @@
     beside, face, layer, behind = (2, 3, 0, 1) if low else (11, 10, 7, 6)
     first = 0 if low else 1
 
-    def mixed(row, q):
-        value = message[row]
-        if q:
-            opposite = message[row + 1 if q % 2 else row - 1]
-            value = shift_yz(value + solid * (opposite - value), q, 1)
-        return value
-
-    adj = {q: message[ROW_ADJ + i] for i, q in enumerate(Q_ZERO + outward)}
-    f = {q: mixed(ROW_FAR + 2 * i + first, q) for i, q in enumerate(inward)}
-    f.update({q: mixed(q, q) for q in Q_ZERO})
-    f.update({q: f_next[q, beside] for q in outward})
+    part = [message[ROW_MOMENTS + i] for i in range(4)]
+    for k, motion in enumerate(Z_MOTIONS):
+        moved = pltpu.roll(solid, motion % 128, 1) if motion else solid
+        away = [moved * message[ROW_TURNED + 3 * k + i] for i in range(3)]
+        part = [a - b for a, b in zip(part, away)] + [add_signed(part[3], away[0], -motion)]
+    for q in outward:
+        value = f_next[q, beside]
+        part = [add_signed(kept, value, sign) for kept, sign in zip(part, (1,) + VELOCITIES[q])]
     g = {q: message[ROW_ADJ_FAR + i] for i, q in enumerate(outward)}
-    g.update({q: adj[q] for q in Q_ZERO})
-    g.update({q: adj_ref[q, layer] for q in inward})
-    g = {q: shift_yz(g[q], q, -1) for q in range(Q)}
-    density, momentum, _, _ = moments(f)
-    adj_beside = collide_adjoint((density, momentum), g, solid, accel)
+    g.update({q: shift_yz(adj_ref[q, layer], q, -1) for q in inward})
+    plus, minus = pair_sums(g, Q_PLUS)
+    fluid = 1.0 - 2.0 * solid
+    still = [message[ROW_LEVEL + i] for i in range(6)]
+    rest, pull = adjoint_parts((part[0], part[1:]), *all_sums(still, plus, minus, fluid), accel)
+    adj_beside = {}
+    for p in Q_PLUS:
+        both = pair_adjoint(plus[p], fluid * minus[p], rest, pull, p)
+        q = p + 1 if low else p
+        adj_beside[q] = shift_yz(both[q - p], q, -1)
 
     f = {q: f_next[q, face] for q in Q_ZERO + outward}
-    f.update({q: mixed(q, q) for q in inward})
-    g = {q: adj[q] for q in outward}
-    g.update({q: adj_ref[q, layer] for q in Q_ZERO})
-    g.update({q: adj_ref[q, behind] for q in inward})
-    g = {q: shift_yz(g[q], q, -1) for q in range(Q)}
+    for i, q in enumerate(inward):
+        value, opposite = message[2 * i + first], message[2 * i + 1 - first]
+        f[q] = shift_yz(value + solid * (opposite - value), q, 1)
+    g = {q: message[ROW_ADJ + i] for i, q in enumerate(outward)}
+    g.update({q: shift_yz(adj_ref[q, layer], q, -1) for q in Q_ZERO})
+    g.update({q: shift_yz(adj_ref[q, behind], q, -1) for q in inward})
     density, momentum, _, minus = moments(f)
     odd = odd_parts(density, momentum, minus, accel)
     adj_face = collide_adjoint((density, momentum), g, solid_own, accel)
-    adj_beside = {q: shift_yz(adj_beside[q], q, -1) for q in outward}
     adj_face = {q: shift_yz(adj_face[q], q, -1) for q in Q_ZERO + outward}
     return adj_beside, adj_face, sens_terms(g, odd)
 
@@ -337,24 +397,20 @@
     return total
 
 
-def sens_kernel(
+def interior_kernel(
     accel_ref,
     f_ref,
     adj_ref,
     from_a,
     from_b,
     own_ref,
-    within_ref,
-    across_ref,
     g_out,
+    f_next,
+    odd_ext,
     mom_out,
     solid_out,
-    sums_out,
-    turned_out,
-    f_next,
-    odd_ext,
+    total_out,
     row,
-    past_row,
 ):
     accel_first = read_accel(accel_ref, 0)
     accel_second = read_accel(accel_ref, 1)
@@ -398,11 +454,32 @@
                 total = total + value * turned(odd_ext, to, q)
         return total
 
-    total = lax.fori_loop(
+    total_out[...] = lax.fori_loop(
         3, 9, backward, jnp.zeros((8, 128), jnp.float32), unroll=BACKWARD_UNROLL
     )
-    row[...] = total
-
+
+
+def sides_kernel(
+    accel_ref,
+    adj_ref,
+    from_a,
+    from_b,
+    own_ref,
+    solid_ref,
+    f_next,
+    odd_ext,
+    total_ref,
+    across_ref,
+    within_ref,
+    low_out,
+    high_out,
+    sums_out,
+    row,
+    past_row,
+):
+    accel_second = read_accel(accel_ref, 1)
+    own = spread(row, own_ref[...])
+    row[...] = total_ref[...]
     odd_chip = lax.axis_index("tile") & 2 == 2
 
     def side(low, message):
@@ -410,14 +487,14 @@
         past = jnp.where(odd_chip == low, within_ref[...], across_ref[...])
         solid = SOLID_MAX * smooth(own + spread(past_row, past), message[ROW_BLOCKS])
         adj_beside, adj_face, sens = boundary(
-            low, message, solid, solid_own, f_next, adj_ref, accel_second
+            low, message, solid, solid_ref[...], f_next, adj_ref, accel_second
         )
-        face, behind = (2, 3) if low else (9, 8)
-        for q in Q_ZERO:
-            g_out[q, face] = adj_face[q]
-        for q in outward:
-            g_out[q, face] = adj_beside[q]
-            g_out[q, behind] = adj_face[q]
+        out = low_out if low else high_out
+        for i, q in enumerate(Q_ZERO):
+            out[i] = adj_face[q]
+        for i, q in enumerate(outward):
+            out[len(Q_ZERO) + i] = adj_beside[q]
+            out[len(Q_ZERO) + len(outward) + i] = adj_face[q]
         row[...] += sens + boundary_sens(low, adj_beside, adj_face, odd_ext)
 
     def both(low, high):
@@ -432,36 +509,61 @@
     for step in (1, 2, 4):
         total = total + pltpu.roll(total, 128 - step, 1)
     total = jnp.where(lanes() % BLOCK == 0, total, 0.0)
-    sums_out[...] = total[0:1]
-    turned_out[...] = pltpu.roll(total, 1, 1)[0:1]
+    sums_out[...] = jnp.broadcast_to(total[0:1][None], sums_out.shape)
 
 
 def turned(odd_ref, layer, q):
     return -odd_ref[q // 2, layer] if q % 2 else odd_ref[q // 2 - 1, layer]
 
 
-def start_kernel(accel_ref, solid_ref, g_ref, mom_ref, out_ref):
+def start_kernel(accel_ref, solid_ref, g_ref, mom_ref, low_ref, high_ref, out_ref):
     accel = read_accel(accel_ref, 0)
     solid = solid_ref[...]
 
-    def layer(x, _):
-        g = [g_ref[q, x + 2] for q in range(Q)]
+    def layer(x, changed):
+        g = {q: g_ref[q, x + 2] for q in range(Q)}
+        g.update(changed)
         momentum = [mom_ref[1 + axis, x] for axis in range(3)]
         adjoint = collide_adjoint((mom_ref[0, x], momentum), g, solid, accel)
         for q in range(Q):
             out_ref[q, x] = adjoint[q]
+
+    def inner(x, _):
+        layer(x, {})
         return 0
 
-    lax.fori_loop(0, 8, layer, 0)
-
-
-def share_kernel(sums_ref, outside_ref, out):
-    out[...] = jnp.broadcast_to((sums_ref[...] + outside_ref[...])[None], out.shape)
+    lax.fori_loop(2, 6, inner, 0)
+    for side, face, behind, outward in ((low_ref, 0, 1, Q_MINUS), (high_ref, 7, 6, Q_PLUS)):
+        layer(face, {q: side[i] for i, q in enumerate(Q_ZERO + outward)})
+        first = len(Q_ZERO) + len(outward)
+        layer(behind, {q: side[first + i] for i, q in enumerate(outward)})
+
+
+def group_order(cases):
+    places = tuple(range(1, GROUP)) + (0,)
+    listed = [(place, case) for half in (0, 1) for place in places for case in range(half, cases, 2)]
+    listed.remove((0, 0))
+    return [(0, 0)] + listed
+
+
+def place_in_group():
+    return (lax.axis_index("tile") - OFFSET) & (GROUP - 1)
+
+
+def tile_total(sums_ref, cases, tile):
+    ranks = [rank for rank, (place, _) in enumerate(group_order(cases)) if place == tile]
+    return sum(sums_ref[rank] for rank in ranks)
+
+
+def end_kernel(cases, sums_ref, out):
+    first, last = tile_total(sums_ref, cases, 0), tile_total(sums_ref, cases, GROUP - 1)
+    out[...] = jnp.where(place_in_group() == 0, first, last)
 
 
 def update_kernel(
     cases,
     sums_ref,
+    outside_ref,
     design_ref,
     mask_ref,
     first_ref,
@@ -470,15 +572,10 @@
     first_out,
     second_out,
 ):
-    place = (lax.axis_index("tile") - OFFSET) & (GROUP - 1)
-    totals = []
-    for tile in range(GROUP):
-        total = sums_ref[tile * cases]
-        for case in range(1, cases):
-            total = total + sums_ref[tile * cases + case]
-        totals.append(jnp.broadcast_to(total, (8, 128)))
-
-    line = [pltpu.roll(totals[0], 127, 1)] + totals + [pltpu.roll(totals[-1], 127, 1)]
+    place = place_in_group()
+    totals = [tile_total(sums_ref, cases, tile) for tile in range(GROUP)]
+    line = [outside_ref[...]] + totals + [outside_ref[...]]
+    line = [jnp.broadcast_to(row, (8, 128)) for row in line]
 
     def pick(shift):
         value = line[shift]
@@ -527,7 +624,7 @@
             if place == GROUP - 1:
                 found["ends"].append((here, device(tile + 1, case)))
     groups = [
-        [device(OFFSET + g * GROUP + k, case) for k in range(GROUP) for case in range(cases)]
+        [device(OFFSET + g * GROUP + place, case) for place, case in group_order(cases)]
         for g in range(tiles // GROUP)
     ]
     return found, groups
@@ -610,57 +707,79 @@
     from_a = send(to_a, "chip")
     within = send(blocks, "within")
     across = send(blocks, "across")
-    g_one, mom, solid, sums, turned_sums = call(
-        sens_kernel,
-        "sensitivity",
+    g_one, f_next, odd, mom, solid, total = call(
+        interior_kernel,
+        "interior",
         (
             shape(Q, 12, 8, 128),
+            shape(Q, 14, 8, 128),
+            shape(len(PAIRS), 12, 8, 128),
             shape(4, 8, 8, 128),
             shape(8, 128),
-            shape(1, 128),
-            shape(1, 128),
+            shape(8, 128),
         ),
-        [VMEM_SPEC] * 8,
-        [
-            pltpu.VMEM((Q, 14, 8, 128), F32),
-            pltpu.VMEM((len(PAIRS), 12, 8, 128), F32),
-            row,
-            row,
-        ],
+        [VMEM_SPEC] * 6,
+        [row],
         accel,
         f_zero,
         adjoint,
         from_a,
         from_b,
         blocks,
+    )
+    face = shape(len(Q_ZERO) + 2 * len(Q_PLUS), 8, 128)
+    low, high, sums = call(
+        sides_kernel,
+        "sides",
+        (face, face, shape(GROUP * cases, 1, 128)),
+        [VMEM_SPEC] * 11,
+        [row, row],
+        accel,
+        adjoint,
+        from_a,
+        from_b,
+        blocks,
+        solid,
+        f_next,
+        odd,
+        total,
+        across,
         within,
-        across,
-    )
-    outside = send(turned_sums, "ends")
-    payload = call(
-        share_kernel, "share", shape(GROUP * cases, 1, 128), [VMEM_SPEC] * 2, [], sums, outside
-    )
-    payload, g_one = lax.optimization_barrier((payload, g_one))
-    shared = lax.all_to_all(payload, axes, 0, 0, axis_index_groups=groups, tiled=True)
+    )
+    sums, low = lax.optimization_barrier((sums, low))
+    shared = lax.all_to_all(sums, axes, 0, 0, axis_index_groups=groups, tiled=True)
     start = call(
         start_kernel,
         "adjoint_start",
         shape(Q, 8, 8, 128),
-        [VMEM_SPEC] * 4,
+        [VMEM_SPEC] * 6,
         [],
         accel,
         solid,
         g_one,
         mom,
-    )
+        low,
+        high,
+    )
+    ends = call(
+        functools.partial(end_kernel, cases),
+        "group_end",
+        shape(1, 128),
+        [VMEM_SPEC],
+        [],
+        shared,
+    )
+    ends, start = lax.optimization_barrier((ends, start))
+    outside = send(ends, "ends")
     small = shape(1, 16)
     updated = call(
         functools.partial(update_kernel, cases),
         "update",
         (small, small, small),
-        [VMEM_SPEC] * 5,
+        [VMEM_SPEC] * 6,
         [],
         shared,
+        outside,
         *kept,
     )
     return (start[None],) + tuple(u.reshape(1, 1, 16) for u in updated)

time: 60.9 us -> 60.1 us (0.987)
  waiting for transfers between devices: 8.77 us -> 6.96 us
  starting transfers between devices: 45.6 us -> 46.5 us
    ppermute x5, waiting for transfers between devices: 2.36 us -> 1.41 us  [send(): return lax.ppermute(value, axes, pairs[name])]
    all_to_all x1, starting transfers between devices: 16.3 us -> 17.2 us  [body(): lax.all_to_all(sums, axes, 0, 0, axis_index_groups=groups, tiled=True)]
    all_to_all x1, waiting for transfers between devices: 6.41 us -> 5.55 us  [body(): lax.all_to_all(sums, axes, 0, 0, axis_index_groups=groups, tiled=True)]
    pallas_call x6 -> x7, Pallas kernels: 5.54 us -> 5.58 us  [call(): pl.pallas_call(kernel, out_shape=out_shape, in_specs=in_specs, out_specs=...]
  transfers between devices with their start and end apart: 6 -> 6, of which waited for: 3 -> 3; matrix products, arithmetic and copies ran while one was open for 0% -> 0% of each run, Pallas kernels for 2% -> 3%
where the time goes in v5:
time: 60.1 us; the launch traced here: 59.8 us
  starting transfers between devices  46.5 us (77%)
  waiting for transfers between devices  6.96 us (12%)
  Pallas kernels  5.58 us (9%)
  between operations  0.73 us (1%)
    ppermute x5, starting transfers between devices, send(): return lax.ppermute(value, axes, pairs[name])  29.3 us
    all_to_all x1, starting transfers between devices, body(): lax.all_to_all(sums, axes, 0, 0, axis_index_groups=groups, tiled=True)  17.2 us
    pallas_call x7, Pallas kernels, call(): pl.pallas_call(kernel, out_shape=out_shape, in_specs=in_specs, out_specs=...  5.58 us
    all_to_all x1, waiting for transfers between devices, body(): lax.all_to_all(sums, axes, 0, 0, axis_index_groups=groups, tiled=True)  5.55 us
    ppermute x5, waiting for transfers between devices, send(): return lax.ppermute(value, axes, pairs[name])  1.41 us
  transfers between devices with their start and end apart: 6, of which 3 were waited for; matrix products, arithmetic and copies ran while one was open for 0% of the time, Pallas kernels for 3%

profile of v5, /device:TPU:1, one launch (start us, length us, event | category | flops | bytes accessed | tf_op | source)
XLA Modules:
  0.0 59.8 jit_solution(8670130802083783352)
XLA Ops:
  0.6 1.3 %load.1 = (f32[1,16]{1,0:T(1,128)S(1)}, f32[2,3,8,128]{3,2,1,0:T(8,128)S(1)}, f32[1,16]{1,0:T(1,128)S(1)}, s32[1,16]{1,0:T(1,128)S(1)}, f32[1,16]{1,0:T(1,128)S(...) custom-call(f32[1,16]{1,0:T(1,128)} %bitcast.15, s32[1,16]{1,0:T(1,128)} %bitcast.16, ...), custom_call_target="tpu_custom_call" | custom-call | tf_op jit(solution)/shard_map/load/pallas_call | solution.py:661
  1.9 0.3 pack_faces.1
  2.2 5.4 %collective-permute-start.1 = (f32[41,8,128]{2,1,0:T(8,128)S(1)}, f32[41,8,128]{2,1,0:T(8,128)S(1)}, u32[]{:S(2)}, u32[]{:S(2)}) collective-permute-start(f32[41,8,128]{2,1,0:T(8,128)S(1)} %get-tuple-element.35), channel_id=1, source_target_pairs={{0,1016},{1,1017},{2,1018},{3,1019},{4,1020},{5,1021},{6,1022},{7,... | collective-permute-start | bytes 503816 | tf_op jit(solution)/shard_map/ppermute | solution.py:657
  7.6 16.7 %collective-permute-start = (f32[40,8,128]{2,1,0:T(8,128)S(1)}, f32[40,8,128]{2,1,0:T(8,128)S(1)}, u32[]{:S(2)}, u32[]{:S(2)}) collective-permute-start(f32[40,8,128]{2,1,0:T(8,128)S(1)} %get-tuple-element.34), channel_id=1, source_target_pairs={{0,8},{1,9},{2,10},{3,11},{4,12},{5,13},{6,14},{7,15},{8,0},{9,1},... | collective-permute-start | bytes 491528 | tf_op jit(solution)/shard_map/ppermute | solution.py:657
  24.3 4.6 %collective-permute-start.2 = (f32[1,16]{1,0:T(1,128)S(1)}, f32[1,16]{1,0:T(1,128)S(1)}, u32[]{:S(2)}, u32[]{:S(2)}) collective-permute-start(f32[1,16]{1,0:T(1,128)S(1)} %get-tuple-element.33.own_ref), channel_id=1, source_target_pairs={{0,1009},{1,1008},{2,1011},{3,1010},{4,1013},{5,1012},{6,1015},{7,... | collective-permute-start | bytes 200 | tf_op jit(solution)/shard_map/ppermute | solution.py:657
  28.9 1.9 %collective-permute-start.3 = (f32[1,16]{1,0:T(1,128)S(1)}, f32[1,16]{1,0:T(1,128)S(1)}, u32[]{:S(2)}, u32[]{:S(2)}) collective-permute-start(f32[1,16]{1,0:T(1,128)S(1)} %get-tuple-element.33.own_ref), channel_id=1, source_target_pairs={{0,16},{1,17},{2,18},{3,19},{4,20},{5,21},{6,22},{7,23},{8,24},{9,... | collective-permute-start | bytes 200 | tf_op jit(solution)/shard_map/ppermute | solution.py:657
  30.9 0.0 collective-permute-done.from_a
  30.9 0.0 collective-permute-done.1.from_b
  30.9 0.9 %interior.1 = (f32[19,12,8,128]{3,2,1,0:T(8,128)S(1)}, f32[19,14,8,128]{3,2,1,0:T(8,128)S(1)}, f32[9,12,8,128]{3,2,1,0:T(8,128)S(1)}, f32[4,8,8,128]{3,2,1,0:T(8...) custom-call(f32[2,3,8,128]{3,2,1,0:T(8,128)S(1)} %get-tuple-element.30.accel_ref, ...), custom_call_target="tpu_custom_call" | custom-call | tf_op jit(solution)/shard_map/interior/pallas_call | solution.py:661
  31.8 0.1 collective-permute-done.2.across_ref
  31.9 1.3 %collective-permute-done.3.within_ref = f32[1,16]{1,0:T(1,128)S(1)} collective-permute-done((f32[1,16]{1,0:T(1,128)S(1)}, f32[1,16]{1,0:T(1,128)S(1)}, u32[]{:S(2)}, u32[]{:S(2)}) %collective-permute-start.3) | collective-permute-done | bytes 96 | tf_op jit(solution)/shard_map/ppermute | solution.py:657
  33.2 1.2 %sides.1 = (f32[19,8,128]{2,1,0:T(8,128)S(1)}, f32[19,8,128]{2,1,0:T(8,128)S(1)}, f32[64,1,128]{2,1,0:T(1,128)}) custom-call(f32[2,3,8,128]{3,2,1,0:T(8,128)S(1)} %get-tuple-element.30.accel_ref, f32[19,8,8,128]{3,2,1,0:T(8,128)S(1)} %get-tuple-element.31.adj_ref, f32[40,8,128]{2,1,0:T(8,128)S(1)} %collective-permute-done.from_a, ...), custom_call_target="tpu_custom_call" | custom-call | tf_op jit(solution)/shard_map/sides/pallas_call | solution.py:661
  34.5 17.2 %all-to-all-start = ((f32[64,1,128]{2,1,0:T(1,128)}), f32[64,1,128]{2,1,0:T(1,128)S(1)}, u32[]{:S(2)}, u32[]{:S(2)}) async-start(f32[64,1,128]{2,1,0:T(1,128)} %get-tuple-element.42), calls=%async_computation | async-start | bytes 65536 | tf_op jit(solution)/shard_map/all_to_all | solution.py:750
  51.7 1.1 %adjoint_start.1 = f32[19,8,8,128]{3,2,1,0:T(8,128)} custom-call(f32[2,3,8,128]{3,2,1,0:T(8,128)S(1)} %get-tuple-element.30.accel_ref, f32[8,128]{1,0:T(8,128)S(1)} %get-tuple-element.36.solid_ref, f32[19,12,8,128]{3,2,1,0:T(8,128)S(1)} %get-tuple-element.43.g_ref, f32[4,8,8,128]{3,2,1,0:T(8,128)S(1)} %get-tuple-element.44.mom_ref, ...), custom_call_target="tpu_custom_call" | custom-call | tf_op jit(solution)/shard_map/adjoint_start/pallas_call | solution.py:661
  52.8 5.5 %all-to-all-done.sums_ref = f32[64,1,128]{2,1,0:T(1,128)S(1)} async-done(((f32[64,1,128]{2,1,0:T(1,128)}), f32[64,1,128]{2,1,0:T(1,128)S(1)}, u32[]{:S(2)}, u32[]{:S(2)}) %all-to-all-start) | async-done | bytes 32800 | tf_op jit(solution)/shard_map/all_to_all | solution.py:750
  58.4 0.7 %collective-permute-start.4 = (f32[1,128]{1,0:T(1,128)S(1)}, f32[1,128]{1,0:T(1,128)S(1)}, u32[]{:S(2)}, u32[]{:S(2)}) collective-permute-start(f32[1,128]{1,0:T(1,128)S(1)} %group_end.1), channel_id=1, source_target_pairs={{48,56},{49,57},{50,58},{51,59},{52,60},{53,61},{54,62},{55,63},{5... | collective-permute-start | bytes 1544 | tf_op jit(solution)/shard_map/ppermute | solution.py:657
  59.1 0.0 collective-permute-done.4.outside_ref
  59.1 0.7 %update.1 = (f32[1,16]{1,0:T(1,128)}, f32[1,16]{1,0:T(1,128)}, f32[1,16]{1,0:T(1,128)}) custom-call(f32[64,1,128]{2,1,0:T(1,128)S(1)} %all-to-all-done.sums_ref, f32[1,128]{1,0:T(1,128)S(1)} %collective-permute-done.4.outside_ref, f32[1,16]{1,0:T(1,128)S(1)} %get-tuple-element.49.design_ref, s32[1,16]{1,0:T(1,128)S(1)} %get-tuple-element.50.mask_ref, ...), custom_call_target="tpu_custom_call" | custom-call | tf_op jit(solution)/shard_map/update/pallas_call | solution.py:661
  (1 shorter events, 0.0 us)
Async XLA Ops:
  2.2 28.7 %collective-permute-start.1 = (f32[41,8,128]{2,1,0:T(8,128)S(1)}, f32[41,8,128]{2,1,0:T(8,128)S(1)}, u32[]{:S(2)}, u32[]{:S(2)}) collective-permute-start(f32[41,8,128]{2,1,0:T(8,128)S(1)} %get-tuple-element.35), channel_id=1, source_target_pairs={{0,1016},{1,1017},{2,1018},{3,1019},{4,1020},{5,1021},{6,1022},{7,... | collective-permute-start | bytes 503816 | tf_op jit(solution)/shard_map/ppermute | solution.py:657
  7.6 23.2 %collective-permute-start = (f32[40,8,128]{2,1,0:T(8,128)S(1)}, f32[40,8,128]{2,1,0:T(8,128)S(1)}, u32[]{:S(2)}, u32[]{:S(2)}) collective-permute-start(f32[40,8,128]{2,1,0:T(8,128)S(1)} %get-tuple-element.34), channel_id=1, source_target_pairs={{0,8},{1,9},{2,10},{3,11},{4,12},{5,13},{6,14},{7,15},{8,0},{9,1},... | collective-permute-start | bytes 491528 | tf_op jit(solution)/shard_map/ppermute | solution.py:657
  24.3 7.6 %collective-permute-start.2 = (f32[1,16]{1,0:T(1,128)S(1)}, f32[1,16]{1,0:T(1,128)S(1)}, u32[]{:S(2)}, u32[]{:S(2)}) collective-permute-start(f32[1,16]{1,0:T(1,128)S(1)} %get-tuple-element.33.own_ref), channel_id=1, source_target_pairs={{0,1009},{1,1008},{2,1011},{3,1010},{4,1013},{5,1012},{6,1015},{7,... | collective-permute-start | bytes 200 | tf_op jit(solution)/shard_map/ppermute | solution.py:657
  28.9 4.3 %collective-permute-start.3 = (f32[1,16]{1,0:T(1,128)S(1)}, f32[1,16]{1,0:T(1,128)S(1)}, u32[]{:S(2)}, u32[]{:S(2)}) collective-permute-start(f32[1,16]{1,0:T(1,128)S(1)} %get-tuple-element.33.own_ref), channel_id=1, source_target_pairs={{0,16},{1,17},{2,18},{3,19},{4,20},{5,21},{6,22},{7,23},{8,24},{9,... | collective-permute-start | bytes 200 | tf_op jit(solution)/shard_map/ppermute | solution.py:657
  34.5 23.9 %all-to-all-start = ((f32[64,1,128]{2,1,0:T(1,128)}), f32[64,1,128]{2,1,0:T(1,128)S(1)}, u32[]{:S(2)}, u32[]{:S(2)}) async-start(f32[64,1,128]{2,1,0:T(1,128)} %get-tuple-element.42), calls=%async_computation | async-start | bytes 65536 | tf_op jit(solution)/shard_map/all_to_all | solution.py:750
  58.4 0.7 %collective-permute-start.4 = (f32[1,128]{1,0:T(1,128)S(1)}, f32[1,128]{1,0:T(1,128)S(1)}, u32[]{:S(2)}, u32[]{:S(2)}) collective-permute-start(f32[1,128]{1,0:T(1,128)S(1)} %group_end.1), channel_id=1, source_target_pairs={{48,56},{49,57},{50,58},{51,59},{52,60},{53,61},{54,62},{55,63},{5... | collective-permute-start | bytes 1544 | tf_op jit(solution)/shard_map/ppermute | solution.py:657

commit v6 on v5

--- a/solution.py
+++ b/solution.py
@@ -542,8 +542,8 @@
 def group_order(cases):
     places = tuple(range(1, GROUP)) + (0,)
     listed = [(place, case) for half in (0, 1) for place in places for case in range(half, cases, 2)]
-    listed.remove((0, 0))
-    return [(0, 0)] + listed
+    listed.remove((1, 1))
+    return [(1, 1)] + listed
 
 
 def place_in_group():

time: 60.1 us -> 59.6 us (level)
  waiting for transfers between devices: 6.96 us -> 6.17 us
    all_to_all x1, waiting for transfers between devices: 5.55 us -> 4.76 us  [body(): lax.all_to_all(sums, axes, 0, 0, axis_index_groups=groups, tiled=True)]
where the time goes in v6:
time: 59.6 us; the launch traced here: 59.3 us
  starting transfers between devices  46.8 us (79%)
  waiting for transfers between devices  6.17 us (10%)
  Pallas kernels  5.58 us (9%)
  between operations  0.73 us (1%)
    ppermute x5, starting transfers between devices, send(): return lax.ppermute(value, axes, pairs[name])  29.3 us
    all_to_all x1, starting transfers between devices, body(): lax.all_to_all(sums, axes, 0, 0, axis_index_groups=groups, tiled=True)  17.5 us
    pallas_call x7, Pallas kernels, call(): pl.pallas_call(kernel, out_shape=out_shape, in_specs=in_specs, out_specs=...  5.58 us
    all_to_all x1, waiting for transfers between devices, body(): lax.all_to_all(sums, axes, 0, 0, axis_index_groups=groups, tiled=True)  4.76 us
    ppermute x5, waiting for transfers between devices, send(): return lax.ppermute(value, axes, pairs[name])  1.41 us
  transfers between devices with their start and end apart: 6, of which 3 were waited for; matrix products, arithmetic and copies ran while one was open for 0% of the time, Pallas kernels for 3%

profile of v6, /device:TPU:1, one launch (start us, length us, event | category | flops | bytes accessed | tf_op | source)
XLA Modules:
  0.0 59.3 jit_solution(12812494404391224285)
XLA Ops:
  0.6 1.3 %load.1 = (f32[1,16]{1,0:T(1,128)S(1)}, f32[2,3,8,128]{3,2,1,0:T(8,128)S(1)}, f32[1,16]{1,0:T(1,128)S(1)}, s32[1,16]{1,0:T(1,128)S(1)}, f32[1,16]{1,0:T(1,128)S(...) custom-call(f32[1,16]{1,0:T(1,128)} %bitcast.15, s32[1,16]{1,0:T(1,128)} %bitcast.16, ...), custom_call_target="tpu_custom_call" | custom-call | tf_op jit(solution)/shard_map/load/pallas_call | solution.py:661
  1.9 0.3 pack_faces.1
  2.2 5.4 %collective-permute-start.1 = (f32[41,8,128]{2,1,0:T(8,128)S(1)}, f32[41,8,128]{2,1,0:T(8,128)S(1)}, u32[]{:S(2)}, u32[]{:S(2)}) collective-permute-start(f32[41,8,128]{2,1,0:T(8,128)S(1)} %get-tuple-element.35), channel_id=1, source_target_pairs={{0,1016},{1,1017},{2,1018},{3,1019},{4,1020},{5,1021},{6,1022},{7,... | collective-permute-start | bytes 503816 | tf_op jit(solution)/shard_map/ppermute | solution.py:657
  7.6 16.7 %collective-permute-start = (f32[40,8,128]{2,1,0:T(8,128)S(1)}, f32[40,8,128]{2,1,0:T(8,128)S(1)}, u32[]{:S(2)}, u32[]{:S(2)}) collective-permute-start(f32[40,8,128]{2,1,0:T(8,128)S(1)} %get-tuple-element.34), channel_id=1, source_target_pairs={{0,8},{1,9},{2,10},{3,11},{4,12},{5,13},{6,14},{7,15},{8,0},{9,1},... | collective-permute-start | bytes 491528 | tf_op jit(solution)/shard_map/ppermute | solution.py:657
  24.3 4.6 %collective-permute-start.2 = (f32[1,16]{1,0:T(1,128)S(1)}, f32[1,16]{1,0:T(1,128)S(1)}, u32[]{:S(2)}, u32[]{:S(2)}) collective-permute-start(f32[1,16]{1,0:T(1,128)S(1)} %get-tuple-element.33.own_ref), channel_id=1, source_target_pairs={{0,1009},{1,1008},{2,1011},{3,1010},{4,1013},{5,1012},{6,1015},{7,... | collective-permute-start | bytes 200 | tf_op jit(solution)/shard_map/ppermute | solution.py:657
  28.9 1.9 %collective-permute-start.3 = (f32[1,16]{1,0:T(1,128)S(1)}, f32[1,16]{1,0:T(1,128)S(1)}, u32[]{:S(2)}, u32[]{:S(2)}) collective-permute-start(f32[1,16]{1,0:T(1,128)S(1)} %get-tuple-element.33.own_ref), channel_id=1, source_target_pairs={{0,16},{1,17},{2,18},{3,19},{4,20},{5,21},{6,22},{7,23},{8,24},{9,... | collective-permute-start | bytes 200 | tf_op jit(solution)/shard_map/ppermute | solution.py:657
  30.9 0.0 collective-permute-done.from_a
  30.9 0.0 collective-permute-done.1.from_b
  30.9 0.9 %interior.1 = (f32[19,12,8,128]{3,2,1,0:T(8,128)S(1)}, f32[19,14,8,128]{3,2,1,0:T(8,128)S(1)}, f32[9,12,8,128]{3,2,1,0:T(8,128)S(1)}, f32[4,8,8,128]{3,2,1,0:T(8...) custom-call(f32[2,3,8,128]{3,2,1,0:T(8,128)S(1)} %get-tuple-element.30.accel_ref, ...), custom_call_target="tpu_custom_call" | custom-call | tf_op jit(solution)/shard_map/interior/pallas_call | solution.py:661
  31.8 0.1 collective-permute-done.2.across_ref
  31.9 1.3 %collective-permute-done.3.within_ref = f32[1,16]{1,0:T(1,128)S(1)} collective-permute-done((f32[1,16]{1,0:T(1,128)S(1)}, f32[1,16]{1,0:T(1,128)S(1)}, u32[]{:S(2)}, u32[]{:S(2)}) %collective-permute-start.3) | collective-permute-done | bytes 96 | tf_op jit(solution)/shard_map/ppermute | solution.py:657
  33.2 1.2 %sides.1 = (f32[19,8,128]{2,1,0:T(8,128)S(1)}, f32[19,8,128]{2,1,0:T(8,128)S(1)}, f32[64,1,128]{2,1,0:T(1,128)}) custom-call(f32[2,3,8,128]{3,2,1,0:T(8,128)S(1)} %get-tuple-element.30.accel_ref, f32[19,8,8,128]{3,2,1,0:T(8,128)S(1)} %get-tuple-element.31.adj_ref, f32[40,8,128]{2,1,0:T(8,128)S(1)} %collective-permute-done.from_a, ...), custom_call_target="tpu_custom_call" | custom-call | tf_op jit(solution)/shard_map/sides/pallas_call | solution.py:661
  34.5 17.5 %all-to-all-start = ((f32[64,1,128]{2,1,0:T(1,128)}), f32[64,1,128]{2,1,0:T(1,128)S(1)}, u32[]{:S(2)}, u32[]{:S(2)}) async-start(f32[64,1,128]{2,1,0:T(1,128)} %get-tuple-element.42), calls=%async_computation | async-start | bytes 65536 | tf_op jit(solution)/shard_map/all_to_all | solution.py:750
  52.0 1.1 %adjoint_start.1 = f32[19,8,8,128]{3,2,1,0:T(8,128)} custom-call(f32[2,3,8,128]{3,2,1,0:T(8,128)S(1)} %get-tuple-element.30.accel_ref, f32[8,128]{1,0:T(8,128)S(1)} %get-tuple-element.36.solid_ref, f32[19,12,8,128]{3,2,1,0:T(8,128)S(1)} %get-tuple-element.43.g_ref, f32[4,8,8,128]{3,2,1,0:T(8,128)S(1)} %get-tuple-element.44.mom_ref, ...), custom_call_target="tpu_custom_call" | custom-call | tf_op jit(solution)/shard_map/adjoint_start/pallas_call | solution.py:661
  53.1 4.8 %all-to-all-done.sums_ref = f32[64,1,128]{2,1,0:T(1,128)S(1)} async-done(((f32[64,1,128]{2,1,0:T(1,128)}), f32[64,1,128]{2,1,0:T(1,128)S(1)}, u32[]{:S(2)}, u32[]{:S(2)}) %all-to-all-start) | async-done | bytes 32800 | tf_op jit(solution)/shard_map/all_to_all | solution.py:750
  57.9 0.7 %collective-permute-start.4 = (f32[1,128]{1,0:T(1,128)S(1)}, f32[1,128]{1,0:T(1,128)S(1)}, u32[]{:S(2)}, u32[]{:S(2)}) collective-permute-start(f32[1,128]{1,0:T(1,128)S(1)} %group_end.1), channel_id=1, source_target_pairs={{48,56},{49,57},{50,58},{51,59},{52,60},{53,61},{54,62},{55,63},{5... | collective-permute-start | bytes 1544 | tf_op jit(solution)/shard_map/ppermute | solution.py:657
  58.6 0.0 collective-permute-done.4.outside_ref
  58.6 0.7 %update.1 = (f32[1,16]{1,0:T(1,128)}, f32[1,16]{1,0:T(1,128)}, f32[1,16]{1,0:T(1,128)}) custom-call(f32[64,1,128]{2,1,0:T(1,128)S(1)} %all-to-all-done.sums_ref, f32[1,128]{1,0:T(1,128)S(1)} %collective-permute-done.4.outside_ref, f32[1,16]{1,0:T(1,128)S(1)} %get-tuple-element.49.design_ref, s32[1,16]{1,0:T(1,128)S(1)} %get-tuple-element.50.mask_ref, ...), custom_call_target="tpu_custom_call" | custom-call | tf_op jit(solution)/shard_map/update/pallas_call | solution.py:661
  (1 shorter events, 0.0 us)
Async XLA Ops:
  2.2 28.7 %collective-permute-start.1 = (f32[41,8,128]{2,1,0:T(8,128)S(1)}, f32[41,8,128]{2,1,0:T(8,128)S(1)}, u32[]{:S(2)}, u32[]{:S(2)}) collective-permute-start(f32[41,8,128]{2,1,0:T(8,128)S(1)} %get-tuple-element.35), channel_id=1, source_target_pairs={{0,1016},{1,1017},{2,1018},{3,1019},{4,1020},{5,1021},{6,1022},{7,... | collective-permute-start | bytes 503816 | tf_op jit(solution)/shard_map/ppermute | solution.py:657
  7.6 23.2 %collective-permute-start = (f32[40,8,128]{2,1,0:T(8,128)S(1)}, f32[40,8,128]{2,1,0:T(8,128)S(1)}, u32[]{:S(2)}, u32[]{:S(2)}) collective-permute-start(f32[40,8,128]{2,1,0:T(8,128)S(1)} %get-tuple-element.34), channel_id=1, source_target_pairs={{0,8},{1,9},{2,10},{3,11},{4,12},{5,13},{6,14},{7,15},{8,0},{9,1},... | collective-permute-start | bytes 491528 | tf_op jit(solution)/shard_map/ppermute | solution.py:657
  24.3 7.6 %collective-permute-start.2 = (f32[1,16]{1,0:T(1,128)S(1)}, f32[1,16]{1,0:T(1,128)S(1)}, u32[]{:S(2)}, u32[]{:S(2)}) collective-permute-start(f32[1,16]{1,0:T(1,128)S(1)} %get-tuple-element.33.own_ref), channel_id=1, source_target_pairs={{0,1009},{1,1008},{2,1011},{3,1010},{4,1013},{5,1012},{6,1015},{7,... | collective-permute-start | bytes 200 | tf_op jit(solution)/shard_map/ppermute | solution.py:657
  28.9 4.3 %collective-permute-start.3 = (f32[1,16]{1,0:T(1,128)S(1)}, f32[1,16]{1,0:T(1,128)S(1)}, u32[]{:S(2)}, u32[]{:S(2)}) collective-permute-start(f32[1,16]{1,0:T(1,128)S(1)} %get-tuple-element.33.own_ref), channel_id=1, source_target_pairs={{0,16},{1,17},{2,18},{3,19},{4,20},{5,21},{6,22},{7,23},{8,24},{9,... | collective-permute-start | bytes 200 | tf_op jit(solution)/shard_map/ppermute | solution.py:657
  34.5 23.4 %all-to-all-start = ((f32[64,1,128]{2,1,0:T(1,128)}), f32[64,1,128]{2,1,0:T(1,128)S(1)}, u32[]{:S(2)}, u32[]{:S(2)}) async-start(f32[64,1,128]{2,1,0:T(1,128)} %get-tuple-element.42), calls=%async_computation | async-start | bytes 65536 | tf_op jit(solution)/shard_map/all_to_all | solution.py:750
  57.9 0.7 %collective-permute-start.4 = (f32[1,128]{1,0:T(1,128)S(1)}, f32[1,128]{1,0:T(1,128)S(1)}, u32[]{:S(2)}, u32[]{:S(2)}) collective-permute-start(f32[1,128]{1,0:T(1,128)S(1)} %group_end.1), channel_id=1, source_target_pairs={{48,56},{49,57},{50,58},{51,59},{52,60},{53,61},{54,62},{55,63},{5... | collective-permute-start | bytes 1544 | tf_op jit(solution)/shard_map/ppermute | solution.py:657

commit v7 on v6

--- a/solution.py
+++ b/solution.py
@@ -59,8 +59,8 @@
 RUN = 16
 FORWARD_UNROLL = 2
 BACKWARD_UNROLL = 6
-GROUP = 8
-OFFSET = 7
+GROUP = 4
+OFFSET = 3
 
 
 def shift_yz(value, vel_id, direction):
@@ -540,10 +540,10 @@
 
 
 def group_order(cases):
-    places = tuple(range(1, GROUP)) + (0,)
+    places = (2, 1) + tuple(range(3, GROUP)) + (0,)
     listed = [(place, case) for half in (0, 1) for place in places for case in range(half, cases, 2)]
-    listed.remove((1, 1))
-    return [(1, 1)] + listed
+    listed.remove((3, 1))
+    return [(3, 1)] + listed
 
 
 def place_in_group():

time: 59.6 us -> 59.2 us (level)
  starting transfers between devices: 46.8 us -> 45.5 us
  waiting for transfers between devices: 6.17 us -> 7.07 us
    all_to_all x1, starting transfers between devices: 17.5 us -> 16.2 us  [body(): lax.all_to_all(sums, axes, 0, 0, axis_index_groups=groups, tiled=True)]
    all_to_all x1, waiting for transfers between devices: 4.76 us -> 5.67 us  [body(): lax.all_to_all(sums, axes, 0, 0, axis_index_groups=groups, tiled=True)]
where the time goes in v7:
time: 59.2 us; the launch traced here: 58.8 us
  starting transfers between devices  45.5 us (77%)
  waiting for transfers between devices  7.07 us (12%)
  Pallas kernels  5.57 us (9%)
  between operations  0.73 us (1%)
    ppermute x5, starting transfers between devices, send(): return lax.ppermute(value, axes, pairs[name])  29.3 us
    all_to_all x1, starting transfers between devices, body(): lax.all_to_all(sums, axes, 0, 0, axis_index_groups=groups, tiled=True)  16.2 us
    all_to_all x1, waiting for transfers between devices, body(): lax.all_to_all(sums, axes, 0, 0, axis_index_groups=groups, tiled=True)  5.67 us
    pallas_call x7, Pallas kernels, call(): pl.pallas_call(kernel, out_shape=out_shape, in_specs=in_specs, out_specs=...  5.57 us
    ppermute x5, waiting for transfers between devices, send(): return lax.ppermute(value, axes, pairs[name])  1.41 us
  transfers between devices with their start and end apart: 6, of which 3 were waited for; matrix products, arithmetic and copies ran while one was open for 0% of the time, Pallas kernels for 3%

profile of v7, /device:TPU:1, one launch (start us, length us, event | category | flops | bytes accessed | tf_op | source)
XLA Modules:
  0.0 58.8 jit_solution(9041152163284056189)
XLA Ops:
  0.6 1.3 %load.1 = (f32[1,16]{1,0:T(1,128)S(1)}, f32[2,3,8,128]{3,2,1,0:T(8,128)S(1)}, f32[1,16]{1,0:T(1,128)S(1)}, s32[1,16]{1,0:T(1,128)S(1)}, f32[1,16]{1,0:T(1,128)S(...) custom-call(f32[1,16]{1,0:T(1,128)} %bitcast.15, s32[1,16]{1,0:T(1,128)} %bitcast.16, ...), custom_call_target="tpu_custom_call" | custom-call | tf_op jit(solution)/shard_map/load/pallas_call | solution.py:661
  1.9 0.3 pack_faces.1
  2.2 5.4 %collective-permute-start.1 = (f32[41,8,128]{2,1,0:T(8,128)S(1)}, f32[41,8,128]{2,1,0:T(8,128)S(1)}, u32[]{:S(2)}, u32[]{:S(2)}) collective-permute-start(f32[41,8,128]{2,1,0:T(8,128)S(1)} %get-tuple-element.35), channel_id=1, source_target_pairs={{0,1016},{1,1017},{2,1018},{3,1019},{4,1020},{5,1021},{6,1022},{7,... | collective-permute-start | bytes 503816 | tf_op jit(solution)/shard_map/ppermute | solution.py:657
  7.6 16.7 %collective-permute-start = (f32[40,8,128]{2,1,0:T(8,128)S(1)}, f32[40,8,128]{2,1,0:T(8,128)S(1)}, u32[]{:S(2)}, u32[]{:S(2)}) collective-permute-start(f32[40,8,128]{2,1,0:T(8,128)S(1)} %get-tuple-element.34), channel_id=1, source_target_pairs={{0,8},{1,9},{2,10},{3,11},{4,12},{5,13},{6,14},{7,15},{8,0},{9,1},... | collective-permute-start | bytes 491528 | tf_op jit(solution)/shard_map/ppermute | solution.py:657
  24.3 4.6 %collective-permute-start.2 = (f32[1,16]{1,0:T(1,128)S(1)}, f32[1,16]{1,0:T(1,128)S(1)}, u32[]{:S(2)}, u32[]{:S(2)}) collective-permute-start(f32[1,16]{1,0:T(1,128)S(1)} %get-tuple-element.33.own_ref), channel_id=1, source_target_pairs={{0,1009},{1,1008},{2,1011},{3,1010},{4,1013},{5,1012},{6,1015},{7,... | collective-permute-start | bytes 200 | tf_op jit(solution)/shard_map/ppermute | solution.py:657
  28.9 1.9 %collective-permute-start.3 = (f32[1,16]{1,0:T(1,128)S(1)}, f32[1,16]{1,0:T(1,128)S(1)}, u32[]{:S(2)}, u32[]{:S(2)}) collective-permute-start(f32[1,16]{1,0:T(1,128)S(1)} %get-tuple-element.33.own_ref), channel_id=1, source_target_pairs={{0,16},{1,17},{2,18},{3,19},{4,20},{5,21},{6,22},{7,23},{8,24},{9,... | collective-permute-start | bytes 200 | tf_op jit(solution)/shard_map/ppermute | solution.py:657
  30.9 0.0 collective-permute-done.from_a
  30.9 0.0 collective-permute-done.1.from_b
  30.9 0.9 %interior.1 = (f32[19,12,8,128]{3,2,1,0:T(8,128)S(1)}, f32[19,14,8,128]{3,2,1,0:T(8,128)S(1)}, f32[9,12,8,128]{3,2,1,0:T(8,128)S(1)}, f32[4,8,8,128]{3,2,1,0:T(8...) custom-call(f32[2,3,8,128]{3,2,1,0:T(8,128)S(1)} %get-tuple-element.30.accel_ref, ...), custom_call_target="tpu_custom_call" | custom-call | tf_op jit(solution)/shard_map/interior/pallas_call | solution.py:661
  31.8 0.1 collective-permute-done.2.across_ref
  31.9 1.3 %collective-permute-done.3.within_ref = f32[1,16]{1,0:T(1,128)S(1)} collective-permute-done((f32[1,16]{1,0:T(1,128)S(1)}, f32[1,16]{1,0:T(1,128)S(1)}, u32[]{:S(2)}, u32[]{:S(2)}) %collective-permute-start.3) | collective-permute-done | bytes 96 | tf_op jit(solution)/shard_map/ppermute | solution.py:657
  33.2 1.2 %sides.1 = (f32[19,8,128]{2,1,0:T(8,128)S(1)}, f32[19,8,128]{2,1,0:T(8,128)S(1)}, f32[32,1,128]{2,1,0:T(1,128)}) custom-call(f32[2,3,8,128]{3,2,1,0:T(8,128)S(1)} %get-tuple-element.30.accel_ref, f32[19,8,8,128]{3,2,1,0:T(8,128)S(1)} %get-tuple-element.31.adj_ref, f32[40,8,128]{2,1,0:T(8,128)S(1)} %collective-permute-done.from_a, ...), custom_call_target="tpu_custom_call" | custom-call | tf_op jit(solution)/shard_map/sides/pallas_call | solution.py:661
  34.5 16.2 %all-to-all-start = ((f32[32,1,128]{2,1,0:T(1,128)}), f32[32,1,128]{2,1,0:T(1,128)S(1)}, u32[]{:S(2)}, u32[]{:S(2)}) async-start(f32[32,1,128]{2,1,0:T(1,128)} %get-tuple-element.42), calls=%async_computation | async-start | bytes 32768 | tf_op jit(solution)/shard_map/all_to_all | solution.py:750
  50.6 1.1 %adjoint_start.1 = f32[19,8,8,128]{3,2,1,0:T(8,128)} custom-call(f32[2,3,8,128]{3,2,1,0:T(8,128)S(1)} %get-tuple-element.30.accel_ref, f32[8,128]{1,0:T(8,128)S(1)} %get-tuple-element.36.solid_ref, f32[19,12,8,128]{3,2,1,0:T(8,128)S(1)} %get-tuple-element.43.g_ref, f32[4,8,8,128]{3,2,1,0:T(8,128)S(1)} %get-tuple-element.44.mom_ref, ...), custom_call_target="tpu_custom_call" | custom-call | tf_op jit(solution)/shard_map/adjoint_start/pallas_call | solution.py:661
  51.8 5.7 %all-to-all-done.sums_ref = f32[32,1,128]{2,1,0:T(1,128)S(1)} async-done(((f32[32,1,128]{2,1,0:T(1,128)}), f32[32,1,128]{2,1,0:T(1,128)S(1)}, u32[]{:S(2)}, u32[]{:S(2)}) %all-to-all-start) | async-done | bytes 16416 | tf_op jit(solution)/shard_map/all_to_all | solution.py:750
  57.4 0.7 %collective-permute-start.4 = (f32[1,128]{1,0:T(1,128)S(1)}, f32[1,128]{1,0:T(1,128)S(1)}, u32[]{:S(2)}, u32[]{:S(2)}) collective-permute-start(f32[1,128]{1,0:T(1,128)S(1)} %group_end.1), channel_id=1, source_target_pairs={{16,24},{17,25},{18,26},{19,27},{20,28},{21,29},{22,30},{23,31},{2... | collective-permute-start | bytes 1544 | tf_op jit(solution)/shard_map/ppermute | solution.py:657
  58.1 0.0 collective-permute-done.4.outside_ref
  58.1 0.7 %update.1 = (f32[1,16]{1,0:T(1,128)}, f32[1,16]{1,0:T(1,128)}, f32[1,16]{1,0:T(1,128)}) custom-call(f32[32,1,128]{2,1,0:T(1,128)S(1)} %all-to-all-done.sums_ref, f32[1,128]{1,0:T(1,128)S(1)} %collective-permute-done.4.outside_ref, f32[1,16]{1,0:T(1,128)S(1)} %get-tuple-element.49.design_ref, s32[1,16]{1,0:T(1,128)S(1)} %get-tuple-element.50.mask_ref, ...), custom_call_target="tpu_custom_call" | custom-call | tf_op jit(solution)/shard_map/update/pallas_call | solution.py:661
  (1 shorter events, 0.0 us)
Async XLA Ops:
  2.2 28.7 %collective-permute-start.1 = (f32[41,8,128]{2,1,0:T(8,128)S(1)}, f32[41,8,128]{2,1,0:T(8,128)S(1)}, u32[]{:S(2)}, u32[]{:S(2)}) collective-permute-start(f32[41,8,128]{2,1,0:T(8,128)S(1)} %get-tuple-element.35), channel_id=1, source_target_pairs={{0,1016},{1,1017},{2,1018},{3,1019},{4,1020},{5,1021},{6,1022},{7,... | collective-permute-start | bytes 503816 | tf_op jit(solution)/shard_map/ppermute | solution.py:657
  7.6 23.2 %collective-permute-start = (f32[40,8,128]{2,1,0:T(8,128)S(1)}, f32[40,8,128]{2,1,0:T(8,128)S(1)}, u32[]{:S(2)}, u32[]{:S(2)}) collective-permute-start(f32[40,8,128]{2,1,0:T(8,128)S(1)} %get-tuple-element.34), channel_id=1, source_target_pairs={{0,8},{1,9},{2,10},{3,11},{4,12},{5,13},{6,14},{7,15},{8,0},{9,1},... | collective-permute-start | bytes 491528 | tf_op jit(solution)/shard_map/ppermute | solution.py:657
  24.3 7.6 %collective-permute-start.2 = (f32[1,16]{1,0:T(1,128)S(1)}, f32[1,16]{1,0:T(1,128)S(1)}, u32[]{:S(2)}, u32[]{:S(2)}) collective-permute-start(f32[1,16]{1,0:T(1,128)S(1)} %get-tuple-element.33.own_ref), channel_id=1, source_target_pairs={{0,1009},{1,1008},{2,1011},{3,1010},{4,1013},{5,1012},{6,1015},{7,... | collective-permute-start | bytes 200 | tf_op jit(solution)/shard_map/ppermute | solution.py:657
  28.9 4.3 %collective-permute-start.3 = (f32[1,16]{1,0:T(1,128)S(1)}, f32[1,16]{1,0:T(1,128)S(1)}, u32[]{:S(2)}, u32[]{:S(2)}) collective-permute-start(f32[1,16]{1,0:T(1,128)S(1)} %get-tuple-element.33.own_ref), channel_id=1, source_target_pairs={{0,16},{1,17},{2,18},{3,19},{4,20},{5,21},{6,22},{7,23},{8,24},{9,... | collective-permute-start | bytes 200 | tf_op jit(solution)/shard_map/ppermute | solution.py:657
  34.5 23.0 %all-to-all-start = ((f32[32,1,128]{2,1,0:T(1,128)}), f32[32,1,128]{2,1,0:T(1,128)S(1)}, u32[]{:S(2)}, u32[]{:S(2)}) async-start(f32[32,1,128]{2,1,0:T(1,128)} %get-tuple-element.42), calls=%async_computation | async-start | bytes 32768 | tf_op jit(solution)/shard_map/all_to_all | solution.py:750
  57.4 0.7 %collective-permute-start.4 = (f32[1,128]{1,0:T(1,128)S(1)}, f32[1,128]{1,0:T(1,128)S(1)}, u32[]{:S(2)}, u32[]{:S(2)}) collective-permute-start(f32[1,128]{1,0:T(1,128)S(1)} %group_end.1), channel_id=1, source_target_pairs={{16,24},{17,25},{18,26},{19,27},{20,28},{21,29},{22,30},{23,31},{2... | collective-permute-start | bytes 1544 | tf_op jit(solution)/shard_map/ppermute | solution.py:657

commit v8 on v7

--- a/solution.py
+++ b/solution.py
@@ -346,6 +346,13 @@
     pl.when(jnp.logical_not(even))(lambda: both(to_a, to_b))
 
 
+def enter_kernel(*refs):
+    *loaded, to_b, to_a, table, sems, row = refs
+    load_kernel(*loaded, table, sems)
+    blocks, accel, *_, f_out, adj_out = loaded[7:]
+    pack_kernel(f_out, adj_out, accel, blocks, to_b, to_a, row)
+
+
 def boundary(low, message, solid, solid_own, f_next, adj_ref, accel):
     inward, outward = (Q_PLUS, Q_MINUS) if low else (Q_MINUS, Q_PLUS)
     beside, face, layer, behind = (2, 3, 0, 1) if low else (11, 10, 7, 6)
@@ -672,9 +679,9 @@
         return jax.ShapeDtypeStruct(dims, F32)
 
     row = pltpu.VMEM((8, 128), F32)
-    blocks, accel, *kept, f_zero, adjoint = call(
-        load_kernel,
-        "load",
+    blocks, accel, *kept, f_zero, adjoint, to_b, to_a = call(
+        enter_kernel,
+        "load_and_pack",
         (
             shape(1, 16),
             shape(2, 3, 8, 128),
@@ -684,24 +691,15 @@
             shape(1, 16),
             jax.ShapeDtypeStruct((Q, 64, 128), jnp.bfloat16),
             shape(Q, 8, 8, 128),
+            shape(B_ROWS, 8, 128),
+            shape(ROWS, 8, 128),
         ),
         [HBM_SPEC] * 7,
-        [pltpu.SMEM((2, 3), jnp.int32), pltpu.SemaphoreType.DMA((7,))],
+        [pltpu.SMEM((2, 3), jnp.int32), pltpu.SemaphoreType.DMA((7,)), row],
         *(
             pltpu.with_memory_space_constraint(a, pltpu.HBM)
             for a in (*flat[:2], accel_table[0], *flat[2:], f_zero, adjoint)
         ),
-    )
-    to_b, to_a = call(
-        pack_kernel,
-        "pack_faces",
-        (shape(B_ROWS, 8, 128), shape(ROWS, 8, 128)),
-        [VMEM_SPEC] * 4,
-        [row],
-        f_zero,
-        adjoint,
-        accel,
-        blocks,
     )
     from_b = send(to_b, "beyond")
     from_a = send(to_a, "chip")

time: 59.2 us -> 59.2 us (level)
    pallas_call x7 -> x6, Pallas kernels: 5.57 us -> 5.57 us  [call(): pl.pallas_call(kernel, out_shape=out_shape, in_specs=in_specs, out_specs=...]
where the time goes in v8:
time: 59.2 us; the launch traced here: 58.8 us
  starting transfers between devices  45.5 us (77%)
  waiting for transfers between devices  7.07 us (12%)
  Pallas kernels  5.57 us (9%)
  between operations  0.72 us (1%)
    ppermute x5, starting transfers between devices, send(): return lax.ppermute(value, axes, pairs[name])  29.3 us
    all_to_all x1, starting transfers between devices, body(): lax.all_to_all(sums, axes, 0, 0, axis_index_groups=groups, tiled=True)  16.2 us
    all_to_all x1, waiting for transfers between devices, body(): lax.all_to_all(sums, axes, 0, 0, axis_index_groups=groups, tiled=True)  5.66 us
    pallas_call x6, Pallas kernels, call(): pl.pallas_call(kernel, out_shape=out_shape, in_specs=in_specs, out_specs=...  5.57 us
    ppermute x5, waiting for transfers between devices, send(): return lax.ppermute(value, axes, pairs[name])  1.41 us
  transfers between devices with their start and end apart: 6, of which 3 were waited for; matrix products, arithmetic and copies ran while one was open for 0% of the time, Pallas kernels for 3%

profile of v8, /device:TPU:1, one launch (start us, length us, event | category | flops | bytes accessed | tf_op | source)
XLA Modules:
  0.0 58.8 jit_solution(2102215346415898144)
XLA Ops:
  0.6 1.6 %load_and_pack.1 = (f32[1,16]{1,0:T(1,128)S(1)}, f32[2,3,8,128]{3,2,1,0:T(8,128)S(1)}, f32[1,16]{1,0:T(1,128)S(1)}, s32[1,16]{1,0:T(1,128)S(1)}, f32[1,16]{1,0:T...) custom-call(f32[1,16]{1,0:T(1,128)} %bitcast.15, ...), custom_call_target="tpu_custom_call" | custom-call | tf_op jit(solution)/shard_map/load_and_pack/pallas_call | solution.py:668
  2.2 5.4 %collective-permute-start.1 = (f32[41,8,128]{2,1,0:T(8,128)S(1)}, f32[41,8,128]{2,1,0:T(8,128)S(1)}, u32[]{:S(2)}, u32[]{:S(2)}) collective-permute-start(f32[41,8,128]{2,1,0:T(8,128)S(1)} %get-tuple-element.33), channel_id=1, source_target_pairs={{0,1016},{1,1017},{2,1018},{3,1019},{4,1020},{5,1021},{6,1022},{7,... | collective-permute-start | bytes 503816 | tf_op jit(solution)/shard_map/ppermute | solution.py:664
  7.6 16.7 %collective-permute-start = (f32[40,8,128]{2,1,0:T(8,128)S(1)}, f32[40,8,128]{2,1,0:T(8,128)S(1)}, u32[]{:S(2)}, u32[]{:S(2)}) collective-permute-start(f32[40,8,128]{2,1,0:T(8,128)S(1)} %get-tuple-element.32), channel_id=1, source_target_pairs={{0,8},{1,9},{2,10},{3,11},{4,12},{5,13},{6,14},{7,15},{8,0},{9,1},... | collective-permute-start | bytes 491528 | tf_op jit(solution)/shard_map/ppermute | solution.py:664
  24.3 4.6 %collective-permute-start.2 = (f32[1,16]{1,0:T(1,128)S(1)}, f32[1,16]{1,0:T(1,128)S(1)}, u32[]{:S(2)}, u32[]{:S(2)}) collective-permute-start(f32[1,16]{1,0:T(1,128)S(1)} %get-tuple-element.34.own_ref), channel_id=1, source_target_pairs={{0,1009},{1,1008},{2,1011},{3,1010},{4,1013},{5,1012},{6,1015},{7,... | collective-permute-start | bytes 200 | tf_op jit(solution)/shard_map/ppermute | solution.py:664
  28.9 1.9 %collective-permute-start.3 = (f32[1,16]{1,0:T(1,128)S(1)}, f32[1,16]{1,0:T(1,128)S(1)}, u32[]{:S(2)}, u32[]{:S(2)}) collective-permute-start(f32[1,16]{1,0:T(1,128)S(1)} %get-tuple-element.34.own_ref), channel_id=1, source_target_pairs={{0,16},{1,17},{2,18},{3,19},{4,20},{5,21},{6,22},{7,23},{8,24},{9,... | collective-permute-start | bytes 200 | tf_op jit(solution)/shard_map/ppermute | solution.py:664
  30.9 0.0 collective-permute-done.from_a
  30.9 0.0 collective-permute-done.1.from_b
  30.9 0.9 %interior.1 = (f32[19,12,8,128]{3,2,1,0:T(8,128)S(1)}, f32[19,14,8,128]{3,2,1,0:T(8,128)S(1)}, f32[9,12,8,128]{3,2,1,0:T(8,128)S(1)}, f32[4,8,8,128]{3,2,1,0:T(8...) custom-call(f32[2,3,8,128]{3,2,1,0:T(8,128)S(1)} %get-tuple-element.30.accel_ref, ...), custom_call_target="tpu_custom_call" | custom-call | tf_op jit(solution)/shard_map/interior/pallas_call | solution.py:668
  31.8 0.1 collective-permute-done.2.across_ref
  31.9 1.3 %collective-permute-done.3.within_ref = f32[1,16]{1,0:T(1,128)S(1)} collective-permute-done((f32[1,16]{1,0:T(1,128)S(1)}, f32[1,16]{1,0:T(1,128)S(1)}, u32[]{:S(2)}, u32[]{:S(2)}) %collective-permute-start.3) | collective-permute-done | bytes 96 | tf_op jit(solution)/shard_map/ppermute | solution.py:664
  33.2 1.2 %sides.1 = (f32[19,8,128]{2,1,0:T(8,128)S(1)}, f32[19,8,128]{2,1,0:T(8,128)S(1)}, f32[32,1,128]{2,1,0:T(1,128)}) custom-call(f32[2,3,8,128]{3,2,1,0:T(8,128)S(1)} %get-tuple-element.30.accel_ref, f32[19,8,8,128]{3,2,1,0:T(8,128)S(1)} %get-tuple-element.31.adj_ref, f32[40,8,128]{2,1,0:T(8,128)S(1)} %collective-permute-done.from_a, ...), custom_call_target="tpu_custom_call" | custom-call | tf_op jit(solution)/shard_map/sides/pallas_call | solution.py:668
  34.5 16.2 %all-to-all-start = ((f32[32,1,128]{2,1,0:T(1,128)}), f32[32,1,128]{2,1,0:T(1,128)S(1)}, u32[]{:S(2)}, u32[]{:S(2)}) async-start(f32[32,1,128]{2,1,0:T(1,128)} %get-tuple-element.42), calls=%async_computation | async-start | bytes 32768 | tf_op jit(solution)/shard_map/all_to_all | solution.py:748
  50.7 1.1 %adjoint_start.1 = f32[19,8,8,128]{3,2,1,0:T(8,128)} custom-call(f32[2,3,8,128]{3,2,1,0:T(8,128)S(1)} %get-tuple-element.30.accel_ref, f32[8,128]{1,0:T(8,128)S(1)} %get-tuple-element.36.solid_ref, f32[19,12,8,128]{3,2,1,0:T(8,128)S(1)} %get-tuple-element.43.g_ref, f32[4,8,8,128]{3,2,1,0:T(8,128)S(1)} %get-tuple-element.44.mom_ref, ...), custom_call_target="tpu_custom_call" | custom-call | tf_op jit(solution)/shard_map/adjoint_start/pallas_call | solution.py:668
  51.8 5.7 %all-to-all-done.sums_ref = f32[32,1,128]{2,1,0:T(1,128)S(1)} async-done(((f32[32,1,128]{2,1,0:T(1,128)}), f32[32,1,128]{2,1,0:T(1,128)S(1)}, u32[]{:S(2)}, u32[]{:S(2)}) %all-to-all-start) | async-done | bytes 16416 | tf_op jit(solution)/shard_map/all_to_all | solution.py:748
  57.4 0.7 %collective-permute-start.4 = (f32[1,128]{1,0:T(1,128)S(1)}, f32[1,128]{1,0:T(1,128)S(1)}, u32[]{:S(2)}, u32[]{:S(2)}) collective-permute-start(f32[1,128]{1,0:T(1,128)S(1)} %group_end.1), channel_id=1, source_target_pairs={{16,24},{17,25},{18,26},{19,27},{20,28},{21,29},{22,30},{23,31},{2... | collective-permute-start | bytes 1544 | tf_op jit(solution)/shard_map/ppermute | solution.py:664
  58.1 0.0 collective-permute-done.4.outside_ref
  58.1 0.7 %update.1 = (f32[1,16]{1,0:T(1,128)}, f32[1,16]{1,0:T(1,128)}, f32[1,16]{1,0:T(1,128)}) custom-call(f32[32,1,128]{2,1,0:T(1,128)S(1)} %all-to-all-done.sums_ref, f32[1,128]{1,0:T(1,128)S(1)} %collective-permute-done.4.outside_ref, f32[1,16]{1,0:T(1,128)S(1)} %get-tuple-element.49.design_ref, s32[1,16]{1,0:T(1,128)S(1)} %get-tuple-element.50.mask_ref, ...), custom_call_target="tpu_custom_call" | custom-call | tf_op jit(solution)/shard_map/update/pallas_call | solution.py:668
  (1 shorter events, 0.0 us)
Async XLA Ops:
  2.2 28.7 %collective-permute-start.1 = (f32[41,8,128]{2,1,0:T(8,128)S(1)}, f32[41,8,128]{2,1,0:T(8,128)S(1)}, u32[]{:S(2)}, u32[]{:S(2)}) collective-permute-start(f32[41,8,128]{2,1,0:T(8,128)S(1)} %get-tuple-element.33), channel_id=1, source_target_pairs={{0,1016},{1,1017},{2,1018},{3,1019},{4,1020},{5,1021},{6,1022},{7,... | collective-permute-start | bytes 503816 | tf_op jit(solution)/shard_map/ppermute | solution.py:664
  7.6 23.2 %collective-permute-start = (f32[40,8,128]{2,1,0:T(8,128)S(1)}, f32[40,8,128]{2,1,0:T(8,128)S(1)}, u32[]{:S(2)}, u32[]{:S(2)}) collective-permute-start(f32[40,8,128]{2,1,0:T(8,128)S(1)} %get-tuple-element.32), channel_id=1, source_target_pairs={{0,8},{1,9},{2,10},{3,11},{4,12},{5,13},{6,14},{7,15},{8,0},{9,1},... | collective-permute-start | bytes 491528 | tf_op jit(solution)/shard_map/ppermute | solution.py:664
  24.3 7.6 %collective-permute-start.2 = (f32[1,16]{1,0:T(1,128)S(1)}, f32[1,16]{1,0:T(1,128)S(1)}, u32[]{:S(2)}, u32[]{:S(2)}) collective-permute-start(f32[1,16]{1,0:T(1,128)S(1)} %get-tuple-element.34.own_ref), channel_id=1, source_target_pairs={{0,1009},{1,1008},{2,1011},{3,1010},{4,1013},{5,1012},{6,1015},{7,... | collective-permute-start | bytes 200 | tf_op jit(solution)/shard_map/ppermute | solution.py:664
  28.9 4.3 %collective-permute-start.3 = (f32[1,16]{1,0:T(1,128)S(1)}, f32[1,16]{1,0:T(1,128)S(1)}, u32[]{:S(2)}, u32[]{:S(2)}) collective-permute-start(f32[1,16]{1,0:T(1,128)S(1)} %get-tuple-element.34.own_ref), channel_id=1, source_target_pairs={{0,16},{1,17},{2,18},{3,19},{4,20},{5,21},{6,22},{7,23},{8,24},{9,... | collective-permute-start | bytes 200 | tf_op jit(solution)/shard_map/ppermute | solution.py:664
  34.5 23.0 %all-to-all-start = ((f32[32,1,128]{2,1,0:T(1,128)}), f32[32,1,128]{2,1,0:T(1,128)S(1)}, u32[]{:S(2)}, u32[]{:S(2)}) async-start(f32[32,1,128]{2,1,0:T(1,128)} %get-tuple-element.42), calls=%async_computation | async-start | bytes 32768 | tf_op jit(solution)/shard_map/all_to_all | solution.py:748
  57.4 0.7 %collective-permute-start.4 = (f32[1,128]{1,0:T(1,128)S(1)}, f32[1,128]{1,0:T(1,128)S(1)}, u32[]{:S(2)}, u32[]{:S(2)}) collective-permute-start(f32[1,128]{1,0:T(1,128)S(1)} %group_end.1), channel_id=1, source_target_pairs={{16,24},{17,25},{18,26},{19,27},{20,28},{21,29},{22,30},{23,31},{2... | collective-permute-start | bytes 1544 | tf_op jit(solution)/shard_map/ppermute | solution.py:664

commit v9 on v8

--- a/solution.py
+++ b/solution.py
@@ -280,7 +280,7 @@
             )
         )
     ]
-    for copy in copies:
+    for copy in copies[5:] + copies[:5]:
         copy.start()
     for copy in copies[:5]:
         copy.wait()

time: 59.2 us -> 59.2 us (level)
  no operation moved by 1% of the time
where the time goes in v9:
time: 59.2 us; the launch traced here: 58.8 us
  starting transfers between devices  45.5 us (77%)
  waiting for transfers between devices  7.07 us (12%)
  Pallas kernels  5.51 us (9%)
  between operations  0.72 us (1%)
    ppermute x5, starting transfers between devices, send(): return lax.ppermute(value, axes, pairs[name])  29.3 us
    all_to_all x1, starting transfers between devices, body(): lax.all_to_all(sums, axes, 0, 0, axis_index_groups=groups, tiled=True)  16.2 us
    all_to_all x1, waiting for transfers between devices, body(): lax.all_to_all(sums, axes, 0, 0, axis_index_groups=groups, tiled=True)  5.66 us
    pallas_call x6, Pallas kernels, call(): pl.pallas_call(kernel, out_shape=out_shape, in_specs=in_specs, out_specs=...  5.51 us
    ppermute x5, waiting for transfers between devices, send(): return lax.ppermute(value, axes, pairs[name])  1.41 us
  transfers between devices with their start and end apart: 6, of which 3 were waited for; matrix products, arithmetic and copies ran while one was open for 0% of the time, Pallas kernels for 3%

profile of v9, /device:TPU:1, one launch (start us, length us, event | category | flops | bytes accessed | tf_op | source)
XLA Modules:
  0.0 58.8 jit_solution(10788611654755846413)
XLA Ops:
  0.6 1.5 %load_and_pack.1 = (f32[1,16]{1,0:T(1,128)S(1)}, f32[2,3,8,128]{3,2,1,0:T(8,128)S(1)}, f32[1,16]{1,0:T(1,128)S(1)}, s32[1,16]{1,0:T(1,128)S(1)}, f32[1,16]{1,0:T...) custom-call(f32[1,16]{1,0:T(1,128)} %bitcast.15, ...), custom_call_target="tpu_custom_call" | custom-call | tf_op jit(solution)/shard_map/load_and_pack/pallas_call | solution.py:668
  2.2 5.4 %collective-permute-start.1 = (f32[41,8,128]{2,1,0:T(8,128)S(1)}, f32[41,8,128]{2,1,0:T(8,128)S(1)}, u32[]{:S(2)}, u32[]{:S(2)}) collective-permute-start(f32[41,8,128]{2,1,0:T(8,128)S(1)} %get-tuple-element.33), channel_id=1, source_target_pairs={{0,1016},{1,1017},{2,1018},{3,1019},{4,1020},{5,1021},{6,1022},{7,... | collective-permute-start | bytes 503816 | tf_op jit(solution)/shard_map/ppermute | solution.py:664
  7.5 16.7 %collective-permute-start = (f32[40,8,128]{2,1,0:T(8,128)S(1)}, f32[40,8,128]{2,1,0:T(8,128)S(1)}, u32[]{:S(2)}, u32[]{:S(2)}) collective-permute-start(f32[40,8,128]{2,1,0:T(8,128)S(1)} %get-tuple-element.32), channel_id=1, source_target_pairs={{0,8},{1,9},{2,10},{3,11},{4,12},{5,13},{6,14},{7,15},{8,0},{9,1},... | collective-permute-start | bytes 491528 | tf_op jit(solution)/shard_map/ppermute | solution.py:664
  24.3 4.6 %collective-permute-start.2 = (f32[1,16]{1,0:T(1,128)S(1)}, f32[1,16]{1,0:T(1,128)S(1)}, u32[]{:S(2)}, u32[]{:S(2)}) collective-permute-start(f32[1,16]{1,0:T(1,128)S(1)} %get-tuple-element.34.own_ref), channel_id=1, source_target_pairs={{0,1009},{1,1008},{2,1011},{3,1010},{4,1013},{5,1012},{6,1015},{7,... | collective-permute-start | bytes 200 | tf_op jit(solution)/shard_map/ppermute | solution.py:664
  28.9 1.9 %collective-permute-start.3 = (f32[1,16]{1,0:T(1,128)S(1)}, f32[1,16]{1,0:T(1,128)S(1)}, u32[]{:S(2)}, u32[]{:S(2)}) collective-permute-start(f32[1,16]{1,0:T(1,128)S(1)} %get-tuple-element.34.own_ref), channel_id=1, source_target_pairs={{0,16},{1,17},{2,18},{3,19},{4,20},{5,21},{6,22},{7,23},{8,24},{9,... | collective-permute-start | bytes 200 | tf_op jit(solution)/shard_map/ppermute | solution.py:664
  30.8 0.0 collective-permute-done.from_a
  30.8 0.0 collective-permute-done.1.from_b
  30.8 0.9 %interior.1 = (f32[19,12,8,128]{3,2,1,0:T(8,128)S(1)}, f32[19,14,8,128]{3,2,1,0:T(8,128)S(1)}, f32[9,12,8,128]{3,2,1,0:T(8,128)S(1)}, f32[4,8,8,128]{3,2,1,0:T(8...) custom-call(f32[2,3,8,128]{3,2,1,0:T(8,128)S(1)} %get-tuple-element.30.accel_ref, ...), custom_call_target="tpu_custom_call" | custom-call | tf_op jit(solution)/shard_map/interior/pallas_call | solution.py:668
  31.7 0.1 collective-permute-done.2.across_ref
  31.9 1.3 %collective-permute-done.3.within_ref = f32[1,16]{1,0:T(1,128)S(1)} collective-permute-done((f32[1,16]{1,0:T(1,128)S(1)}, f32[1,16]{1,0:T(1,128)S(1)}, u32[]{:S(2)}, u32[]{:S(2)}) %collective-permute-start.3) | collective-permute-done | bytes 96 | tf_op jit(solution)/shard_map/ppermute | solution.py:664
  33.2 1.2 %sides.1 = (f32[19,8,128]{2,1,0:T(8,128)S(1)}, f32[19,8,128]{2,1,0:T(8,128)S(1)}, f32[32,1,128]{2,1,0:T(1,128)}) custom-call(f32[2,3,8,128]{3,2,1,0:T(8,128)S(1)} %get-tuple-element.30.accel_ref, f32[19,8,8,128]{3,2,1,0:T(8,128)S(1)} %get-tuple-element.31.adj_ref, f32[40,8,128]{2,1,0:T(8,128)S(1)} %collective-permute-done.from_a, ...), custom_call_target="tpu_custom_call" | custom-call | tf_op jit(solution)/shard_map/sides/pallas_call | solution.py:668
  34.4 16.2 %all-to-all-start = ((f32[32,1,128]{2,1,0:T(1,128)}), f32[32,1,128]{2,1,0:T(1,128)S(1)}, u32[]{:S(2)}, u32[]{:S(2)}) async-start(f32[32,1,128]{2,1,0:T(1,128)} %get-tuple-element.42), calls=%async_computation | async-start | bytes 32768 | tf_op jit(solution)/shard_map/all_to_all | solution.py:748
  50.6 1.1 %adjoint_start.1 = f32[19,8,8,128]{3,2,1,0:T(8,128)} custom-call(f32[2,3,8,128]{3,2,1,0:T(8,128)S(1)} %get-tuple-element.30.accel_ref, f32[8,128]{1,0:T(8,128)S(1)} %get-tuple-element.36.solid_ref, f32[19,12,8,128]{3,2,1,0:T(8,128)S(1)} %get-tuple-element.43.g_ref, f32[4,8,8,128]{3,2,1,0:T(8,128)S(1)} %get-tuple-element.44.mom_ref, ...), custom_call_target="tpu_custom_call" | custom-call | tf_op jit(solution)/shard_map/adjoint_start/pallas_call | solution.py:668
  51.7 5.7 %all-to-all-done.sums_ref = f32[32,1,128]{2,1,0:T(1,128)S(1)} async-done(((f32[32,1,128]{2,1,0:T(1,128)}), f32[32,1,128]{2,1,0:T(1,128)S(1)}, u32[]{:S(2)}, u32[]{:S(2)}) %all-to-all-start) | async-done | bytes 16416 | tf_op jit(solution)/shard_map/all_to_all | solution.py:748
  57.4 0.7 %collective-permute-start.4 = (f32[1,128]{1,0:T(1,128)S(1)}, f32[1,128]{1,0:T(1,128)S(1)}, u32[]{:S(2)}, u32[]{:S(2)}) collective-permute-start(f32[1,128]{1,0:T(1,128)S(1)} %group_end.1), channel_id=1, source_target_pairs={{16,24},{17,25},{18,26},{19,27},{20,28},{21,29},{22,30},{23,31},{2... | collective-permute-start | bytes 1544 | tf_op jit(solution)/shard_map/ppermute | solution.py:664
  58.1 0.0 collective-permute-done.4.outside_ref
  58.1 0.7 %update.1 = (f32[1,16]{1,0:T(1,128)}, f32[1,16]{1,0:T(1,128)}, f32[1,16]{1,0:T(1,128)}) custom-call(f32[32,1,128]{2,1,0:T(1,128)S(1)} %all-to-all-done.sums_ref, f32[1,128]{1,0:T(1,128)S(1)} %collective-permute-done.4.outside_ref, f32[1,16]{1,0:T(1,128)S(1)} %get-tuple-element.49.design_ref, s32[1,16]{1,0:T(1,128)S(1)} %get-tuple-element.50.mask_ref, ...), custom_call_target="tpu_custom_call" | custom-call | tf_op jit(solution)/shard_map/update/pallas_call | solution.py:668
  (1 shorter events, 0.0 us)
Async XLA Ops:
  2.2 28.7 %collective-permute-start.1 = (f32[41,8,128]{2,1,0:T(8,128)S(1)}, f32[41,8,128]{2,1,0:T(8,128)S(1)}, u32[]{:S(2)}, u32[]{:S(2)}) collective-permute-start(f32[41,8,128]{2,1,0:T(8,128)S(1)} %get-tuple-element.33), channel_id=1, source_target_pairs={{0,1016},{1,1017},{2,1018},{3,1019},{4,1020},{5,1021},{6,1022},{7,... | collective-permute-start | bytes 503816 | tf_op jit(solution)/shard_map/ppermute | solution.py:664
  7.5 23.2 %collective-permute-start = (f32[40,8,128]{2,1,0:T(8,128)S(1)}, f32[40,8,128]{2,1,0:T(8,128)S(1)}, u32[]{:S(2)}, u32[]{:S(2)}) collective-permute-start(f32[40,8,128]{2,1,0:T(8,128)S(1)} %get-tuple-element.32), channel_id=1, source_target_pairs={{0,8},{1,9},{2,10},{3,11},{4,12},{5,13},{6,14},{7,15},{8,0},{9,1},... | collective-permute-start | bytes 491528 | tf_op jit(solution)/shard_map/ppermute | solution.py:664
  24.3 7.6 %collective-permute-start.2 = (f32[1,16]{1,0:T(1,128)S(1)}, f32[1,16]{1,0:T(1,128)S(1)}, u32[]{:S(2)}, u32[]{:S(2)}) collective-permute-start(f32[1,16]{1,0:T(1,128)S(1)} %get-tuple-element.34.own_ref), channel_id=1, source_target_pairs={{0,1009},{1,1008},{2,1011},{3,1010},{4,1013},{5,1012},{6,1015},{7,... | collective-permute-start | bytes 200 | tf_op jit(solution)/shard_map/ppermute | solution.py:664
  28.9 4.3 %collective-permute-start.3 = (f32[1,16]{1,0:T(1,128)S(1)}, f32[1,16]{1,0:T(1,128)S(1)}, u32[]{:S(2)}, u32[]{:S(2)}) collective-permute-start(f32[1,16]{1,0:T(1,128)S(1)} %get-tuple-element.34.own_ref), channel_id=1, source_target_pairs={{0,16},{1,17},{2,18},{3,19},{4,20},{5,21},{6,22},{7,23},{8,24},{9,... | collective-permute-start | bytes 200 | tf_op jit(solution)/shard_map/ppermute | solution.py:664
  34.4 23.0 %all-to-all-start = ((f32[32,1,128]{2,1,0:T(1,128)}), f32[32,1,128]{2,1,0:T(1,128)S(1)}, u32[]{:S(2)}, u32[]{:S(2)}) async-start(f32[32,1,128]{2,1,0:T(1,128)} %get-tuple-element.42), calls=%async_computation | async-start | bytes 32768 | tf_op jit(solution)/shard_map/all_to_all | solution.py:748
  57.4 0.7 %collective-permute-start.4 = (f32[1,128]{1,0:T(1,128)S(1)}, f32[1,128]{1,0:T(1,128)S(1)}, u32[]{:S(2)}, u32[]{:S(2)}) collective-permute-start(f32[1,128]{1,0:T(1,128)S(1)} %group_end.1), channel_id=1, source_target_pairs={{16,24},{17,25},{18,26},{19,27},{20,28},{21,29},{22,30},{23,31},{2... | collective-permute-start | bytes 1544 | tf_op jit(solution)/shard_map/ppermute | solution.py:664
